TPU v7x, 32 devices: a whole 2x2x4 slice. The times are simulated.
32 devices in a mesh: lat: 8 (over z, y), tok: 4 (over x, core).
Axes of the slice: x: 2, y: 2, z: 4, core: 2. Of those that a mesh axis runs over, the one named last changes fastest.
Arguments:
- inputs: bfloat16 [256, 3, 2304], P('lat', None, 'tok'), may hold values from -6 to 6
- targets: bfloat16 [256, 3, 2304], P('lat', None, 'tok'), may hold values from -6 to 6
- enc_weight: bfloat16 [3, 2304, 2048], P(None, 'tok', 'lat'), may hold values from -0.125 to 0.125
- enc_bias: float32 [3, 2048], P(None, 'lat'), may hold values from -3 to 3
- dec_weight: bfloat16 [6, 2048, 2304], P(None, 'lat', 'tok'), may hold values from -0.125 to 0.125
- counts: int32 [3, 8], P(None, 'lat'), may hold values from 32 to 256, as said below
Outputs:
- recon: bfloat16 [256, 3, 2304], P('lat', None, 'tok')
- dec_grad: bfloat16 [6, 2048, 2304], P(None, 'lat', 'tok')
- latent_grad: bfloat16 [256, 3, 2048], P('tok', None, 'lat')
Inputs may be any that keep to these rules, and one draw needn't show every extreme that they name: Latents 0 to counts[l, t] - 1 of layer l's tile on index t of lat are live, the rest dead; in every layer some tile has all 256 live.
All inputs are finite; a program needn't handle non-finite values.
Results may differ from a plain program's by a relative error of at most 0.0054.
Values may be sent and summed in bfloat16 or wider, within the bound.
No kernel may reach another device: no remote copies, remote signals or barrier semaphores. Data moves between devices by JAX's collectives and lax.ppermute only.
A program may use at most 64 MiB of HBM per device.

v0:
```python
import jax
import jax.numpy as jnp
from jax import lax
from jax.sharding import PartitionSpec as P


def block_index(source, target, layers):
    return source * layers - source * (source - 1) // 2 + (target - source)


def forward_tile(tile_values, weight):
    return jnp.dot(tile_values, weight, preferred_element_type=jnp.float32)


def backward_tile(error_rows, weight):
    contract = (((1,), (1,)), ((), ()))
    return lax.dot_general(error_rows, weight, contract, preferred_element_type=jnp.float32)


def weight_tile(tile_values, error_rows):
    contract = (((0,), (0,)), ((), ()))
    return lax.dot_general(tile_values, error_rows, contract, preferred_element_type=jnp.float32)


def local(inputs, targets, enc_weight, enc_bias, dec_weight, counts):
    layers = inputs.shape[1]
    tile_width = enc_weight.shape[2]
    live_mask = lax.broadcasted_iota(jnp.int32, (layers, tile_width), 1) < counts
    gathered = lax.all_gather(inputs, "lat", axis=0, tiled=True)
    partial_pre = jnp.einsum(
        "tld,ldk->tlk", gathered, enc_weight, preferred_element_type=jnp.float32
    )
    preact = lax.psum(partial_pre, "tok")
    preact = preact + enc_bias[None]
    latents = jnp.where(live_mask[None], jnp.maximum(preact, 0.0), 0.0).astype(jnp.bfloat16)
    own_rows = inputs.shape[0]
    whole_targets = lax.all_gather(targets, "lat", axis=0, tiled=True)
    picked = latents
    stacked = []
    for decode_target in range(layers):
        summed = forward_tile(picked[:, 0, :], dec_weight[block_index(0, decode_target, layers)])
        for decode_source in range(1, decode_target + 1):
            summed = summed + forward_tile(
                picked[:, decode_source, :],
                dec_weight[block_index(decode_source, decode_target, layers)],
            )
        stacked.append(summed)
    whole_recon = lax.psum(jnp.stack(stacked, axis=1), "lat")
    errors = (whole_recon - whole_targets.astype(jnp.float32)).astype(jnp.bfloat16)
    full_recon = lax.dynamic_slice_in_dim(
        whole_recon, lax.axis_index("lat") * own_rows, own_rows, 0
    )
    recon = full_recon.astype(jnp.bfloat16)
    grads = []
    for source in range(layers):
        for target in range(source, layers):
            grads.append(
                weight_tile(latents[:, source, :], errors[:, target, :]).astype(jnp.bfloat16)
            )
    dec_grad = jnp.stack(grads, axis=0)
    picked = errors
    stacked = []
    for source in range(layers):
        summed = backward_tile(
            picked[:, source, :], dec_weight[block_index(source, source, layers)]
        )
        for target in range(source + 1, layers):
            summed = summed + backward_tile(
                picked[:, target, :], dec_weight[block_index(source, target, layers)]
            )
        stacked.append(summed)
    latent_sum = lax.psum_scatter(
        jnp.stack(stacked, axis=1), "tok", scatter_dimension=0, tiled=True
    )
    latent_grad = jnp.where(live_mask[None], latent_sum, 0.0).astype(jnp.bfloat16)
    return (recon, dec_grad, latent_grad)


def solution(mesh):
    in_specs = (
        P("lat", None, "tok"),
        P("lat", None, "tok"),
        P(None, "tok", "lat"),
        P(None, "lat"),
        P(None, "lat", "tok"),
        P(None, "lat"),
    )
    out_specs = (P("lat", None, "tok"), P(None, "lat", "tok"), P("tok", None, "lat"))
    return jax.shard_map(local, mesh=mesh, in_specs=in_specs, out_specs=out_specs, check_vma=False)
```

profile of v0, /device:TPU:0, one launch (start us, length us, event | category | flops | bytes accessed | tf_op | source)
XLA Modules:
  0.0 220.7 jit_solution(1469137658321735)
XLA Ops:
  7.2 0.0 copy-start
  7.2 0.0 all-reduce.3.cloned.1.call-start
  7.2 34.8 %all_gather.6 = bf16[256,3,576]{2,0,1:T(8,128)(2,1)S(1)} all-gather(bf16[32,3,576]{2,0,1:T(8,128)(2,1)} %param.6), channel_id=1, replica_groups=mesh['lat'=8,'tok'=4] {'lat'}, dimensions={0}, use_global_device_ids=true | all-gather | bytes 995328 | tf_op jit(solution)/shard_map/all_gather | solution.py:29
  42.0 0.0 copy-done
  42.0 0.0 copy-start.8
  42.0 0.0 copy-start.7
  42.0 0.0 copy-start.1
  42.0 1.4 convolution_bitcast_fusion
  43.5 0.0 all-reduce.3.cloned.1.call-update
  43.5 0.0 all-reduce.5.cloned.1.call-start
  43.5 0.0 copy-done.8
  43.5 0.1 iota_compare_fusion
  43.6 35.5 %all-reduce.3.cloned.1.call-done = f32[256,3,256]{0,2,1:T(8,128)} async-done(((f32[256,3,256]{0,2,1:T(8,128)}), f32[256,3,256]{0,2,1:T(8,128)}) %all-reduce.3.cloned.1.call-update) | async-done | bytes 786448 | tf_op jit(solution)/shard_map/psum | solution.py:33
  79.1 0.0 copy-done.7
  79.1 1.4 select_convert_fusion
  80.5 0.0 copy-done.1
  80.5 0.0 copy-start.4
  80.5 0.2 fusion.21
  80.8 0.2 fusion.27
  81.0 0.2 convolution_bitcast_fusion.1
  81.2 0.2 convolution_add_fusion.1
  81.5 0.2 fusion.1
  81.7 0.0 copy-done.4
  81.7 0.2 fusion
  82.0 1.3 pad_maximum_fusion
  83.3 0.0 copy-start.6
  83.3 0.0 all-reduce.5.cloned.1.call-update
  83.3 0.0 reduce-scatter.2.cloned.1.call-start
  83.4 0.8 copy-done.6
  84.2 37.2 %all_gather.7 = bf16[256,3,576]{2,0,1:T(8,128)(2,1)} all-gather(bf16[32,3,576]{2,0,1:T(8,128)(2,1)S(1)} %copy-done.6), channel_id=1, replica_groups=mesh['lat'=8,'tok'=4] {'lat'}, dimensions={0}, use_global_device_ids=true | all-gather | bytes 995328 | tf_op jit(solution)/shard_map/all_gather | solution.py:37
  121.4 1.6 copy.11
  123.0 62.1 %all-reduce.5.cloned.1.call-done = f32[256,3,576]{0,2,1:T(8,128)} async-done(((f32[256,3,576]{0,2,1:T(8,128)}), f32[256,3,576]{0,2,1:T(8,128)}) %all-reduce.5.cloned.1.call-update) | async-done | bytes 1769488 | tf_op jit(solution)/shard_map/psum | solution.py:48
  185.1 1.7 subtract_convert_fusion
  186.8 0.0 copy-start.2
  186.8 0.3 convolution_bitcast_fusion.2
  187.1 0.3 fusion.23
  187.4 0.3 fusion.29
  187.7 0.3 fusion.14
  188.0 0.3 convolution_add_fusion.5
  188.3 0.0 copy-done.2
  188.3 0.3 fusion.15
  188.6 0.0 copy-start.3
  188.6 0.0 copy-start.5
  188.7 0.9 pad_maximum_fusion.1
  189.6 0.0 reduce-scatter.2.cloned.1.call-update
  189.6 1.4 dynamic-slice_convert_fusion
  191.0 0.8 copy.12
  191.8 0.0 copy-done.3
  191.8 0.0 copy-done.5
  191.8 1.0 fusion.3
  192.8 1.0 fusion.5
  193.8 1.0 fusion.7
  194.8 1.0 fusion.9
  195.7 1.0 fusion.11
  196.7 1.0 fusion.13
  197.7 14.9 %reduce-scatter.2.cloned.1.call-done = f32[64,3,256]{2,0,1:T(8,128)} async-done(((f32[256,3,256]{2,0,1:T(8,128)}), f32[64,3,256]{2,0,1:T(8,128)}) %reduce-scatter.2.cloned.1.call-update) | async-done | bytes 196624 | tf_op jit(solution)/shard_map/reduce_scatter | solution.py:72
  212.6 1.6 select_convert_fusion.1
Async XLA Ops:
  7.2 34.9 %copy-start = (bf16[3,576,256]{2,1,0:T(8,128)(2,1)S(1)}, bf16[3,576,256]{2,1,0:T(8,128)(2,1)}, u32[]{:S(2)}) copy-start(bf16[3,576,256]{2,1,0:T(8,128)(2,1)} %param.8) | copy-start | bytes 2654212
  7.2 71.9 %all-reduce.3.cloned.1.call-start = ((), (), s32[]{:S(2)}) async-start(), calls=%async_computation.1 | async-start | bytes 1572864 | tf_op jit(solution)/shard_map/psum | solution.py:33
  42.0 1.5 copy-start.8
  42.0 37.1 %copy-start.7 = (f32[3,256]{1,0:T(4,128)S(1)}, f32[3,256]{1,0:T(4,128)}, u32[]{:S(2)}) copy-start(f32[3,256]{1,0:T(4,128)} %param.9) | copy-start | bytes 9220
  42.0 38.5 %copy-start.1 = (bf16[6,256,576]{1,2,0:T(8,128)(2,1)S(1)}, bf16[6,256,576]{1,2,0:T(8,128)(2,1)}, u32[]{:S(2)}) copy-start(bf16[6,256,576]{1,2,0:T(8,128)(2,1)} %param.10) | copy-start | bytes 5308420
  43.5 141.6 %all-reduce.5.cloned.1.call-start = ((), (), s32[]{:S(2)}) async-start(), calls=%async_computation.2 | async-start | bytes 3538944 | tf_op jit(solution)/shard_map/psum | solution.py:48
  80.5 1.2 copy-start.4
  83.3 0.9 copy-start.6
  83.3 129.3 %reduce-scatter.2.cloned.1.call-start = ((), (), s32[]{:S(2)}) async-start(), calls=%async_computation.3 | async-start | bytes 983040 | tf_op jit(solution)/shard_map/reduce_scatter | solution.py:72
  186.8 1.5 copy-start.2
  188.6 3.2 %copy-start.3 = (bf16[256,3,576]{0,2,1:T(8,128)(2,1)S(1)}, bf16[256,3,576]{0,2,1:T(8,128)(2,1)}, u32[]{:S(2)}) copy-start(bf16[256,3,576]{0,2,1:T(8,128)(2,1)} %copy-done.2) | copy-start | bytes 2654212
  188.6 3.2 %copy-start.5 = (bf16[256,3,256]{0,2,1:T(8,128)(2,1)S(1)}, bf16[256,3,256]{0,2,1:T(8,128)(2,1)}, u32[]{:S(2)}) copy-start(bf16[256,3,256]{0,2,1:T(8,128)(2,1)} %copy-done.4) | copy-start | bytes 1179652
Sparse Core Ops, SparseCore 0:
  43.6 35.4 all-reduce.2
  83.4 101.6 all-reduce.4
  189.7 22.8 reduce-scatter.1
where the time goes:
time: 221 us
  waiting for transfers between devices  113 us (51%)
  blocking collectives  72 us (33%)
  between operations  14 us (6%)
  matrix products  10.5 us (5%)
  other arithmetic  6.97 us (3%)
  local copies, waits for them, and re-layouts  4.64 us (2%)
    psum x1, waiting for transfers between devices, local(): whole_recon = lax.psum(jnp.stack(stacked, axis=1), 'lat')  62.1 us
    all_gather x1, blocking collectives, local(): whole_targets = lax.all_gather(targets, 'lat', axis=0, tiled=True)  37.2 us
    psum x1, waiting for transfers between devices, local(): preact = lax.psum(partial_pre, 'tok')  35.5 us
    all_gather x1, blocking collectives, local(): gathered = lax.all_gather(inputs, 'lat', axis=0, tiled=True)  34.8 us
    reduce_scatter x1, waiting for transfers between devices, local(): lax.psum_scatter(jnp.stack(stacked, axis=1), 'tok', scatter_dimension=0,...  14.9 us
    dot_general x6, matrix products, weight_tile(): lax.dot_general(tile_values, error_rows, contract, preferred_element_type...  5.88 us
  transfers between devices with their start and end apart: 3, of which 3 were waited for; matrix products, arithmetic and copies ran while one was open for 4% of the time, Pallas kernels for 0%

commit v1 on v0

v1 whole, which is shorter than its diff:
```python
import functools

import jax
import jax.numpy as jnp
from jax import lax
from jax.experimental import pallas as pl
from jax.experimental.pallas import tpu as pltpu
from jax.sharding import PartitionSpec as P

BF = jnp.bfloat16
F32 = jnp.float32
AXES = ("lat", "tok")


def block_index(source, target, layers):
    return source * layers - source * (source - 1) // 2 + (target - source)


def fused(body, outs, *args, scratch=(), scalars=1):
    specs = [pl.BlockSpec(memory_space=pltpu.SMEM)] * scalars
    specs += [pl.BlockSpec(memory_space=pltpu.VMEM)] * (len(args) - scalars)
    out_shape = [jax.ShapeDtypeStruct(s, d) for s, d in outs]
    return pl.pallas_call(
        body,
        out_shape=out_shape,
        in_specs=specs,
        out_specs=[pl.BlockSpec(memory_space=pltpu.VMEM)] * len(outs),
        scratch_shapes=[pltpu.VMEM(s, d) for s, d in scratch],
        compiler_params=pltpu.CompilerParams(vmem_limit_bytes=40 * 2**20),
    )(*args)


HOME, CORE, OFF = 0, 1, 2


def join_kernel(info, own, other, out):
    width = own.shape[2]

    @pl.when(info[CORE] == 0)
    def _():
        out[:, :, :width] = own[...]
        out[:, :, width:] = other[...]

    @pl.when(info[CORE] != 0)
    def _():
        out[:, :, :width] = other[...]
        out[:, :, width:] = own[...]


def stack_kernel(info, own, other, out):
    rows = own.shape[1]
    core = info[CORE]
    out[:, pl.ds(pl.multiple_of(core * rows, rows), rows), :] = own[...]
    out[:, pl.ds(pl.multiple_of((1 - core) * rows, rows), rows), :] = other[...]


def place(info, own, r1, r2, r3, r4, out):
    rows = own.shape[1]

    def at(i):
        return pl.ds(pl.multiple_of(info[OFF + i], rows), rows)

    @pl.when(info[HOME] != 0)
    def _():
        out[:, at(0), :] = own[...]
        out[:, at(1), :] = r2[...]

    @pl.when(info[HOME] == 0)
    def _():
        out[:, at(0), :] = r2[...]
        out[:, at(1), :] = r4[...]

    out[:, at(2), :] = r1[...]
    out[:, at(3), :] = r3[...]


def encode_kernel(info, own, r1, r2, r3, r4, weight, part, sent, held):
    place(info, own, r1, r2, r3, r4, held)
    for layer in range(part.shape[0]):
        value = jnp.dot(held[layer], weight[layer], preferred_element_type=F32)
        part[layer] = value
        sent[layer] = value.astype(BF)


def decode_kernel(info, counts, part, got, bias, weight, latents, q0, q1, q2, q3, recon):
    layers, half = part.shape[0], part.shape[1] // 2
    rows = q0.shape[1]
    width = part.shape[2]
    for layer in range(layers):
        live = lax.broadcasted_iota(jnp.int32, (half, width), 1) < counts[layer]
        for side in range(2):
            mine = pl.ds(side * half, half)
            theirs = pl.ds((1 - side) * half, half)
            pre = part[layer, mine, :] + got[layer, theirs, :].astype(F32) + bias[layer : layer + 1, :]
            latents[layer, mine, :] = jnp.where(live, jnp.maximum(pre, 0.0), 0.0).astype(BF)
    for target in range(layers):
        total = None
        for source in range(target + 1):
            value = lax.dot_general(
                latents[source],
                weight[block_index(source, target, layers)],
                (((1,), (1,)), ((), ())),
                preferred_element_type=F32,
            )
            total = value if total is None else total + value
        recon[...] = total

        def at(i):
            return recon[pl.ds(pl.multiple_of(info[OFF + i], rows), rows), :]

        q0[target] = at(0)
        q1[target] = at(1).astype(BF)
        q2[target] = at(2)
        q3[target] = at(3).astype(BF)


def add_keep_kernel(info, kept, got, total, sent):
    value = kept[...] + got[...].astype(F32)
    total[...] = value
    sent[...] = value.astype(BF)


def add_kernel(info, kept, got, sent):
    sent[...] = (kept[...] + got[...].astype(F32)).astype(BF)


def own_sum_kernel(info, kept, u0, u2, out):
    home = info[HOME] != 0
    out[...] = jnp.where(home, kept[...], u0[...].astype(F32)) + u2[...].astype(F32)


def error_kernel(info, mine, theirs, wanted, recon, errors):
    width = recon.shape[2]
    total = mine[...] + theirs[...]
    errors[...] = (total - wanted[...].astype(F32)).astype(BF)

    @pl.when(info[CORE] == 0)
    def _():
        recon[...] = total[:, :, :width].astype(BF)

    @pl.when(info[CORE] != 0)
    def _():
        recon[...] = total[:, :, width:].astype(BF)


def backward_kernel(info, own, r1, r2, r3, r4, weight, kept, sent, mine, other, held):
    place(info, own, r1, r2, r3, r4, held)
    layers, half = kept.shape[0], kept.shape[1]
    width = mine.shape[2]
    for source in range(layers):
        total = None
        for target in range(source, layers):
            value = jnp.dot(
                held[target], weight[block_index(source, target, layers)], preferred_element_type=F32
            )
            total = value if total is None else total + value
        kept[source] = total[:half]
        sent[source] = total[half:].astype(BF)

    @pl.when(info[CORE] == 0)
    def _():
        mine[...] = held[:, :, :width]
        other[...] = held[:, :, width:]

    @pl.when(info[CORE] != 0)
    def _():
        mine[...] = held[:, :, width:]
        other[...] = held[:, :, :width]


def weight_grad_kernel(info, errors, errors_got, latents, latents_got, out):
    layers = latents.shape[0]
    contract = (((0,), (0,)), ((), ()))
    for source in range(layers):
        for target in range(source, layers):
            total = lax.dot_general(errors[target], latents[source], contract, preferred_element_type=F32)
            total += lax.dot_general(
                errors_got[target], latents_got[source], contract, preferred_element_type=F32
            )
            out[block_index(source, target, layers)] = total.astype(BF)


def latent_grad_kernel(info, counts, kept, got, out):
    live_at = lax.broadcasted_iota(jnp.int32, kept.shape[1:], 1)
    for layer in range(kept.shape[0]):
        value = kept[layer] + got[layer].astype(F32)
        out[layer] = jnp.where(live_at < counts[layer], value, 0.0).astype(BF)


def make_paired(n_tok):
    places = [(z, y, x, c) for z in range(n_tok) for y in range(2) for x in range(n_tok // 2) for c in range(2)]

    def swap(value, where):
        pairs = []
        for i, (z, y, x, c) in enumerate(places):
            to = where(z, y, x, c, c == z % 2)
            if to is not None:
                pairs.append((i, places.index(to)))
        return lax.ppermute(value, AXES, pairs)

    def over_c(value):
        return swap(value, lambda z, y, x, c, home: (z, y, x, 1 - c))

    def over_x(value):
        return swap(value, lambda z, y, x, c, home: (z, y, 1 - x, c))

    def over_y(value):
        return swap(value, lambda z, y, x, c, home: (z, 1 - y, x, c))

    def over_y_away(value):
        return swap(value, lambda z, y, x, c, home: None if home else (z, 1 - y, x, c))

    def over_z2_z1(value):
        return swap(value, lambda z, y, x, c, home: (z ^ 2, y, x, c) if home else (z ^ 1, y, x, 1 - c))

    def over_y_z3(value):
        return swap(value, lambda z, y, x, c, home: (z, 1 - y, x, c) if home else (z ^ 3, y, x, 1 - c))

    def over_z3_away(value):
        return swap(value, lambda z, y, x, c, home: None if home else (z ^ 3, y, x, 1 - c))

    def gather(own):
        r1 = over_z2_z1(own)
        r2 = over_y_z3(own)
        return own, r1, r2, over_y(r1), over_y_away(r2)

    def local(inputs, targets, enc_weight, enc_bias, dec_weight, counts):
        rows, layers, width = inputs.shape
        latent_width = enc_weight.shape[2]
        both = 2 * width
        held = rows * 2 * n_tok // 2
        lat, tok = lax.axis_index("lat"), lax.axis_index("tok")
        z, y, x, c = lat // 2, lat % 2, tok // 2, tok % 2
        home = z % 2 == c
        near = jnp.where(home, z, z ^ 3)
        base = jnp.where(near // 2 == x, 0, held // 2)
        far = held // 2 - base
        info = jnp.stack(
            [home.astype(jnp.int32), c]
            + [base + rows * y, base + rows * (1 - y), far + rows * y, far + rows * (1 - y)]
        ).astype(jnp.int32)
        counts = counts[:, 0]

        own_in = jnp.swapaxes(inputs, 0, 1)
        own_want = jnp.swapaxes(targets, 0, 1)
        dec_t = jnp.swapaxes(dec_weight, 1, 2)
        (block,) = fused(join_kernel, [((layers, rows, both), BF)], info, own_in, over_c(own_in))
        arrived = gather(block)
        (wanted,) = fused(join_kernel, [((layers, rows, both), BF)], info, own_want, over_c(own_want))
        (enc_all,) = fused(stack_kernel, [((layers, both, latent_width), BF)], info, enc_weight, over_c(enc_weight))
        (dec_all,) = fused(stack_kernel, [((dec_t.shape[0], both, latent_width), BF)], info, dec_t, over_c(dec_t))

        tile = (layers, held, latent_width)
        rest = [((layers, held, both), BF)]
        part, sent = fused(encode_kernel, [(tile, F32), (tile, BF)], info, *arrived, enc_all, scratch=rest)
        piece = (layers, rows, both)
        latents, q0, q1, q2, q3 = fused(
            decode_kernel,
            [(tile, BF), (piece, F32), (piece, BF), (piece, F32), (piece, BF)],
            info,
            counts,
            part,
            over_x(sent),
            enc_bias,
            dec_all,
            scratch=[((held, both), F32)],
            scalars=2,
        )
        total, sent = fused(add_keep_kernel, [(piece, F32), (piece, BF)], info, q0, over_y(q1))
        u0 = over_z3_away(sent)
        (sent,) = fused(add_kernel, [(piece, BF)], info, q2, over_y(q3))
        u2 = over_z2_z1(sent)
        latents_got = over_c(latents)
        (mine,) = fused(own_sum_kernel, [(piece, F32)], info, total, u0, u2)
        recon, errors = fused(
            error_kernel, [((layers, rows, width), BF), (piece, BF)], info, mine, over_c(mine), wanted
        )
        arrived = gather(errors)
        quarter = (layers, held // 2, latent_width)
        wide = (layers, held, width)
        kept, sent, err_mine, err_other = fused(
            backward_kernel,
            [(quarter, F32), (quarter, BF), (wide, BF), (wide, BF)],
            info,
            *arrived,
            dec_all,
            scratch=rest,
        )
        got = over_x(sent)
        (grads,) = fused(
            weight_grad_kernel,
            [((dec_t.shape[0], width, latent_width), BF)],
            info,
            err_mine,
            over_c(err_other),
            latents,
            latents_got,
        )
        (latent_grad,) = fused(latent_grad_kernel, [(quarter, BF)], info, counts, kept, got, scalars=2)
        return jnp.swapaxes(recon, 0, 1), jnp.swapaxes(grads, 1, 2), jnp.swapaxes(latent_grad, 0, 1)

    return local


def general(inputs, targets, enc_weight, enc_bias, dec_weight, counts):
    layers = inputs.shape[1]
    width = enc_weight.shape[2]
    live = (lax.broadcasted_iota(jnp.int32, (layers, width), 1) < counts)[None]
    gathered = lax.all_gather(inputs, "lat", axis=0, tiled=True)
    part = jnp.einsum("tld,ldk->tlk", gathered, enc_weight, preferred_element_type=F32)
    preact = lax.psum(part, "tok") + enc_bias[None]
    latents = jnp.where(live, jnp.maximum(preact, 0.0), 0.0).astype(BF)
    recons = []
    for target in range(layers):
        recons.append(
            sum(
                jnp.dot(
                    latents[:, source],
                    dec_weight[block_index(source, target, layers)],
                    preferred_element_type=F32,
                )
                for source in range(target + 1)
            )
        )
    full = lax.psum_scatter(jnp.stack(recons, 1), "lat", scatter_dimension=0, tiled=True)
    own_errors = (full - targets.astype(F32)).astype(BF)
    errors = lax.all_gather(own_errors, "lat", axis=0, tiled=True)
    grads, sums = [], []
    for source in range(layers):
        total = 0.0
        for target in range(source, layers):
            weight = dec_weight[block_index(source, target, layers)]
            total = total + lax.dot_general(
                errors[:, target], weight, (((1,), (1,)), ((), ())), preferred_element_type=F32
            )
            grads.append(
                lax.dot_general(
                    latents[:, source],
                    errors[:, target],
                    (((0,), (0,)), ((), ())),
                    preferred_element_type=F32,
                ).astype(BF)
            )
        sums.append(total)
    latent_sum = lax.psum_scatter(jnp.stack(sums, 1), "tok", scatter_dimension=0, tiled=True)
    latent_grad = jnp.where(live, latent_sum, 0.0).astype(BF)
    return full.astype(BF), jnp.stack(grads, 0), latent_grad


def solution(mesh):
    n_lat, n_tok = mesh.shape["lat"], mesh.shape["tok"]
    in_specs = (
        P("lat", None, "tok"),
        P("lat", None, "tok"),
        P(None, "tok", "lat"),
        P(None, "lat"),
        P(None, "lat", "tok"),
        P(None, "lat"),
    )
    out_specs = (P("lat", None, "tok"), P(None, "lat", "tok"), P("tok", None, "lat"))
    paired = n_lat == 2 * n_tok and n_tok == 4
    local = make_paired(n_tok) if paired else general
    return jax.shard_map(local, mesh=mesh, in_specs=in_specs, out_specs=out_specs, check_vma=False)
```

time: 221 us -> 95.9 us (0.43)
  blocking collectives: 72 us -> 0 us
  waiting for transfers between devices: 113 us -> 58.4 us
  starting transfers between devices: 0.12 us -> 20.1 us
  Pallas kernels: 0 us -> 14.3 us
  between operations: 14 us -> 0.82 us
  matrix products: 10.5 us -> 0 us
  other arithmetic: 6.97 us -> 0 us
  local copies, waits for them, and re-layouts: 4.64 us -> 2.17 us
    psum x2 -> x0, waiting for transfers between devices: 97.6 us -> none  [the longest x1 62.1 us: local(): whole_recon = lax.psum(jnp.stack(stacked, axis=1), 'lat')]
    all_gather x2 -> x0, blocking collectives: 72 us -> none  [the longest x1 37.2 us: local(): whole_targets = lax.all_gather(targets, 'lat', axis=0, tiled=True)]
    ppermute x0 -> x21, waiting for transfers between devices: none -> 58.4 us  [swap(): return lax.ppermute(value, AXES, pairs)]
    ppermute x0 -> x21, starting transfers between devices: none -> 20.1 us  [swap(): return lax.ppermute(value, AXES, pairs)]
    reduce_scatter x1 -> x0, waiting for transfers between devices: 14.9 us -> none  [local(): lax.psum_scatter(jnp.stack(stacked, axis=1), 'tok', scatter_dimension=0,...]
    pallas_call x0 -> x13, Pallas kernels: none -> 14.3 us  [fused(): pl.pallas_call(body, out_shape=out_shape, in_specs=specs, out_specs=[pl.B...]
    dot_general x19 -> x0, matrix products: 10.5 us -> none  [the longest x6 5.88 us: weight_tile(): lax.dot_general(tile_values, error_rows, contract, preferred_element_type...]
    convert_element_type x3 -> x0, other arithmetic: 4.65 us -> none  [the longest x1 1.67 us: local(): (whole_recon - whole_targets.astype(jnp.float32)).astype(jnp.bfloat16)]
  transfers between devices with their start and end apart: 3 -> 21, of which waited for: 3 -> 11; matrix products, arithmetic and copies ran while one was open for 4% -> 0% of each run, Pallas kernels for 0% -> 7%
where the time goes in v1:
time: 95.9 us; the launch traced here: 95.7 us
  waiting for transfers between devices  58.4 us (61%)
  starting transfers between devices  20.1 us (21%)
  Pallas kernels  14.3 us (15%)
  local copies, waits for them, and re-layouts  2.17 us (2%)
    ppermute x21, waiting for transfers between devices, swap(): return lax.ppermute(value, AXES, pairs)  58.4 us
    ppermute x21, starting transfers between devices, swap(): return lax.ppermute(value, AXES, pairs)  20.1 us
    pallas_call x13, Pallas kernels, fused(): pl.pallas_call(body, out_shape=out_shape, in_specs=specs, out_specs=[pl.B...  14.3 us
    unnamed x12, local copies, waits for them, and re-layouts  2.09 us
  transfers between devices with their start and end apart: 21, of which 11 were waited for; matrix products, arithmetic and copies ran while one was open for 0% of the time, Pallas kernels for 7%

profile of v1, /device:TPU:0, one launch (start us, length us, event | category | flops | bytes accessed | tf_op | source)
XLA Modules:
  0.0 95.7 jit_solution(4733761788843179626)
XLA Ops:
  0.6 0.5 collective-permute-start.7
  1.1 0.1 collective-permute-start.5
  1.2 0.4 collective-permute-start
  1.7 0.1 stack.31.info
  1.7 4.4 %collective-permute-done.other = bf16[3,32,576]{2,1,0:T(8,128)(2,1)S(1)} collective-permute-done((bf16[3,32,576]{2,1,0:T(8,128)(2,1)}, bf16[3,32,576]{2,1,0:T(8,128)(2,1)S(1)}, u32[]{:S(2)}, u32[]{:S(2)}) %collective-permute-start) | collective-permute-done | bytes 110624 | tf_op jit(solution)/shard_map/ppermute | solution.py:199
  6.1 0.9 copy-done.2
  7.0 0.7 shard_map.85.own
  7.7 4.0 %collective-permute-start.1 = (bf16[3,32,1152]{2,1,0:T(8,128)(2,1)S(1)}, bf16[3,32,1152]{2,1,0:T(8,128)(2,1)S(1)}, u32[]{:S(2)}, u32[]{:S(2)}) collective-permute-start(bf16[3,32,1152]{2,1,0:T(8,128)(2,1)S(1)} %shard_map.85.own), channel_id=1, source_target_pairs={{0,16},{1,8},{2,18},{3,10},{4,20},{5,12},{6,22},{7,14},{8,1},{9,25... | collective-permute-start | bytes 663560 | tf_op jit(solution)/shard_map/ppermute | solution.py:199
  11.7 1.5 %collective-permute-start.2 = (bf16[3,32,1152]{2,1,0:T(8,128)(2,1)S(1)}, bf16[3,32,1152]{2,1,0:T(8,128)(2,1)S(1)}, u32[]{:S(2)}, u32[]{:S(2)}) collective-permute-start(bf16[3,32,1152]{2,1,0:T(8,128)(2,1)S(1)} %shard_map.85.own), channel_id=1, source_target_pairs={{0,4},{1,24},{2,6},{3,26},{4,0},{5,28},{6,2},{7,30},{8,17},{9,13},... | collective-permute-start | bytes 663560 | tf_op jit(solution)/shard_map/ppermute | solution.py:199
  13.2 8.9 %collective-permute-done.1.r1 = bf16[3,32,1152]{2,1,0:T(8,128)(2,1)S(1)} collective-permute-done((bf16[3,32,1152]{2,1,0:T(8,128)(2,1)S(1)}, bf16[3,32,1152]{2,1,0:T(8,128)(2,1)S(1)}, u32[]{:S(2)}, u32[]{:S(2)}) %collective-permute-start.1) | collective-permute-done | bytes 221216 | tf_op jit(solution)/shard_map/ppermute | solution.py:199
  22.1 2.2 %collective-permute-start.3 = (bf16[3,32,1152]{2,1,0:T(8,128)(2,1)S(1)}, bf16[3,32,1152]{2,1,0:T(8,128)(2,1)S(1)}, u32[]{:S(2)}, u32[]{:S(2)}) collective-permute-start(bf16[3,32,1152]{2,1,0:T(8,128)(2,1)S(1)} %collective-permute-done.1.r1), channel_id=1, source_target_pairs={{0,4},{1,5},{2,6},{3,7},{4,0},{5,1},{6,2},{7,3},{8,12},{9,13},{10,... | collective-permute-start | bytes 663560 | tf_op jit(solution)/shard_map/ppermute | solution.py:199
  24.3 0.0 collective-permute-done.2.r2
  24.3 0.7 collective-permute-start.4
  25.0 0.0 collective-permute-done.5.other
  25.0 0.0 copy-start.1
  25.0 1.2 %copy-done.1 = bf16[3,576,256]{2,1,0:T(8,128)(2,1)S(1)} copy-done((bf16[3,576,256]{2,1,0:T(8,128)(2,1)S(1)}, bf16[3,576,256]{2,1,0:T(8,128)(2,1)}, u32[]{:S(2)}) %copy-start.1) | copy-done | bytes 884760
  26.1 0.7 shard_map.86.weight
  26.8 0.0 copy-start
  26.8 3.2 %collective-permute-done.3.r3 = bf16[3,32,1152]{2,1,0:T(8,128)(2,1)S(1)} collective-permute-done((bf16[3,32,1152]{2,1,0:T(8,128)(2,1)S(1)}, bf16[3,32,1152]{2,1,0:T(8,128)(2,1)S(1)}, u32[]{:S(2)}, u32[]{:S(2)}) %collective-permute-start.3) | collective-permute-done | bytes 221216 | tf_op jit(solution)/shard_map/ppermute | solution.py:199
  30.0 0.0 collective-permute-done.4.r4
  30.0 1.1 %shard_map.87 = (f32[3,128,256]{2,1,0:T(8,128)S(1)}, bf16[3,128,256]{2,1,0:T(8,128)(2,1)S(1)}) custom-call(s32[6]{0:T(128)S(1)} %stack.31.info, bf16[3,32,1152]{2,1,0:T(8,128)(2,1)S(1)} %shard_map.85.own, bf16[3,32,1152]{2,1,0:T(8,128)(2,1)S(1)} %collective-permute-done.1.r1, bf16[3,32,1152]{2,1,0:T(8,128)(2,1)S(1)} %collective-permute-done.2.r2, ...), custom_call_target="tpu_custom_call" | custom-call | tf_op jit(solution)/shard_map/pallas_call | solution.py:23
  31.1 0.0 copy-start.4
  31.1 0.0 copy-start.5
  31.1 1.6 %collective-permute-start.6 = (bf16[3,128,256]{2,1,0:T(8,128)(2,1)S(1)}, bf16[3,128,256]{2,1,0:T(8,128)(2,1)S(1)}, u32[]{:S(2)}, u32[]{:S(2)}) collective-permute-start(bf16[3,128,256]{2,1,0:T(8,128)(2,1)S(1)} %get-tuple-element.19), channel_id=1, source_target_pairs={{0,2},{1,3},{2,0},{3,1},{4,6},{5,7},{6,4},{7,5},{8,10},{9,11},{10,... | collective-permute-start | bytes 589832 | tf_op jit(solution)/shard_map/ppermute | solution.py:199
  32.7 0.0 collective-permute-done.7.other
  32.7 0.0 copy-done
  32.7 0.8 shard_map.88.weight
  33.5 4.1 %collective-permute-done.6.got = bf16[3,128,256]{2,1,0:T(8,128)(2,1)S(1)} collective-permute-done((bf16[3,128,256]{2,1,0:T(8,128)(2,1)S(1)}, bf16[3,128,256]{2,1,0:T(8,128)(2,1)S(1)}, u32[]{:S(2)}, u32[]{:S(2)}) %collective-permute-start.6) | collective-permute-done | bytes 196640 | tf_op jit(solution)/shard_map/ppermute | solution.py:199
  37.6 1.8 %shard_map.89 = (bf16[3,128,256]{2,1,0:T(8,128)(2,1)S(1)}, f32[3,32,1152]{2,1,0:T(8,128)S(1)}, bf16[3,32,1152]{2,1,0:T(8,128)(2,1)S(1)}, f32[3,32,1152]{2,1,0:T(8,128)S(1)}, bf16[3,32,1152]{2,1,0:T(8,128)(2,1)S(1)}) custom-call(s32[6]{0:T(128)S(1)} %stack.31.info, s32[3]{0:T(128)S(1)} %bitcast.19, f32[3,128,256]{2,1,0:T(8,128)S(1)} %get-tuple-element.18.part, ...), custom_call_target="tpu_custom_call" | custom-call | tf_op jit(solution)/shard_map/pallas_call | solution.py:23
  39.4 0.0 copy-start.3
  39.4 1.0 %collective-permute-start.8 = (bf16[3,32,1152]{2,1,0:T(8,128)(2,1)S(1)}, bf16[3,32,1152]{2,1,0:T(8,128)(2,1)S(1)}, u32[]{:S(2)}, u32[]{:S(2)}) collective-permute-start(bf16[3,32,1152]{2,1,0:T(8,128)(2,1)S(1)} %get-tuple-element.21), channel_id=1, source_target_pairs={{0,4},{1,5},{2,6},{3,7},{4,0},{5,1},{6,2},{7,3},{8,12},{9,13},{10,... | collective-permute-start | bytes 663560 | tf_op jit(solution)/shard_map/ppermute | solution.py:199
  40.4 1.1 %collective-permute-start.10 = (bf16[3,32,1152]{2,1,0:T(8,128)(2,1)S(1)}, bf16[3,32,1152]{2,1,0:T(8,128)(2,1)S(1)}, u32[]{:S(2)}, u32[]{:S(2)}) collective-permute-start(bf16[3,32,1152]{2,1,0:T(8,128)(2,1)S(1)} %get-tuple-element.25), channel_id=1, source_target_pairs={{0,4},{1,5},{2,6},{3,7},{4,0},{5,1},{6,2},{7,3},{8,12},{9,13},{10,... | collective-permute-start | bytes 663560 | tf_op jit(solution)/shard_map/ppermute | solution.py:199
  41.5 6.3 %collective-permute-done.8.got = bf16[3,32,1152]{2,1,0:T(8,128)(2,1)S(1)} collective-permute-done((bf16[3,32,1152]{2,1,0:T(8,128)(2,1)S(1)}, bf16[3,32,1152]{2,1,0:T(8,128)(2,1)S(1)}, u32[]{:S(2)}, u32[]{:S(2)}) %collective-permute-start.8) | collective-permute-done | bytes 221216 | tf_op jit(solution)/shard_map/ppermute | solution.py:199
  47.8 0.6 shard_map.90
  48.4 0.7 collective-permute-start.9
  49.1 1.1 %collective-permute-done.10.got = bf16[3,32,1152]{2,1,0:T(8,128)(2,1)S(1)} collective-permute-done((bf16[3,32,1152]{2,1,0:T(8,128)(2,1)S(1)}, bf16[3,32,1152]{2,1,0:T(8,128)(2,1)S(1)}, u32[]{:S(2)}, u32[]{:S(2)}) %collective-permute-start.10) | collective-permute-done | bytes 221216 | tf_op jit(solution)/shard_map/ppermute | solution.py:199
  50.2 0.6 shard_map.91
  50.8 0.1 collective-permute-start.11
  50.9 0.0 collective-permute-done.9.u0
  50.9 9.2 %collective-permute-done.11.u2 = bf16[3,32,1152]{2,1,0:T(8,128)(2,1)S(1)} collective-permute-done((bf16[3,32,1152]{2,1,0:T(8,128)(2,1)S(1)}, bf16[3,32,1152]{2,1,0:T(8,128)(2,1)S(1)}, u32[]{:S(2)}, u32[]{:S(2)}) %collective-permute-start.11) | collective-permute-done | bytes 221216 | tf_op jit(solution)/shard_map/ppermute | solution.py:199
  60.1 0.6 shard_map.92.mine
  60.7 0.2 collective-permute-start.12
  60.9 0.4 collective-permute-start.13
  61.3 1.5 %collective-permute-done.13.other = bf16[3,32,576]{2,1,0:T(8,128)(2,1)S(1)} collective-permute-done((bf16[3,32,576]{2,1,0:T(8,128)(2,1)S(1)}, bf16[3,32,576]{2,1,0:T(8,128)(2,1)S(1)}, u32[]{:S(2)}, u32[]{:S(2)}) %collective-permute-start.13) | collective-permute-done | bytes 110624 | tf_op jit(solution)/shard_map/ppermute | solution.py:199
  62.8 0.7 shard_map.93.wanted
  63.4 0.0 collective-permute-done.12.theirs
  63.4 1.3 %shard_map.94 = (bf16[3,32,576]{2,1,0:T(8,128)(2,1)}, bf16[3,32,1152]{2,1,0:T(8,128)(2,1)S(1)}) custom-call(s32[6]{0:T(128)S(1)} %stack.31.info, f32[3,32,1152]{2,1,0:T(8,128)S(1)} %shard_map.92.mine, f32[3,32,1152]{2,1,0:T(8,128)S(1)} %collective-permute-done.12.theirs, bf16[3,32,1152]{2,1,0:T(8,128)(2,1)S(1)} %shard_map.93.wanted), custom_call_target="tpu_custom_call" | custom-call | tf_op jit(solution)/shard_map/pallas_call | solution.py:23
  64.7 0.9 collective-permute-start.14
  65.6 1.5 %collective-permute-start.15 = (bf16[3,32,1152]{2,1,0:T(8,128)(2,1)S(1)}, bf16[3,32,1152]{2,1,0:T(8,128)(2,1)S(1)}, u32[]{:S(2)}, u32[]{:S(2)}) collective-permute-start(bf16[3,32,1152]{2,1,0:T(8,128)(2,1)S(1)} %get-tuple-element.27.own), channel_id=1, source_target_pairs={{0,4},{1,24},{2,6},{3,26},{4,0},{5,28},{6,2},{7,30},{8,17},{9,13},... | collective-permute-start | bytes 663560 | tf_op jit(solution)/shard_map/ppermute | solution.py:199
  67.0 11.5 %collective-permute-done.14.r1 = bf16[3,32,1152]{2,1,0:T(8,128)(2,1)S(1)} collective-permute-done((bf16[3,32,1152]{2,1,0:T(8,128)(2,1)S(1)}, bf16[3,32,1152]{2,1,0:T(8,128)(2,1)S(1)}, u32[]{:S(2)}, u32[]{:S(2)}) %collective-permute-start.14) | collective-permute-done | bytes 221216 | tf_op jit(solution)/shard_map/ppermute | solution.py:199
  78.5 1.0 %collective-permute-start.16 = (bf16[3,32,1152]{2,1,0:T(8,128)(2,1)S(1)}, bf16[3,32,1152]{2,1,0:T(8,128)(2,1)S(1)}, u32[]{:S(2)}, u32[]{:S(2)}) collective-permute-start(bf16[3,32,1152]{2,1,0:T(8,128)(2,1)S(1)} %collective-permute-done.14.r1), channel_id=1, source_target_pairs={{0,4},{1,5},{2,6},{3,7},{4,0},{5,1},{6,2},{7,3},{8,12},{9,13},{10,... | collective-permute-start | bytes 663560 | tf_op jit(solution)/shard_map/ppermute | solution.py:199
  79.5 0.0 collective-permute-done.15.r2
  79.5 0.7 collective-permute-start.17
  80.1 4.6 %collective-permute-done.16.r3 = bf16[3,32,1152]{2,1,0:T(8,128)(2,1)S(1)} collective-permute-done((bf16[3,32,1152]{2,1,0:T(8,128)(2,1)S(1)}, bf16[3,32,1152]{2,1,0:T(8,128)(2,1)S(1)}, u32[]{:S(2)}, u32[]{:S(2)}) %collective-permute-start.16) | collective-permute-done | bytes 221216 | tf_op jit(solution)/shard_map/ppermute | solution.py:199
  84.8 0.0 collective-permute-done.17.r4
  84.8 1.5 %shard_map.95 = (f32[3,64,256]{2,1,0:T(8,128)S(1)}, bf16[3,64,256]{2,1,0:T(8,128)(2,1)S(1)}, bf16[3,128,576]{2,1,0:T(8,128)(2,1)S(1)}, bf16[3,128,576]{2,1,0:T(8,128)(2,1)S(1)}) custom-call(s32[6]{0:T(128)S(1)} %stack.31.info, bf16[3,32,1152]{2,1,0:T(8,128)(2,1)S(1)} %get-tuple-element.27.own, bf16[3,32,1152]{2,1,0:T(8,128)(2,1)S(1)} %collective-permute-done.14.r1, ...), custom_call_target="tpu_custom_call" | custom-call | tf_op jit(solution)/shard_map/pallas_call | solution.py:23
  86.3 0.1 collective-permute-start.18
  86.4 0.5 collective-permute-start.19
  86.9 1.2 %collective-permute-start.20 = (bf16[3,64,256]{2,1,0:T(8,128)(2,1)S(1)}, bf16[3,64,256]{2,1,0:T(8,128)(2,1)S(1)}, u32[]{:S(2)}, u32[]{:S(2)}) collective-permute-start(bf16[3,64,256]{2,1,0:T(8,128)(2,1)S(1)} %get-tuple-element.32), channel_id=1, source_target_pairs={{0,2},{1,3},{2,0},{3,1},{4,6},{5,7},{6,4},{7,5},{8,10},{9,11},{10,... | collective-permute-start | bytes 294920 | tf_op jit(solution)/shard_map/ppermute | solution.py:199
  88.1 3.6 %collective-permute-done.20.got = bf16[3,64,256]{2,1,0:T(8,128)(2,1)S(1)} collective-permute-done((bf16[3,64,256]{2,1,0:T(8,128)(2,1)S(1)}, bf16[3,64,256]{2,1,0:T(8,128)(2,1)S(1)}, u32[]{:S(2)}, u32[]{:S(2)}) %collective-permute-start.20) | collective-permute-done | bytes 98336 | tf_op jit(solution)/shard_map/ppermute | solution.py:199
  91.6 1.2 %shard_map.97 = bf16[3,64,256]{2,1,0:T(8,128)(2,1)} custom-call(s32[6]{0:T(128)S(1)} %stack.31.info, s32[3]{0:T(128)S(1)} %bitcast.20, f32[3,64,256]{2,1,0:T(8,128)S(1)} %get-tuple-element.31.kept, bf16[3,64,256]{2,1,0:T(8,128)(2,1)S(1)} %collective-permute-done.20.got), custom_call_target="tpu_custom_call" | custom-call | tf_op jit(solution)/shard_map/pallas_call | solution.py:23
  92.9 0.0 collective-permute-done.19.latents_got
  92.9 0.0 collective-permute-done.18.errors_got
  92.9 2.9 %shard_map.96 = bf16[6,576,256]{2,1,0:T(8,128)(2,1)} custom-call(s32[6]{0:T(128)S(1)} %stack.31.info, bf16[3,128,576]{2,1,0:T(8,128)(2,1)S(1)} %get-tuple-element.28.errors, bf16[3,128,576]{2,1,0:T(8,128)(2,1)S(1)} %collective-permute-done.18.errors_got, bf16[3,128,256]{2,1,0:T(8,128)(2,1)S(1)} %get-tuple-element.30.latents, ...), custom_call_target="tpu_custom_call" | custom-call | tf_op jit(solution)/shard_map/pallas_call | solution.py:23
  (4 shorter events, 0.0 us)
Async XLA Ops:
  0.6 32.1 %collective-permute-start.7 = (bf16[6,576,256]{2,1,0:T(8,128)(2,1)}, bf16[6,576,256]{2,1,0:T(8,128)(2,1)S(1)}, u32[]{:S(2)}, u32[]{:S(2)}) collective-permute-start(bf16[6,576,256]{2,1,0:T(8,128)(2,1)} %bitcast.13), channel_id=1, source_target_pairs={{0,1},{1,0},{2,3},{3,2},{4,5},{5,4},{6,7},{7,6},{8,9},{9,8},{10,11... | collective-permute-start | bytes 5308424 | tf_op jit(solution)/shard_map/ppermute | solution.py:199
  1.1 23.8 %collective-permute-start.5 = (bf16[3,576,256]{2,1,0:T(8,128)(2,1)}, bf16[3,576,256]{2,1,0:T(8,128)(2,1)S(1)}, u32[]{:S(2)}, u32[]{:S(2)}) collective-permute-start(bf16[3,576,256]{2,1,0:T(8,128)(2,1)} %own.1), channel_id=1, source_target_pairs={{0,1},{1,0},{2,3},{3,2},{4,5},{5,4},{6,7},{7,6},{8,9},{9,8},{10,11... | collective-permute-start | bytes 2654216 | tf_op jit(solution)/shard_map/ppermute | solution.py:199
  1.2 4.9 %collective-permute-start = (bf16[3,32,576]{2,1,0:T(8,128)(2,1)}, bf16[3,32,576]{2,1,0:T(8,128)(2,1)S(1)}, u32[]{:S(2)}, u32[]{:S(2)}) collective-permute-start(bf16[3,32,576]{2,1,0:T(8,128)(2,1)} %bitcast.15), channel_id=1, source_target_pairs={{0,1},{1,0},{2,3},{3,2},{4,5},{5,4},{6,7},{7,6},{8,9},{9,8},{10,11... | collective-permute-start | bytes 331784 | tf_op jit(solution)/shard_map/ppermute | solution.py:199
  6.1 0.9 copy-start.2
  7.7 14.4 %collective-permute-start.1 = (bf16[3,32,1152]{2,1,0:T(8,128)(2,1)S(1)}, bf16[3,32,1152]{2,1,0:T(8,128)(2,1)S(1)}, u32[]{:S(2)}, u32[]{:S(2)}) collective-permute-start(bf16[3,32,1152]{2,1,0:T(8,128)(2,1)S(1)} %shard_map.85.own), channel_id=1, source_target_pairs={{0,16},{1,8},{2,18},{3,10},{4,20},{5,12},{6,22},{7,14},{8,1},{9,25... | collective-permute-start | bytes 663560 | tf_op jit(solution)/shard_map/ppermute | solution.py:199
  11.7 12.6 %collective-permute-start.2 = (bf16[3,32,1152]{2,1,0:T(8,128)(2,1)S(1)}, bf16[3,32,1152]{2,1,0:T(8,128)(2,1)S(1)}, u32[]{:S(2)}, u32[]{:S(2)}) collective-permute-start(bf16[3,32,1152]{2,1,0:T(8,128)(2,1)S(1)} %shard_map.85.own), channel_id=1, source_target_pairs={{0,4},{1,24},{2,6},{3,26},{4,0},{5,28},{6,2},{7,30},{8,17},{9,13},... | collective-permute-start | bytes 663560 | tf_op jit(solution)/shard_map/ppermute | solution.py:199
  22.1 7.9 %collective-permute-start.3 = (bf16[3,32,1152]{2,1,0:T(8,128)(2,1)S(1)}, bf16[3,32,1152]{2,1,0:T(8,128)(2,1)S(1)}, u32[]{:S(2)}, u32[]{:S(2)}) collective-permute-start(bf16[3,32,1152]{2,1,0:T(8,128)(2,1)S(1)} %collective-permute-done.1.r1), channel_id=1, source_target_pairs={{0,4},{1,5},{2,6},{3,7},{4,0},{5,1},{6,2},{7,3},{8,12},{9,13},{10,... | collective-permute-start | bytes 663560 | tf_op jit(solution)/shard_map/ppermute | solution.py:199
  24.3 5.7 %collective-permute-start.4 = (bf16[3,32,1152]{2,1,0:T(8,128)(2,1)S(1)}, bf16[3,32,1152]{2,1,0:T(8,128)(2,1)S(1)}, u32[]{:S(2)}, u32[]{:S(2)}) collective-permute-start(bf16[3,32,1152]{2,1,0:T(8,128)(2,1)S(1)} %collective-permute-done.2.r2), channel_id=1, source_target_pairs={{1,5},{3,7},{5,1},{7,3},{8,12},{10,14},{12,8},{14,10},{17,21},{19,... | collective-permute-start | bytes 663560 | tf_op jit(solution)/shard_map/ppermute | solution.py:199
  25.0 1.2 %copy-start.1 = (bf16[3,576,256]{2,1,0:T(8,128)(2,1)S(1)}, bf16[3,576,256]{2,1,0:T(8,128)(2,1)}, u32[]{:S(2)}) copy-start(bf16[3,576,256]{2,1,0:T(8,128)(2,1)} %own.1) | copy-start | bytes 2654212
  26.8 5.9 %copy-start = (bf16[6,256,576]{1,2,0:T(8,128)(2,1)S(1)}, bf16[6,256,576]{1,2,0:T(8,128)(2,1)}, u32[]{:S(2)}) copy-start(bf16[6,256,576]{1,2,0:T(8,128)(2,1)} %param.10) | copy-start | bytes 5308420
  31.1 6.5 %copy-start.4 = (f32[3,256]{1,0:T(4,128)S(1)}, f32[3,256]{1,0:T(4,128)}, u32[]{:S(2)}) copy-start(f32[3,256]{1,0:T(4,128)} %bias.1) | copy-start | bytes 9220
  31.1 6.5 %copy-start.5 = (s32[3,1]{0,1:T(1,128)S(1)}, s32[3,1]{0,1:T(1,128)}, u32[]{:S(2)}) copy-start(s32[3,1]{0,1:T(1,128)} %param.11) | copy-start | bytes 40
  31.1 6.5 %collective-permute-start.6 = (bf16[3,128,256]{2,1,0:T(8,128)(2,1)S(1)}, bf16[3,128,256]{2,1,0:T(8,128)(2,1)S(1)}, u32[]{:S(2)}, u32[]{:S(2)}) collective-permute-start(bf16[3,128,256]{2,1,0:T(8,128)(2,1)S(1)} %get-tuple-element.19), channel_id=1, source_target_pairs={{0,2},{1,3},{2,0},{3,1},{4,6},{5,7},{6,4},{7,5},{8,10},{9,11},{10,... | collective-permute-start | bytes 589832 | tf_op jit(solution)/shard_map/ppermute | solution.py:199
  39.4 21.6 %copy-start.3 = (bf16[32,3,576]{2,0,1:T(8,128)(2,1)S(1)}, bf16[32,3,576]{2,0,1:T(8,128)(2,1)}, u32[]{:S(2)}) copy-start(bf16[32,3,576]{2,0,1:T(8,128)(2,1)} %param.7) | copy-start | bytes 331780
  39.4 8.4 %collective-permute-start.8 = (bf16[3,32,1152]{2,1,0:T(8,128)(2,1)S(1)}, bf16[3,32,1152]{2,1,0:T(8,128)(2,1)S(1)}, u32[]{:S(2)}, u32[]{:S(2)}) collective-permute-start(bf16[3,32,1152]{2,1,0:T(8,128)(2,1)S(1)} %get-tuple-element.21), channel_id=1, source_target_pairs={{0,4},{1,5},{2,6},{3,7},{4,0},{5,1},{6,2},{7,3},{8,12},{9,13},{10,... | collective-permute-start | bytes 663560 | tf_op jit(solution)/shard_map/ppermute | solution.py:199
  40.4 9.8 %collective-permute-start.10 = (bf16[3,32,1152]{2,1,0:T(8,128)(2,1)S(1)}, bf16[3,32,1152]{2,1,0:T(8,128)(2,1)S(1)}, u32[]{:S(2)}, u32[]{:S(2)}) collective-permute-start(bf16[3,32,1152]{2,1,0:T(8,128)(2,1)S(1)} %get-tuple-element.25), channel_id=1, source_target_pairs={{0,4},{1,5},{2,6},{3,7},{4,0},{5,1},{6,2},{7,3},{8,12},{9,13},{10,... | collective-permute-start | bytes 663560 | tf_op jit(solution)/shard_map/ppermute | solution.py:199
  48.4 2.5 %collective-permute-start.9 = (bf16[3,32,1152]{2,1,0:T(8,128)(2,1)S(1)}, bf16[3,32,1152]{2,1,0:T(8,128)(2,1)S(1)}, u32[]{:S(2)}, u32[]{:S(2)}) collective-permute-start(bf16[3,32,1152]{2,1,0:T(8,128)(2,1)S(1)} %get-tuple-element.23), channel_id=1, source_target_pairs={{1,24},{3,26},{5,28},{7,30},{8,17},{10,19},{12,21},{14,23},{17,8},... | collective-permute-start | bytes 663560 | tf_op jit(solution)/shard_map/ppermute | solution.py:199
  50.8 9.3 %collective-permute-start.11 = (bf16[3,32,1152]{2,1,0:T(8,128)(2,1)S(1)}, bf16[3,32,1152]{2,1,0:T(8,128)(2,1)S(1)}, u32[]{:S(2)}, u32[]{:S(2)}) collective-permute-start(bf16[3,32,1152]{2,1,0:T(8,128)(2,1)S(1)} %shard_map.91), channel_id=1, source_target_pairs={{0,16},{1,8},{2,18},{3,10},{4,20},{5,12},{6,22},{7,14},{8,1},{9,25... | collective-permute-start | bytes 663560 | tf_op jit(solution)/shard_map/ppermute | solution.py:199
  60.7 2.7 %collective-permute-start.12 = (f32[3,32,1152]{2,1,0:T(8,128)S(1)}, f32[3,32,1152]{2,1,0:T(8,128)S(1)}, u32[]{:S(2)}, u32[]{:S(2)}) collective-permute-start(f32[3,32,1152]{2,1,0:T(8,128)S(1)} %shard_map.92.mine), channel_id=1, source_target_pairs={{0,1},{1,0},{2,3},{3,2},{4,5},{5,4},{6,7},{7,6},{8,9},{9,8},{10,11... | collective-permute-start | bytes 1327112 | tf_op jit(solution)/shard_map/ppermute | solution.py:199
  60.9 1.8 %collective-permute-start.13 = (bf16[3,32,576]{2,1,0:T(8,128)(2,1)S(1)}, bf16[3,32,576]{2,1,0:T(8,128)(2,1)S(1)}, u32[]{:S(2)}, u32[]{:S(2)}) collective-permute-start(bf16[3,32,576]{2,1,0:T(8,128)(2,1)S(1)} %bitcast.17), channel_id=1, source_target_pairs={{0,1},{1,0},{2,3},{3,2},{4,5},{5,4},{6,7},{7,6},{8,9},{9,8},{10,11... | collective-permute-start | bytes 331784 | tf_op jit(solution)/shard_map/ppermute | solution.py:199
  64.7 13.8 %collective-permute-start.14 = (bf16[3,32,1152]{2,1,0:T(8,128)(2,1)S(1)}, bf16[3,32,1152]{2,1,0:T(8,128)(2,1)S(1)}, u32[]{:S(2)}, u32[]{:S(2)}) collective-permute-start(bf16[3,32,1152]{2,1,0:T(8,128)(2,1)S(1)} %get-tuple-element.27.own), channel_id=1, source_target_pairs={{0,16},{1,8},{2,18},{3,10},{4,20},{5,12},{6,22},{7,14},{8,1},{9,25... | collective-permute-start | bytes 663560 | tf_op jit(solution)/shard_map/ppermute | solution.py:199
  65.6 13.9 %collective-permute-start.15 = (bf16[3,32,1152]{2,1,0:T(8,128)(2,1)S(1)}, bf16[3,32,1152]{2,1,0:T(8,128)(2,1)S(1)}, u32[]{:S(2)}, u32[]{:S(2)}) collective-permute-start(bf16[3,32,1152]{2,1,0:T(8,128)(2,1)S(1)} %get-tuple-element.27.own), channel_id=1, source_target_pairs={{0,4},{1,24},{2,6},{3,26},{4,0},{5,28},{6,2},{7,30},{8,17},{9,13},... | collective-permute-start | bytes 663560 | tf_op jit(solution)/shard_map/ppermute | solution.py:199
  78.5 6.3 %collective-permute-start.16 = (bf16[3,32,1152]{2,1,0:T(8,128)(2,1)S(1)}, bf16[3,32,1152]{2,1,0:T(8,128)(2,1)S(1)}, u32[]{:S(2)}, u32[]{:S(2)}) collective-permute-start(bf16[3,32,1152]{2,1,0:T(8,128)(2,1)S(1)} %collective-permute-done.14.r1), channel_id=1, source_target_pairs={{0,4},{1,5},{2,6},{3,7},{4,0},{5,1},{6,2},{7,3},{8,12},{9,13},{10,... | collective-permute-start | bytes 663560 | tf_op jit(solution)/shard_map/ppermute | solution.py:199
  79.5 5.3 %collective-permute-start.17 = (bf16[3,32,1152]{2,1,0:T(8,128)(2,1)S(1)}, bf16[3,32,1152]{2,1,0:T(8,128)(2,1)S(1)}, u32[]{:S(2)}, u32[]{:S(2)}) collective-permute-start(bf16[3,32,1152]{2,1,0:T(8,128)(2,1)S(1)} %collective-permute-done.15.r2), channel_id=1, source_target_pairs={{1,5},{3,7},{5,1},{7,3},{8,12},{10,14},{12,8},{14,10},{17,21},{19,... | collective-permute-start | bytes 663560 | tf_op jit(solution)/shard_map/ppermute | solution.py:199
  86.3 6.6 %collective-permute-start.18 = (bf16[3,128,576]{2,1,0:T(8,128)(2,1)S(1)}, bf16[3,128,576]{2,1,0:T(8,128)(2,1)S(1)}, u32[]{:S(2)}, u32[]{:S(2)}) collective-permute-start(bf16[3,128,576]{2,1,0:T(8,128)(2,1)S(1)} %get-tuple-element.29), channel_id=1, source_target_pairs={{0,1},{1,0},{2,3},{3,2},{4,5},{5,4},{6,7},{7,6},{8,9},{9,8},{10,11... | collective-permute-start | bytes 1327112 | tf_op jit(solution)/shard_map/ppermute | solution.py:199
  86.4 6.5 %collective-permute-start.19 = (bf16[3,128,256]{2,1,0:T(8,128)(2,1)S(1)}, bf16[3,128,256]{2,1,0:T(8,128)(2,1)S(1)}, u32[]{:S(2)}, u32[]{:S(2)}) collective-permute-start(bf16[3,128,256]{2,1,0:T(8,128)(2,1)S(1)} %get-tuple-element.30.latents), channel_id=1, source_target_pairs={{0,1},{1,0},{2,3},{3,2},{4,5},{5,4},{6,7},{7,6},{8,9},{9,8},{10,11... | collective-permute-start | bytes 589832 | tf_op jit(solution)/shard_map/ppermute | solution.py:199
  86.9 4.8 %collective-permute-start.20 = (bf16[3,64,256]{2,1,0:T(8,128)(2,1)S(1)}, bf16[3,64,256]{2,1,0:T(8,128)(2,1)S(1)}, u32[]{:S(2)}, u32[]{:S(2)}) collective-permute-start(bf16[3,64,256]{2,1,0:T(8,128)(2,1)S(1)} %get-tuple-element.32), channel_id=1, source_target_pairs={{0,2},{1,3},{2,0},{3,1},{4,6},{5,7},{6,4},{7,5},{8,10},{9,11},{10,... | collective-permute-start | bytes 294920 | tf_op jit(solution)/shard_map/ppermute | solution.py:199

commit v2 on v1

v2 whole, which is shorter than its diff:
```python
import functools

import jax
import jax.numpy as jnp
from jax import lax
from jax.experimental import pallas as pl
from jax.experimental.pallas import tpu as pltpu
from jax.sharding import PartitionSpec as P

BF = jnp.bfloat16
F32 = jnp.float32
AXES = ("lat", "tok")


def block_index(source, target, layers):
    return source * layers - source * (source - 1) // 2 + (target - source)


def fused(body, outs, *args, scratch=(), scalars=1):
    specs = [pl.BlockSpec(memory_space=pltpu.SMEM)] * scalars
    specs += [pl.BlockSpec(memory_space=pltpu.VMEM)] * (len(args) - scalars)
    out_shape = [jax.ShapeDtypeStruct(s, d) for s, d in outs]
    return pl.pallas_call(
        body,
        out_shape=out_shape,
        in_specs=specs,
        out_specs=[pl.BlockSpec(memory_space=pltpu.VMEM)] * len(outs),
        scratch_shapes=[pltpu.VMEM(s, d) for s, d in scratch],
        compiler_params=pltpu.CompilerParams(vmem_limit_bytes=40 * 2**20),
    )(*args)


HOME, CORE, NEAR = 0, 1, 2


def stack_kernel(info, own, other, out):
    rows = own.shape[1]
    core = info[CORE]
    out[:, pl.ds(pl.multiple_of(core * rows, rows), rows), :] = own[...]
    out[:, pl.ds(pl.multiple_of((1 - core) * rows, rows), rows), :] = other[...]


def place(info, own, r1, r2, r3, r4, out):
    rows = own.shape[1]

    @pl.when(info[HOME] != 0)
    def _():
        out[:, :rows, :] = own[...]
        out[:, rows : 2 * rows, :] = r2[...]

    @pl.when(info[HOME] == 0)
    def _():
        out[:, :rows, :] = r2[...]
        out[:, rows : 2 * rows, :] = r4[...]

    out[:, 2 * rows : 3 * rows, :] = r1[...]
    out[:, 3 * rows :, :] = r3[...]


def encode_kernel(info, own, r1, r2, r3, r4, weight, part, sent, held):
    place(info, own, r1, r2, r3, r4, held)
    for layer in range(part.shape[0]):
        value = jnp.dot(held[layer], weight[layer], preferred_element_type=F32)
        part[layer] = value
        sent[layer] = value.astype(BF)


def decode_kernel(counts, part, got, bias, weight, latents, kept0, kept1, sent0, sent1):
    kept, sent = (kept0, kept1), (sent0, sent1)
    layers, held, width = part.shape
    rows = kept0.shape[1]
    for layer in range(layers):
        live = lax.broadcasted_iota(jnp.int32, (held, width), 1) < counts[layer]
        pre = part[layer] + got[layer].astype(F32) + bias[layer : layer + 1, :]
        latents[layer] = jnp.where(live, jnp.maximum(pre, 0.0), 0.0).astype(BF)
    for target in range(layers):
        total = None
        for source in range(target + 1):
            value = lax.dot_general(
                latents[source],
                weight[block_index(source, target, layers)],
                (((1,), (1,)), ((), ())),
                preferred_element_type=F32,
            )
            total = value if total is None else total + value
        for i in range(2):
            kept[i][target] = total[2 * i * rows : (2 * i + 1) * rows]
            sent[i][target] = total[(2 * i + 1) * rows : (2 * i + 2) * rows].astype(BF)


def backward_kernel(info, own, r1, r2, r3, r4, weight, kept, sent, held):
    place(info, own, r1, r2, r3, r4, held)
    layers, half = kept.shape[0], kept.shape[1]
    for source in range(layers):
        total = None
        for target in range(source, layers):
            value = jnp.dot(
                held[target], weight[block_index(source, target, layers)], preferred_element_type=F32
            )
            total = value if total is None else total + value
        stays = info[NEAR] != 0
        kept[source] = jnp.where(stays, total[:half], total[half:])
        sent[source] = jnp.where(stays, total[half:], total[:half]).astype(BF)


def weight_grad_kernel(info, held, errors_got, latents, latents_got, out, own):
    layers = latents.shape[0]
    width = errors_got.shape[2]
    contract = (((0,), (0,)), ((), ()))

    @pl.when(info[CORE] == 0)
    def _():
        own[...] = held[:, :, :width]

    @pl.when(info[CORE] != 0)
    def _():
        own[...] = held[:, :, width:]

    for source in range(layers):
        values = jnp.concatenate([latents[source], latents_got[source]], 0)
        for target in range(source, layers):
            rows = jnp.concatenate([own[target], errors_got[target]], 0)
            total = lax.dot_general(rows, values, contract, preferred_element_type=F32)
            out[block_index(source, target, layers)] = total.astype(BF)


def make_paired(n_tok):
    places = [(z, y, x, c) for z in range(n_tok) for y in range(2) for x in range(n_tok // 2) for c in range(2)]

    def swap(value, where):
        pairs = []
        for i, (z, y, x, c) in enumerate(places):
            to = where(z, y, x, c, c == z % 2)
            if to is not None:
                pairs.append((i, places.index(to)))
        return lax.ppermute(value, AXES, pairs)

    def over_c(value):
        return swap(value, lambda z, y, x, c, home: (z, y, x, 1 - c))

    def over_x(value):
        return swap(value, lambda z, y, x, c, home: (z, y, 1 - x, c))

    def over_y(value):
        return swap(value, lambda z, y, x, c, home: (z, 1 - y, x, c))

    def over_y_away(value):
        return swap(value, lambda z, y, x, c, home: None if home else (z, 1 - y, x, c))

    def over_z2_z1(value):
        return swap(value, lambda z, y, x, c, home: (z ^ 2, y, x, c) if home else (z ^ 1, y, x, 1 - c))

    def over_y_z3(value):
        return swap(value, lambda z, y, x, c, home: (z, 1 - y, x, c) if home else (z ^ 3, y, x, 1 - c))

    def over_z3_away(value):
        return swap(value, lambda z, y, x, c, home: None if home else (z ^ 3, y, x, 1 - c))

    def gather(own):
        r1 = over_z2_z1(own)
        r2 = over_y_z3(own)
        return own, r1, r2, over_y(r1), over_y_away(r2)

    def local(inputs, targets, enc_weight, enc_bias, dec_weight, counts):
        rows, layers, width = inputs.shape
        latent_width = enc_weight.shape[2]
        both = 2 * width
        held = rows * n_tok
        lat, tok = lax.axis_index("lat"), lax.axis_index("tok")
        z, y, x, c = lat // 2, lat % 2, tok // 2, tok % 2
        home = z % 2 == c
        near = jnp.where(home, z, z ^ 3) // 2 == x
        info = jnp.stack([home, c, near]).astype(jnp.int32)
        dec_t = jnp.swapaxes(dec_weight, 1, 2)
        blocks = dec_t.shape[0]
        own_in, own_want = jnp.swapaxes(inputs, 0, 1), jnp.swapaxes(targets, 0, 1)

        def spread(own, first):
            rest = jnp.zeros_like(own)
            return jnp.where(first, jnp.concatenate([own, rest], 2), jnp.concatenate([rest, own], 2))

        def join(own, other):
            own = lax.optimization_barrier(spread(own, c == 0))
            left = lax.broadcasted_iota(jnp.int32, own.shape, 2) < width
            return jnp.where(left == (c == 0), own, spread(other, c != 0))

        block = join(own_in, over_c(own_in))
        block, enc_weight, dec_t, own_want = lax.optimization_barrier((block, enc_weight, dec_t, own_want))
        arrived = gather(block)
        (enc_all,) = fused(stack_kernel, [((layers, both, latent_width), BF)], info, enc_weight, over_c(enc_weight))
        (dec_all,) = fused(stack_kernel, [((blocks, both, latent_width), BF)], info, dec_t, over_c(dec_t))
        wanted = join(own_want, over_c(own_want))

        tile = (layers, held, latent_width)
        part, sent = fused(
            encode_kernel,
            [(tile, F32), (tile, BF)],
            info,
            *arrived,
            enc_all,
            scratch=[((layers, held, both), BF)],
        )
        piece = (layers, rows, both)
        latents, q0, q2, q1, q3 = fused(
            decode_kernel,
            [(tile, BF), (piece, F32), (piece, F32), (piece, BF), (piece, BF)],
            counts[:, 0],
            part,
            over_x(sent),
            enc_bias,
            dec_all,
        )
        q1, q3 = over_y(q1), over_y(q3)
        total = q0 + q1.astype(F32)
        u0 = over_z3_away(total.astype(BF))
        u2 = over_z2_z1((q2 + q3.astype(F32)).astype(BF))
        mine = jnp.where(home, total, u0.astype(F32)) + u2.astype(F32)
        full = mine + over_c(mine)
        errors = (full - wanted.astype(F32)).astype(BF)
        recon = jnp.where(c == 0, full[:, :, :width], full[:, :, width:]).astype(BF)
        arrived = gather(errors)
        latents_got = over_c(latents)
        arrived, recon, latents_got = lax.optimization_barrier((arrived, recon, latents_got))
        narrow = (layers, held // 2, latent_width)
        kept, sent, all_errors = fused(
            backward_kernel,
            [(narrow, F32), (narrow, BF), ((layers, held, both), BF)],
            info,
            *arrived,
            dec_all,
        )
        got = over_x(sent)
        other = jnp.where(c == 0, all_errors[:, :, width:], all_errors[:, :, :width])
        (grads,) = fused(
            weight_grad_kernel,
            [((blocks, width, latent_width), BF)],
            info,
            all_errors,
            over_c(other),
            latents,
            latents_got,
            scratch=[((layers, held, width), BF)],
        )
        got, grads = lax.optimization_barrier((got, grads))
        total = kept + got.astype(F32)
        flipped = jnp.concatenate([total[:, rows:], total[:, :rows]], 1)
        live = (lax.broadcasted_iota(jnp.int32, (layers, latent_width), 1) < counts)[:, None, :]
        latent_grad = jnp.where(live, jnp.where(y == 0, total, flipped), 0.0).astype(BF)
        return jnp.swapaxes(recon, 0, 1), jnp.swapaxes(grads, 1, 2), jnp.swapaxes(latent_grad, 0, 1)

    return local


def general(inputs, targets, enc_weight, enc_bias, dec_weight, counts):
    layers = inputs.shape[1]
    width = enc_weight.shape[2]
    live = (lax.broadcasted_iota(jnp.int32, (layers, width), 1) < counts)[None]
    gathered = lax.all_gather(inputs, "lat", axis=0, tiled=True)
    part = jnp.einsum("tld,ldk->tlk", gathered, enc_weight, preferred_element_type=F32)
    preact = lax.psum(part, "tok") + enc_bias[None]
    latents = jnp.where(live, jnp.maximum(preact, 0.0), 0.0).astype(BF)
    recons = []
    for target in range(layers):
        recons.append(
            sum(
                jnp.dot(
                    latents[:, source],
                    dec_weight[block_index(source, target, layers)],
                    preferred_element_type=F32,
                )
                for source in range(target + 1)
            )
        )
    full = lax.psum_scatter(jnp.stack(recons, 1), "lat", scatter_dimension=0, tiled=True)
    own_errors = (full - targets.astype(F32)).astype(BF)
    errors = lax.all_gather(own_errors, "lat", axis=0, tiled=True)
    grads, sums = [], []
    for source in range(layers):
        total = 0.0
        for target in range(source, layers):
            weight = dec_weight[block_index(source, target, layers)]
            total = total + lax.dot_general(
                errors[:, target], weight, (((1,), (1,)), ((), ())), preferred_element_type=F32
            )
            grads.append(
                lax.dot_general(
                    latents[:, source],
                    errors[:, target],
                    (((0,), (0,)), ((), ())),
                    preferred_element_type=F32,
                ).astype(BF)
            )
        sums.append(total)
    latent_sum = lax.psum_scatter(jnp.stack(sums, 1), "tok", scatter_dimension=0, tiled=True)
    latent_grad = jnp.where(live, latent_sum, 0.0).astype(BF)
    return full.astype(BF), jnp.stack(grads, 0), latent_grad


def solution(mesh):
    n_lat, n_tok = mesh.shape["lat"], mesh.shape["tok"]
    in_specs = (
        P("lat", None, "tok"),
        P("lat", None, "tok"),
        P(None, "tok", "lat"),
        P(None, "lat"),
        P(None, "lat", "tok"),
        P(None, "lat"),
    )
    out_specs = (P("lat", None, "tok"), P(None, "lat", "tok"), P("tok", None, "lat"))
    paired = n_lat == 2 * n_tok and n_tok == 4
    local = make_paired(n_tok) if paired else general
    return jax.shard_map(local, mesh=mesh, in_specs=in_specs, out_specs=out_specs, check_vma=False)
```

time: 95.9 us -> 84.5 us (0.88)
  waiting for transfers between devices: 58.4 us -> 51.3 us
  Pallas kernels: 14.3 us -> 8.44 us
  other arithmetic: 0 us -> 3.5 us
  starting transfers between devices: 20.1 us -> 18.9 us
  local copies, waits for them, and re-layouts: 2.17 us -> 1.2 us
    ppermute x21, waiting for transfers between devices: 58.4 us -> 51.3 us  [swap(): return lax.ppermute(value, AXES, pairs)]
    pallas_call x13 -> x6, Pallas kernels: 14.3 us -> 8.44 us  [fused(): pl.pallas_call(body, out_shape=out_shape, in_specs=specs, out_specs=[pl.B...]
    select_n x0 -> x4, other arithmetic: none -> 1.5 us  [the longest x2 1.19 us: spread(): jnp.where(first, jnp.concatenate([own, rest], 2), jnp.concatenate([rest,...]
    ppermute x21, starting transfers between devices: 20.1 us -> 18.9 us  [swap(): return lax.ppermute(value, AXES, pairs)]
    convert_element_type x0 -> x4, other arithmetic: none -> 1.04 us  [the longest x1 0.75 us: local(): recon = jnp.where(c == 0, full[:, :, :width], full[:, :, width:]).astype(BF)]
    unnamed x12 -> x10, local copies, waits for them, and re-layouts: 2.09 us -> 1.19 us
  transfers between devices with their start and end apart: 21 -> 21, of which waited for: 11 -> 12; matrix products, arithmetic and copies ran while one was open for 0% -> 3% of each run, Pallas kernels for 7% -> 6%
where the time goes in v2:
time: 84.5 us; the launch traced here: 84.2 us
  waiting for transfers between devices  51.3 us (61%)
  starting transfers between devices  18.9 us (22%)
  Pallas kernels  8.44 us (10%)
  other arithmetic  3.5 us (4%)
  local copies, waits for them, and re-layouts  1.2 us (1%)
    ppermute x21, waiting for transfers between devices, swap(): return lax.ppermute(value, AXES, pairs)  51.3 us
    ppermute x21, starting transfers between devices, swap(): return lax.ppermute(value, AXES, pairs)  18.9 us
    pallas_call x6, Pallas kernels, fused(): pl.pallas_call(body, out_shape=out_shape, in_specs=specs, out_specs=[pl.B...  8.44 us
  transfers between devices with their start and end apart: 21, of which 12 were waited for; matrix products, arithmetic and copies ran while one was open for 3% of the time, Pallas kernels for 6%

profile of v2, /device:TPU:0, one launch (start us, length us, event | category | flops | bytes accessed | tf_op | source)
XLA Modules:
  0.0 84.2 jit_solution(17557740058913076366)
XLA Ops:
  0.6 0.5 collective-permute-start
  1.1 1.1 %pad_select_fusion.1 = bf16[3,32,1152]{2,1,0:T(8,128)(2,1)S(1)} fusion(bf16[3,32,576]{2,1,0:T(8,128)(2,1)} %bitcast.18, pred[]{:T(512)S(6)} %eq.34), kind=kLoop, calls=%fused_computation.10 | loop fusion | flops 110592 | bytes 331777 | tf_op jit(solution)/shard_map/jit(_where)/select_n | solution.py:180
  2.2 0.1 collective-permute-done
  2.3 0.1 select_select_fusion.own
  2.4 0.4 collective-permute-start.7
  2.9 0.1 collective-permute-start.5
  3.0 3.9 %collective-permute-start.1 = (bf16[3,32,1152]{2,1,0:T(8,128)(2,1)S(1)}, bf16[3,32,1152]{2,1,0:T(8,128)(2,1)S(1)}, u32[]{:S(2)}, u32[]{:S(2)}) collective-permute-start(bf16[3,32,1152]{2,1,0:T(8,128)(2,1)S(1)} %select_select_fusion.own), channel_id=1, source_target_pairs={{0,16},{1,8},{2,18},{3,10},{4,20},{5,12},{6,22},{7,14},{8,1},{9,25... | collective-permute-start | bytes 663560 | tf_op jit(solution)/shard_map/ppermute | solution.py:136
  7.0 1.5 %collective-permute-start.2 = (bf16[3,32,1152]{2,1,0:T(8,128)(2,1)S(1)}, bf16[3,32,1152]{2,1,0:T(8,128)(2,1)S(1)}, u32[]{:S(2)}, u32[]{:S(2)}) collective-permute-start(bf16[3,32,1152]{2,1,0:T(8,128)(2,1)S(1)} %select_select_fusion.own), channel_id=1, source_target_pairs={{0,4},{1,24},{2,6},{3,26},{4,0},{5,28},{6,2},{7,30},{8,17},{9,13},... | collective-permute-start | bytes 663560 | tf_op jit(solution)/shard_map/ppermute | solution.py:136
  8.5 8.9 %collective-permute-done.1.r1 = bf16[3,32,1152]{2,1,0:T(8,128)(2,1)S(1)} collective-permute-done((bf16[3,32,1152]{2,1,0:T(8,128)(2,1)S(1)}, bf16[3,32,1152]{2,1,0:T(8,128)(2,1)S(1)}, u32[]{:S(2)}, u32[]{:S(2)}) %collective-permute-start.1) | collective-permute-done | bytes 221216 | tf_op jit(solution)/shard_map/ppermute | solution.py:136
  17.4 2.2 %collective-permute-start.3 = (bf16[3,32,1152]{2,1,0:T(8,128)(2,1)S(1)}, bf16[3,32,1152]{2,1,0:T(8,128)(2,1)S(1)}, u32[]{:S(2)}, u32[]{:S(2)}) collective-permute-start(bf16[3,32,1152]{2,1,0:T(8,128)(2,1)S(1)} %collective-permute-done.1.r1), channel_id=1, source_target_pairs={{0,4},{1,5},{2,6},{3,7},{4,0},{5,1},{6,2},{7,3},{8,12},{9,13},{10,... | collective-permute-start | bytes 663560 | tf_op jit(solution)/shard_map/ppermute | solution.py:136
  19.5 0.0 collective-permute-done.2.r2
  19.5 1.3 %collective-permute-start.4 = (bf16[3,32,1152]{2,1,0:T(8,128)(2,1)S(1)}, bf16[3,32,1152]{2,1,0:T(8,128)(2,1)}, u32[]{:S(2)}, u32[]{:S(2)}) collective-permute-start(bf16[3,32,1152]{2,1,0:T(8,128)(2,1)S(1)} %collective-permute-done.2.r2), channel_id=1, source_target_pairs={{1,5},{3,7},{5,1},{7,3},{8,12},{10,14},{12,8},{14,10},{17,21},{19,... | collective-permute-start | bytes 663560 | tf_op jit(solution)/shard_map/ppermute | solution.py:136
  20.9 0.1 pad_add_fusion.info
  21.0 0.0 collective-permute-done.5.other
  21.0 1.2 %copy-done.1 = bf16[3,576,256]{2,1,0:T(8,128)(2,1)S(1)} copy-done((bf16[3,576,256]{2,1,0:T(8,128)(2,1)S(1)}, bf16[3,576,256]{2,1,0:T(8,128)(2,1)}, u32[]{:S(2)}) %copy-start.1) | copy-done | bytes 884760
  22.1 0.7 shard_map.85.weight
  22.8 0.0 copy-start
  22.8 2.5 %collective-permute-done.3.r3 = bf16[3,32,1152]{2,1,0:T(8,128)(2,1)S(1)} collective-permute-done((bf16[3,32,1152]{2,1,0:T(8,128)(2,1)S(1)}, bf16[3,32,1152]{2,1,0:T(8,128)(2,1)S(1)}, u32[]{:S(2)}, u32[]{:S(2)}) %collective-permute-start.3) | collective-permute-done | bytes 221216 | tf_op jit(solution)/shard_map/ppermute | solution.py:136
  25.3 0.0 collective-permute-done.4.r4
  25.3 1.4 %shard_map.86 = (f32[3,128,256]{2,1,0:T(8,128)S(1)}, bf16[3,128,256]{2,1,0:T(8,128)(2,1)S(1)}) custom-call(s32[3]{0:T(128)S(1)} %pad_add_fusion.info, bf16[3,32,1152]{2,1,0:T(8,128)(2,1)S(1)} %select_select_fusion.own, bf16[3,32,1152]{2,1,0:T(8,128)(2,1)S(1)} %collective-permute-done.1.r1, bf16[3,32,1152]{2,1,0:T(8,128)(2,1)S(1)} %collective-permute-done.2.r2, ...), custom_call_target="tpu_custom_call" | custom-call | tf_op jit(solution)/shard_map/pallas_call | solution.py:23
  26.7 0.0 copy-start.2
  26.7 0.0 copy-start.3
  26.7 1.6 %collective-permute-start.6 = (bf16[3,128,256]{2,1,0:T(8,128)(2,1)S(1)}, bf16[3,128,256]{2,1,0:T(8,128)(2,1)S(1)}, u32[]{:S(2)}, u32[]{:S(2)}) collective-permute-start(bf16[3,128,256]{2,1,0:T(8,128)(2,1)S(1)} %get-tuple-element.29), channel_id=1, source_target_pairs={{0,2},{1,3},{2,0},{3,1},{4,6},{5,7},{6,4},{7,5},{8,10},{9,11},{10,... | collective-permute-start | bytes 589832 | tf_op jit(solution)/shard_map/ppermute | solution.py:136
  28.3 0.0 collective-permute-done.7.other
  28.3 0.8 shard_map.87.weight
  29.1 4.1 %collective-permute-done.6.got = bf16[3,128,256]{2,1,0:T(8,128)(2,1)S(1)} collective-permute-done((bf16[3,128,256]{2,1,0:T(8,128)(2,1)S(1)}, bf16[3,128,256]{2,1,0:T(8,128)(2,1)S(1)}, u32[]{:S(2)}, u32[]{:S(2)}) %collective-permute-start.6) | collective-permute-done | bytes 196640 | tf_op jit(solution)/shard_map/ppermute | solution.py:136
  33.3 1.7 %shard_map.88 = (bf16[3,128,256]{2,1,0:T(8,128)(2,1)S(1)}, f32[3,32,1152]{2,1,0:T(8,128)S(1)}, f32[3,32,1152]{2,1,0:T(8,128)S(1)}, bf16[3,32,1152]{2,1,0:T(8,128)(2,1)S(1)}, bf16[3,32,1152]{2,1,0:T(8,128)(2,1)S(1)}) custom-call(s32[3]{0:T(128)S(1)} %bitcast.13, f32[3,128,256]{2,1,0:T(8,128)S(1)} %get-tuple-element.28.part, ...), custom_call_target="tpu_custom_call" | custom-call | tf_op jit(solution)/shard_map/pallas_call | solution.py:23
  35.0 0.0 copy-start.4
  35.0 1.0 %collective-permute-start.10 = (bf16[3,32,1152]{2,1,0:T(8,128)(2,1)S(1)}, bf16[3,32,1152]{2,1,0:T(8,128)(2,1)S(1)}, u32[]{:S(2)}, u32[]{:S(2)}) collective-permute-start(bf16[3,32,1152]{2,1,0:T(8,128)(2,1)S(1)} %get-tuple-element.34), channel_id=1, source_target_pairs={{0,4},{1,5},{2,6},{3,7},{4,0},{5,1},{6,2},{7,3},{8,12},{9,13},{10,... | collective-permute-start | bytes 663560 | tf_op jit(solution)/shard_map/ppermute | solution.py:136
  36.0 1.1 %collective-permute-start.8 = (bf16[3,32,1152]{2,1,0:T(8,128)(2,1)S(1)}, bf16[3,32,1152]{2,1,0:T(8,128)(2,1)S(1)}, u32[]{:S(2)}, u32[]{:S(2)}) collective-permute-start(bf16[3,32,1152]{2,1,0:T(8,128)(2,1)S(1)} %get-tuple-element.32), channel_id=1, source_target_pairs={{0,4},{1,5},{2,6},{3,7},{4,0},{5,1},{6,2},{7,3},{8,12},{9,13},{10,... | collective-permute-start | bytes 663560 | tf_op jit(solution)/shard_map/ppermute | solution.py:136
  37.1 6.3 %collective-permute-done.10 = bf16[3,32,1152]{2,1,0:T(8,128)(2,1)S(1)} collective-permute-done((bf16[3,32,1152]{2,1,0:T(8,128)(2,1)S(1)}, bf16[3,32,1152]{2,1,0:T(8,128)(2,1)S(1)}, u32[]{:S(2)}, u32[]{:S(2)}) %collective-permute-start.10) | collective-permute-done | bytes 221216 | tf_op jit(solution)/shard_map/ppermute | solution.py:136
  43.5 0.1 collective-permute-start.11
  43.5 2.3 %collective-permute-done.8 = bf16[3,32,1152]{2,1,0:T(8,128)(2,1)S(1)} collective-permute-done((bf16[3,32,1152]{2,1,0:T(8,128)(2,1)S(1)}, bf16[3,32,1152]{2,1,0:T(8,128)(2,1)S(1)}, u32[]{:S(2)}, u32[]{:S(2)}) %collective-permute-start.8) | collective-permute-done | bytes 221216 | tf_op jit(solution)/shard_map/ppermute | solution.py:136
  45.8 0.1 fusion
  45.9 0.7 collective-permute-start.9
  46.6 8.1 %collective-permute-done.11 = bf16[3,32,1152]{2,1,0:T(8,128)(2,1)S(1)} collective-permute-done((bf16[3,32,1152]{2,1,0:T(8,128)(2,1)S(1)}, bf16[3,32,1152]{2,1,0:T(8,128)(2,1)S(1)}, u32[]{:S(2)}, u32[]{:S(2)}) %collective-permute-start.11) | collective-permute-done | bytes 221216 | tf_op jit(solution)/shard_map/ppermute | solution.py:136
  54.6 0.0 collective-permute-done.9
  54.6 0.1 convert_add_fusion
  54.7 0.1 collective-permute-start.12
  54.8 0.5 collective-permute-start.13
  55.3 0.1 pad_select_fusion
  55.4 1.3 %collective-permute-done.13 = bf16[3,32,576]{2,1,0:T(8,128)(2,1)S(1)} collective-permute-done((bf16[3,32,576]{2,1,0:T(8,128)(2,1)S(1)}, bf16[3,32,576]{2,1,0:T(8,128)(2,1)S(1)}, u32[]{:S(2)}, u32[]{:S(2)}) %collective-permute-start.13) | collective-permute-done | bytes 110624 | tf_op jit(solution)/shard_map/ppermute | solution.py:136
  56.8 0.0 collective-permute-done.12
  56.8 0.2 subtract_convert_fusion
  57.0 0.1 collective-permute-start.14
  57.0 0.2 collective-permute-start.15
  57.2 1.9 %collective-permute-start.18 = (bf16[3,128,256]{2,1,0:T(8,128)(2,1)S(1)}, bf16[3,128,256]{2,1,0:T(8,128)(2,1)S(1)}, u32[]{:S(2)}, u32[]{:S(2)}) collective-permute-start(bf16[3,128,256]{2,1,0:T(8,128)(2,1)S(1)} %get-tuple-element.36.latents), channel_id=1, source_target_pairs={{0,1},{1,0},{2,3},{3,2},{4,5},{5,4},{6,7},{7,6},{8,9},{9,8},{10,11... | collective-permute-start | bytes 589832 | tf_op jit(solution)/shard_map/ppermute | solution.py:136
  59.1 11.6 %collective-permute-done.14.r1 = bf16[3,32,1152]{2,1,0:T(8,128)(2,1)S(1)} collective-permute-done((bf16[3,32,1152]{2,1,0:T(8,128)(2,1)S(1)}, bf16[3,32,1152]{2,1,0:T(8,128)(2,1)S(1)}, u32[]{:S(2)}, u32[]{:S(2)}) %collective-permute-start.14) | collective-permute-done | bytes 221216 | tf_op jit(solution)/shard_map/ppermute | solution.py:136
  70.6 0.0 collective-permute-start.16
  70.6 0.0 collective-permute-done.15.r2
  70.6 0.7 collective-permute-start.17
  71.3 0.8 fusion.1
  72.1 0.0 collective-permute-done.18.latents_got
  72.1 4.6 %collective-permute-done.16.r3 = bf16[3,32,1152]{2,1,0:T(8,128)(2,1)S(1)} collective-permute-done((bf16[3,32,1152]{2,1,0:T(8,128)(2,1)S(1)}, bf16[3,32,1152]{2,1,0:T(8,128)(2,1)S(1)}, u32[]{:S(2)}, u32[]{:S(2)}) %collective-permute-start.16) | collective-permute-done | bytes 221216 | tf_op jit(solution)/shard_map/ppermute | solution.py:136
  76.7 0.0 collective-permute-done.17.r4
  76.7 1.3 %shard_map.89 = (f32[3,64,256]{2,1,0:T(8,128)S(1)}, bf16[3,64,256]{2,1,0:T(8,128)(2,1)S(1)}, bf16[3,128,1152]{2,1,0:T(8,128)(2,1)S(1)}) custom-call(s32[3]{0:T(128)S(1)} %pad_add_fusion.info, bf16[3,32,1152]{2,1,0:T(8,128)(2,1)S(1)} %get-tuple-element.38.own, bf16[3,32,1152]{2,1,0:T(8,128)(2,1)S(1)} %collective-permute-done.14.r1, ...), custom_call_target="tpu_custom_call" | custom-call | tf_op jit(solution)/shard_map/pallas_call | solution.py:23
  78.0 0.2 slice_select_fusion
  78.2 0.1 collective-permute-start.20
  78.3 1.0 %collective-permute-start.19 = (bf16[3,64,256]{2,1,0:T(8,128)(2,1)S(1)}, bf16[3,64,256]{2,1,0:T(8,128)(2,1)S(1)}, u32[]{:S(2)}, u32[]{:S(2)}) collective-permute-start(bf16[3,64,256]{2,1,0:T(8,128)(2,1)S(1)} %get-tuple-element.43), channel_id=1, source_target_pairs={{0,2},{1,3},{2,0},{3,1},{4,6},{5,7},{6,4},{7,5},{8,10},{9,11},{10,... | collective-permute-start | bytes 294920 | tf_op jit(solution)/shard_map/ppermute | solution.py:136
  79.3 0.1 iota_compare_fusion.1
  79.4 0.7 collective-permute-done.20.errors_got
  80.1 2.6 %shard_map.90 = bf16[6,576,256]{2,1,0:T(8,128)(2,1)} custom-call(s32[3]{0:T(128)S(1)} %pad_add_fusion.info, bf16[3,128,1152]{2,1,0:T(8,128)(2,1)S(1)} %get-tuple-element.44.held, bf16[3,128,576]{2,1,0:T(8,128)(2,1)S(1)} %collective-permute-done.20.errors_got, bf16[3,128,256]{2,1,0:T(8,128)(2,1)S(1)} %get-tuple-element.36.latents, ...), custom_call_target="tpu_custom_call" | custom-call | tf_op jit(solution)/shard_map/pallas_call | solution.py:23
  82.7 0.8 collective-permute-done.19
  83.5 0.7 fusion.4
  (9 shorter events, 0.1 us)
Async XLA Ops:
  0.6 1.7 %collective-permute-start = (bf16[3,32,576]{2,1,0:T(8,128)(2,1)}, bf16[3,32,576]{2,1,0:T(8,128)(2,1)S(1)}, u32[]{:S(2)}, u32[]{:S(2)}) collective-permute-start(bf16[3,32,576]{2,1,0:T(8,128)(2,1)} %bitcast.17), channel_id=1, source_target_pairs={{0,1},{1,0},{2,3},{3,2},{4,5},{5,4},{6,7},{7,6},{8,9},{9,8},{10,11... | collective-permute-start | bytes 331784 | tf_op jit(solution)/shard_map/ppermute | solution.py:136
  2.4 25.9 %collective-permute-start.7 = (bf16[6,576,256]{2,1,0:T(8,128)(2,1)}, bf16[6,576,256]{2,1,0:T(8,128)(2,1)S(1)}, u32[]{:S(2)}, u32[]{:S(2)}) collective-permute-start(bf16[6,576,256]{2,1,0:T(8,128)(2,1)} %bitcast.11), channel_id=1, source_target_pairs={{0,1},{1,0},{2,3},{3,2},{4,5},{5,4},{6,7},{7,6},{8,9},{9,8},{10,11... | collective-permute-start | bytes 5308424 | tf_op jit(solution)/shard_map/ppermute | solution.py:136
  2.9 18.1 %collective-permute-start.5 = (bf16[3,576,256]{2,1,0:T(8,128)(2,1)}, bf16[3,576,256]{2,1,0:T(8,128)(2,1)S(1)}, u32[]{:S(2)}, u32[]{:S(2)}) collective-permute-start(bf16[3,576,256]{2,1,0:T(8,128)(2,1)} %own), channel_id=1, source_target_pairs={{0,1},{1,0},{2,3},{3,2},{4,5},{5,4},{6,7},{7,6},{8,9},{9,8},{10,11... | collective-permute-start | bytes 2654216 | tf_op jit(solution)/shard_map/ppermute | solution.py:136
  3.0 14.3 %collective-permute-start.1 = (bf16[3,32,1152]{2,1,0:T(8,128)(2,1)S(1)}, bf16[3,32,1152]{2,1,0:T(8,128)(2,1)S(1)}, u32[]{:S(2)}, u32[]{:S(2)}) collective-permute-start(bf16[3,32,1152]{2,1,0:T(8,128)(2,1)S(1)} %select_select_fusion.own), channel_id=1, source_target_pairs={{0,16},{1,8},{2,18},{3,10},{4,20},{5,12},{6,22},{7,14},{8,1},{9,25... | collective-permute-start | bytes 663560 | tf_op jit(solution)/shard_map/ppermute | solution.py:136
  7.0 12.6 %collective-permute-start.2 = (bf16[3,32,1152]{2,1,0:T(8,128)(2,1)S(1)}, bf16[3,32,1152]{2,1,0:T(8,128)(2,1)S(1)}, u32[]{:S(2)}, u32[]{:S(2)}) collective-permute-start(bf16[3,32,1152]{2,1,0:T(8,128)(2,1)S(1)} %select_select_fusion.own), channel_id=1, source_target_pairs={{0,4},{1,24},{2,6},{3,26},{4,0},{5,28},{6,2},{7,30},{8,17},{9,13},... | collective-permute-start | bytes 663560 | tf_op jit(solution)/shard_map/ppermute | solution.py:136
  17.4 7.9 %collective-permute-start.3 = (bf16[3,32,1152]{2,1,0:T(8,128)(2,1)S(1)}, bf16[3,32,1152]{2,1,0:T(8,128)(2,1)S(1)}, u32[]{:S(2)}, u32[]{:S(2)}) collective-permute-start(bf16[3,32,1152]{2,1,0:T(8,128)(2,1)S(1)} %collective-permute-done.1.r1), channel_id=1, source_target_pairs={{0,4},{1,5},{2,6},{3,7},{4,0},{5,1},{6,2},{7,3},{8,12},{9,13},{10,... | collective-permute-start | bytes 663560 | tf_op jit(solution)/shard_map/ppermute | solution.py:136
  19.5 5.7 %collective-permute-start.4 = (bf16[3,32,1152]{2,1,0:T(8,128)(2,1)S(1)}, bf16[3,32,1152]{2,1,0:T(8,128)(2,1)}, u32[]{:S(2)}, u32[]{:S(2)}) collective-permute-start(bf16[3,32,1152]{2,1,0:T(8,128)(2,1)S(1)} %collective-permute-done.2.r2), channel_id=1, source_target_pairs={{1,5},{3,7},{5,1},{7,3},{8,12},{10,14},{12,8},{14,10},{17,21},{19,... | collective-permute-start | bytes 663560 | tf_op jit(solution)/shard_map/ppermute | solution.py:136
  21.0 1.2 %copy-start.1 = (bf16[3,576,256]{2,1,0:T(8,128)(2,1)S(1)}, bf16[3,576,256]{2,1,0:T(8,128)(2,1)}, u32[]{:S(2)}) copy-start(bf16[3,576,256]{2,1,0:T(8,128)(2,1)} %own) | copy-start | bytes 2654212
  22.8 5.5 %copy-start = (bf16[6,256,576]{1,2,0:T(8,128)(2,1)S(1)}, bf16[6,256,576]{1,2,0:T(8,128)(2,1)}, u32[]{:S(2)}) copy-start(bf16[6,256,576]{1,2,0:T(8,128)(2,1)} %param.10) | copy-start | bytes 5308420
  26.7 6.5 %copy-start.2 = (f32[3,256]{1,0:T(4,128)S(1)}, f32[3,256]{1,0:T(4,128)}, u32[]{:S(2)}) copy-start(f32[3,256]{1,0:T(4,128)} %bias.1) | copy-start | bytes 9220
  26.7 6.5 %copy-start.3 = (s32[3,1]{0,1:T(1,128)S(1)}, s32[3,1]{0,1:T(1,128)}, u32[]{:S(2)}) copy-start(s32[3,1]{0,1:T(1,128)} %param.11) | copy-start | bytes 40
  26.7 6.5 %collective-permute-start.6 = (bf16[3,128,256]{2,1,0:T(8,128)(2,1)S(1)}, bf16[3,128,256]{2,1,0:T(8,128)(2,1)S(1)}, u32[]{:S(2)}, u32[]{:S(2)}) collective-permute-start(bf16[3,128,256]{2,1,0:T(8,128)(2,1)S(1)} %get-tuple-element.29), channel_id=1, source_target_pairs={{0,2},{1,3},{2,0},{3,1},{4,6},{5,7},{6,4},{7,5},{8,10},{9,11},{10,... | collective-permute-start | bytes 589832 | tf_op jit(solution)/shard_map/ppermute | solution.py:136
  35.0 19.9 %copy-start.4 = (bf16[32,3,576]{2,0,1:T(8,128)(2,1)S(1)}, bf16[32,3,576]{2,0,1:T(8,128)(2,1)}, u32[]{:S(2)}) copy-start(bf16[32,3,576]{2,0,1:T(8,128)(2,1)} %param.7) | copy-start | bytes 331780
  35.0 8.4 %collective-permute-start.10 = (bf16[3,32,1152]{2,1,0:T(8,128)(2,1)S(1)}, bf16[3,32,1152]{2,1,0:T(8,128)(2,1)S(1)}, u32[]{:S(2)}, u32[]{:S(2)}) collective-permute-start(bf16[3,32,1152]{2,1,0:T(8,128)(2,1)S(1)} %get-tuple-element.34), channel_id=1, source_target_pairs={{0,4},{1,5},{2,6},{3,7},{4,0},{5,1},{6,2},{7,3},{8,12},{9,13},{10,... | collective-permute-start | bytes 663560 | tf_op jit(solution)/shard_map/ppermute | solution.py:136
  36.0 9.8 %collective-permute-start.8 = (bf16[3,32,1152]{2,1,0:T(8,128)(2,1)S(1)}, bf16[3,32,1152]{2,1,0:T(8,128)(2,1)S(1)}, u32[]{:S(2)}, u32[]{:S(2)}) collective-permute-start(bf16[3,32,1152]{2,1,0:T(8,128)(2,1)S(1)} %get-tuple-element.32), channel_id=1, source_target_pairs={{0,4},{1,5},{2,6},{3,7},{4,0},{5,1},{6,2},{7,3},{8,12},{9,13},{10,... | collective-permute-start | bytes 663560 | tf_op jit(solution)/shard_map/ppermute | solution.py:136
  43.5 11.2 %collective-permute-start.11 = (bf16[3,32,1152]{2,1,0:T(8,128)(2,1)S(1)}, bf16[3,32,1152]{2,1,0:T(8,128)(2,1)S(1)}, u32[]{:S(2)}, u32[]{:S(2)}) collective-permute-start(bf16[3,32,1152]{2,1,0:T(8,128)(2,1)S(1)} %add_convert_fusion), channel_id=1, source_target_pairs={{0,16},{1,8},{2,18},{3,10},{4,20},{5,12},{6,22},{7,14},{8,1},{9,25... | collective-permute-start | bytes 663560 | tf_op jit(solution)/shard_map/ppermute | solution.py:136
  45.9 8.7 %collective-permute-start.9 = (bf16[3,32,1152]{2,1,0:T(8,128)(2,1)S(1)}, bf16[3,32,1152]{2,1,0:T(8,128)(2,1)S(1)}, u32[]{:S(2)}, u32[]{:S(2)}) collective-permute-start(bf16[3,32,1152]{2,1,0:T(8,128)(2,1)S(1)} %fusion), channel_id=1, source_target_pairs={{1,24},{3,26},{5,28},{7,30},{8,17},{10,19},{12,21},{14,23},{17,8},... | collective-permute-start | bytes 663560 | tf_op jit(solution)/shard_map/ppermute | solution.py:136
  54.7 2.0 %collective-permute-start.12 = (f32[3,32,1152]{2,1,0:T(8,128)S(1)}, f32[3,32,1152]{2,1,0:T(8,128)S(1)}, u32[]{:S(2)}, u32[]{:S(2)}) collective-permute-start(f32[3,32,1152]{2,1,0:T(8,128)S(1)} %convert_add_fusion), channel_id=1, source_target_pairs={{0,1},{1,0},{2,3},{3,2},{4,5},{5,4},{6,7},{7,6},{8,9},{9,8},{10,11... | collective-permute-start | bytes 1327112 | tf_op jit(solution)/shard_map/ppermute | solution.py:136
  54.8 1.9 %collective-permute-start.13 = (bf16[3,32,576]{2,1,0:T(8,128)(2,1)S(1)}, bf16[3,32,576]{2,1,0:T(8,128)(2,1)S(1)}, u32[]{:S(2)}, u32[]{:S(2)}) collective-permute-start(bf16[3,32,576]{2,1,0:T(8,128)(2,1)S(1)} %bitcast.19), channel_id=1, source_target_pairs={{0,1},{1,0},{2,3},{3,2},{4,5},{5,4},{6,7},{7,6},{8,9},{9,8},{10,11... | collective-permute-start | bytes 331784 | tf_op jit(solution)/shard_map/ppermute | solution.py:136
  57.0 13.7 %collective-permute-start.14 = (bf16[3,32,1152]{2,1,0:T(8,128)(2,1)S(1)}, bf16[3,32,1152]{2,1,0:T(8,128)(2,1)S(1)}, u32[]{:S(2)}, u32[]{:S(2)}) collective-permute-start(bf16[3,32,1152]{2,1,0:T(8,128)(2,1)S(1)} %get-tuple-element.38.own), channel_id=1, source_target_pairs={{0,16},{1,8},{2,18},{3,10},{4,20},{5,12},{6,22},{7,14},{8,1},{9,25... | collective-permute-start | bytes 663560 | tf_op jit(solution)/shard_map/ppermute | solution.py:136
  57.0 13.6 %collective-permute-start.15 = (bf16[3,32,1152]{2,1,0:T(8,128)(2,1)S(1)}, bf16[3,32,1152]{2,1,0:T(8,128)(2,1)S(1)}, u32[]{:S(2)}, u32[]{:S(2)}) collective-permute-start(bf16[3,32,1152]{2,1,0:T(8,128)(2,1)S(1)} %get-tuple-element.38.own), channel_id=1, source_target_pairs={{0,4},{1,24},{2,6},{3,26},{4,0},{5,28},{6,2},{7,30},{8,17},{9,13},... | collective-permute-start | bytes 663560 | tf_op jit(solution)/shard_map/ppermute | solution.py:136
  57.2 14.9 %collective-permute-start.18 = (bf16[3,128,256]{2,1,0:T(8,128)(2,1)S(1)}, bf16[3,128,256]{2,1,0:T(8,128)(2,1)S(1)}, u32[]{:S(2)}, u32[]{:S(2)}) collective-permute-start(bf16[3,128,256]{2,1,0:T(8,128)(2,1)S(1)} %get-tuple-element.36.latents), channel_id=1, source_target_pairs={{0,1},{1,0},{2,3},{3,2},{4,5},{5,4},{6,7},{7,6},{8,9},{9,8},{10,11... | collective-permute-start | bytes 589832 | tf_op jit(solution)/shard_map/ppermute | solution.py:136
  70.6 6.0 %collective-permute-start.16 = (bf16[3,32,1152]{2,1,0:T(8,128)(2,1)S(1)}, bf16[3,32,1152]{2,1,0:T(8,128)(2,1)S(1)}, u32[]{:S(2)}, u32[]{:S(2)}) collective-permute-start(bf16[3,32,1152]{2,1,0:T(8,128)(2,1)S(1)} %collective-permute-done.14.r1), channel_id=1, source_target_pairs={{0,4},{1,5},{2,6},{3,7},{4,0},{5,1},{6,2},{7,3},{8,12},{9,13},{10,... | collective-permute-start | bytes 663560 | tf_op jit(solution)/shard_map/ppermute | solution.py:136
  70.6 6.0 %collective-permute-start.17 = (bf16[3,32,1152]{2,1,0:T(8,128)(2,1)S(1)}, bf16[3,32,1152]{2,1,0:T(8,128)(2,1)S(1)}, u32[]{:S(2)}, u32[]{:S(2)}) collective-permute-start(bf16[3,32,1152]{2,1,0:T(8,128)(2,1)S(1)} %collective-permute-done.15.r2), channel_id=1, source_target_pairs={{1,5},{3,7},{5,1},{7,3},{8,12},{10,14},{12,8},{14,10},{17,21},{19,... | collective-permute-start | bytes 663560 | tf_op jit(solution)/shard_map/ppermute | solution.py:136
  78.2 1.9 %collective-permute-start.20 = (bf16[3,128,576]{2,1,0:T(8,128)(2,1)S(1)}, bf16[3,128,576]{2,1,0:T(8,128)(2,1)S(1)}, u32[]{:S(2)}, u32[]{:S(2)}) collective-permute-start(bf16[3,128,576]{2,1,0:T(8,128)(2,1)S(1)} %slice_select_fusion), channel_id=1, source_target_pairs={{0,1},{1,0},{2,3},{3,2},{4,5},{5,4},{6,7},{7,6},{8,9},{9,8},{10,11... | collective-permute-start | bytes 1327112 | tf_op jit(solution)/shard_map/ppermute | solution.py:136
  78.3 5.2 %collective-permute-start.19 = (bf16[3,64,256]{2,1,0:T(8,128)(2,1)S(1)}, bf16[3,64,256]{2,1,0:T(8,128)(2,1)S(1)}, u32[]{:S(2)}, u32[]{:S(2)}) collective-permute-start(bf16[3,64,256]{2,1,0:T(8,128)(2,1)S(1)} %get-tuple-element.43), channel_id=1, source_target_pairs={{0,2},{1,3},{2,0},{3,1},{4,6},{5,7},{6,4},{7,5},{8,10},{9,11},{10,... | collective-permute-start | bytes 294920 | tf_op jit(solution)/shard_map/ppermute | solution.py:136

commit v3 on v2

--- a/solution.py
+++ b/solution.py
@@ -40,25 +40,25 @@
     out[:, pl.ds(pl.multiple_of((1 - core) * rows, rows), rows), :] = other[...]
 
 
-def place(info, own, r1, r2, r3, r4, out):
+def place(info, own, beside, third, fourth, r1, r3, out):
     rows = own.shape[1]
 
     @pl.when(info[HOME] != 0)
     def _():
         out[:, :rows, :] = own[...]
-        out[:, rows : 2 * rows, :] = r2[...]
+        out[:, rows : 2 * rows, :] = beside[...]
 
     @pl.when(info[HOME] == 0)
     def _():
-        out[:, :rows, :] = r2[...]
-        out[:, rows : 2 * rows, :] = r4[...]
+        out[:, :rows, :] = third[...]
+        out[:, rows : 2 * rows, :] = fourth[...]
 
     out[:, 2 * rows : 3 * rows, :] = r1[...]
     out[:, 3 * rows :, :] = r3[...]
 
 
-def encode_kernel(info, own, r1, r2, r3, r4, weight, part, sent, held):
-    place(info, own, r1, r2, r3, r4, held)
+def encode_kernel(info, own, beside, third, fourth, r1, r3, weight, part, sent, held):
+    place(info, own, beside, third, fourth, r1, r3, held)
     for layer in range(part.shape[0]):
         value = jnp.dot(held[layer], weight[layer], preferred_element_type=F32)
         part[layer] = value
@@ -88,8 +88,8 @@
             sent[i][target] = total[(2 * i + 1) * rows : (2 * i + 2) * rows].astype(BF)
 
 
-def backward_kernel(info, own, r1, r2, r3, r4, weight, kept, sent, held):
-    place(info, own, r1, r2, r3, r4, held)
+def backward_kernel(info, own, beside, third, fourth, r1, r3, weight, kept, sent, held):
+    place(info, own, beside, third, fourth, r1, r3, held)
     layers, half = kept.shape[0], kept.shape[1]
     for source in range(layers):
         total = None
@@ -144,22 +144,35 @@
     def over_y(value):
         return swap(value, lambda z, y, x, c, home: (z, 1 - y, x, c))
 
-    def over_y_away(value):
-        return swap(value, lambda z, y, x, c, home: None if home else (z, 1 - y, x, c))
-
     def over_z2_z1(value):
         return swap(value, lambda z, y, x, c, home: (z ^ 2, y, x, c) if home else (z ^ 1, y, x, 1 - c))
 
-    def over_y_z3(value):
+
+    def away_over_y(value):
+        return swap(value, lambda z, y, x, c, home: (z ^ 1, y, x, 1 - c) if home else (z, 1 - y, x, c))
+
+    def to_home_over_y(value):
+        return swap(value, lambda z, y, x, c, home: (z, y if home else 1 - y, x, 1 - c))
+
+    def to_away_over_z1(value):
+        return swap(value, lambda z, y, x, c, home: (z ^ 1, y, x, c) if home else (z, y, x, 1 - c))
+
+    def away_over_z3(value):
         return swap(value, lambda z, y, x, c, home: (z, 1 - y, x, c) if home else (z ^ 3, y, x, 1 - c))
-
-    def over_z3_away(value):
-        return swap(value, lambda z, y, x, c, home: None if home else (z ^ 3, y, x, 1 - c))
 
     def gather(own):
         r1 = over_z2_z1(own)
-        r2 = over_y_z3(own)
-        return own, r1, r2, over_y(r1), over_y_away(r2)
+        beside = to_home_over_y(own)
+        third = to_away_over_z1(r1)
+        r3 = over_y(r1)
+        third, beside = lax.optimization_barrier((third, beside))
+        return own, beside, third, away_over_y(third), r1, r3
+
+    def reduce(q0, q1, q2, q3, home):
+        near = q0 + over_y(q1).astype(F32)
+        third = away_over_z3(near.astype(BF))
+        got = over_z2_z1((q2 + over_y(q3).astype(F32)).astype(BF))
+        return jnp.where(home, near, third.astype(F32)) + got.astype(F32)
 
     def local(inputs, targets, enc_weight, enc_bias, dec_weight, counts):
         rows, layers, width = inputs.shape
@@ -210,11 +223,7 @@
             enc_bias,
             dec_all,
         )
-        q1, q3 = over_y(q1), over_y(q3)
-        total = q0 + q1.astype(F32)
-        u0 = over_z3_away(total.astype(BF))
-        u2 = over_z2_z1((q2 + q3.astype(F32)).astype(BF))
-        mine = jnp.where(home, total, u0.astype(F32)) + u2.astype(F32)
+        mine = reduce(q0, q1, q2, q3, home)
         full = mine + over_c(mine)
         errors = (full - wanted.astype(F32)).astype(BF)
         recon = jnp.where(c == 0, full[:, :, :width], full[:, :, width:]).astype(BF)

time: 84.5 us -> 80.8 us (0.956)
  waiting for transfers between devices: 51.3 us -> 42.7 us
  starting transfers between devices: 18.9 us -> 23.8 us
    ppermute x21 -> x23, waiting for transfers between devices: 51.3 us -> 42.7 us  [swap(): return lax.ppermute(value, AXES, pairs)]
    ppermute x21 -> x23, starting transfers between devices: 18.9 us -> 23.8 us  [swap(): return lax.ppermute(value, AXES, pairs)]
  transfers between devices with their start and end apart: 21 -> 23, of which waited for: 12 -> 15; matrix products, arithmetic and copies ran while one was open for 3% -> 3% of each run, Pallas kernels for 6% -> 7%
where the time goes in v3:
time: 80.8 us; the launch traced here: 80.6 us
  waiting for transfers between devices  42.7 us (53%)
  starting transfers between devices  23.8 us (29%)
  Pallas kernels  8.52 us (11%)
  other arithmetic  3.49 us (4%)
  local copies, waits for them, and re-layouts  1.2 us (1%)
    ppermute x23, waiting for transfers between devices, swap(): return lax.ppermute(value, AXES, pairs)  42.7 us
    ppermute x23, starting transfers between devices, swap(): return lax.ppermute(value, AXES, pairs)  23.8 us
    pallas_call x6, Pallas kernels, fused(): pl.pallas_call(body, out_shape=out_shape, in_specs=specs, out_specs=[pl.B...  8.52 us
  transfers between devices with their start and end apart: 23, of which 15 were waited for; matrix products, arithmetic and copies ran while one was open for 3% of the time, Pallas kernels for 7%

profile of v3, /device:TPU:0, one launch (start us, length us, event | category | flops | bytes accessed | tf_op | source)
XLA Modules:
  0.0 80.6 jit_solution(11294012497935044321)
XLA Ops:
  0.6 0.5 collective-permute-start
  1.1 1.1 %pad_select_fusion.1 = bf16[3,32,1152]{2,1,0:T(8,128)(2,1)S(1)} fusion(bf16[3,32,576]{2,1,0:T(8,128)(2,1)} %bitcast.18, pred[]{:T(512)S(6)} %eq.34), kind=kLoop, calls=%fused_computation.10 | loop fusion | flops 110592 | bytes 331777 | tf_op jit(solution)/shard_map/jit(_where)/select_n | solution.py:193
  2.2 0.1 collective-permute-done
  2.3 0.1 select_select_fusion.own
  2.4 0.4 collective-permute-start.8
  2.9 0.1 collective-permute-start.6
  3.0 3.9 %collective-permute-start.1 = (bf16[3,32,1152]{2,1,0:T(8,128)(2,1)S(1)}, bf16[3,32,1152]{2,1,0:T(8,128)(2,1)S(1)}, u32[]{:S(2)}, u32[]{:S(2)}) collective-permute-start(bf16[3,32,1152]{2,1,0:T(8,128)(2,1)S(1)} %select_select_fusion.own), channel_id=1, source_target_pairs={{0,16},{1,8},{2,18},{3,10},{4,20},{5,12},{6,22},{7,14},{8,1},{9,25... | collective-permute-start | bytes 663560 | tf_op jit(solution)/shard_map/ppermute | solution.py:136
  7.0 0.0 collective-permute-start.3
  7.0 6.3 %collective-permute-done.1.r1 = bf16[3,32,1152]{2,1,0:T(8,128)(2,1)S(1)} collective-permute-done((bf16[3,32,1152]{2,1,0:T(8,128)(2,1)S(1)}, bf16[3,32,1152]{2,1,0:T(8,128)(2,1)S(1)}, u32[]{:S(2)}, u32[]{:S(2)}) %collective-permute-start.1) | collective-permute-done | bytes 221216 | tf_op jit(solution)/shard_map/ppermute | solution.py:136
  13.3 1.9 %collective-permute-start.5 = (bf16[3,32,1152]{2,1,0:T(8,128)(2,1)S(1)}, bf16[3,32,1152]{2,1,0:T(8,128)(2,1)}, u32[]{:S(2)}, u32[]{:S(2)}) collective-permute-start(bf16[3,32,1152]{2,1,0:T(8,128)(2,1)S(1)} %collective-permute-done.1.r1), channel_id=1, source_target_pairs={{0,4},{1,5},{2,6},{3,7},{4,0},{5,1},{6,2},{7,3},{8,12},{9,13},{10,... | collective-permute-start | bytes 663560 | tf_op jit(solution)/shard_map/ppermute | solution.py:136
  15.1 1.6 %collective-permute-done.2.third = bf16[3,32,1152]{2,1,0:T(8,128)(2,1)S(1)} collective-permute-done((bf16[3,32,1152]{2,1,0:T(8,128)(2,1)S(1)}, bf16[3,32,1152]{2,1,0:T(8,128)(2,1)S(1)}, u32[]{:S(2)}, u32[]{:S(2)}) %collective-permute-start.2) | collective-permute-done | bytes 221216 | tf_op jit(solution)/shard_map/ppermute | solution.py:136
  16.7 0.0 collective-permute-start.4
  16.7 0.1 pad_add_fusion.info
  16.8 0.0 collective-permute-done.6.other
  16.8 1.2 %copy-done.1 = bf16[3,576,256]{2,1,0:T(8,128)(2,1)S(1)} copy-done((bf16[3,576,256]{2,1,0:T(8,128)(2,1)S(1)}, bf16[3,576,256]{2,1,0:T(8,128)(2,1)}, u32[]{:S(2)}) %copy-start.1) | copy-done | bytes 884760
  18.0 0.7 shard_map.85.weight
  18.6 0.0 copy-start
  18.6 2.9 %collective-permute-done.5.r3 = bf16[3,32,1152]{2,1,0:T(8,128)(2,1)} collective-permute-done((bf16[3,32,1152]{2,1,0:T(8,128)(2,1)S(1)}, bf16[3,32,1152]{2,1,0:T(8,128)(2,1)}, u32[]{:S(2)}, u32[]{:S(2)}) %collective-permute-start.5) | collective-permute-done | bytes 221216 | tf_op jit(solution)/shard_map/ppermute | solution.py:136
  21.6 0.6 collective-permute-done.4.fourth
  22.2 1.5 %shard_map.86 = (f32[3,128,256]{2,1,0:T(8,128)S(1)}, bf16[3,128,256]{2,1,0:T(8,128)(2,1)S(1)}) custom-call(s32[3]{0:T(128)S(1)} %pad_add_fusion.info, bf16[3,32,1152]{2,1,0:T(8,128)(2,1)S(1)} %select_select_fusion.own, bf16[3,32,1152]{2,1,0:T(8,128)(2,1)S(1)} %collective-permute-done.3.beside, bf16[3,32,1152]{2,1,0:T(8,128)(2,1)S(1)} %collective-permute-done.2.third, ...), custom_call_target="tpu_custom_call" | custom-call | tf_op jit(solution)/shard_map/pallas_call | solution.py:23
  23.7 0.0 copy-start.2
  23.7 0.0 copy-start.3
  23.7 1.9 %collective-permute-start.7 = (bf16[3,128,256]{2,1,0:T(8,128)(2,1)S(1)}, bf16[3,128,256]{2,1,0:T(8,128)(2,1)S(1)}, u32[]{:S(2)}, u32[]{:S(2)}) collective-permute-start(bf16[3,128,256]{2,1,0:T(8,128)(2,1)S(1)} %get-tuple-element.36), channel_id=1, source_target_pairs={{0,2},{1,3},{2,0},{3,1},{4,6},{5,7},{6,4},{7,5},{8,10},{9,11},{10,... | collective-permute-start | bytes 589832 | tf_op jit(solution)/shard_map/ppermute | solution.py:136
  25.6 0.0 collective-permute-done.8.other
  25.6 0.8 shard_map.87.weight
  26.4 4.9 %collective-permute-done.7.got = bf16[3,128,256]{2,1,0:T(8,128)(2,1)S(1)} collective-permute-done((bf16[3,128,256]{2,1,0:T(8,128)(2,1)S(1)}, bf16[3,128,256]{2,1,0:T(8,128)(2,1)S(1)}, u32[]{:S(2)}, u32[]{:S(2)}) %collective-permute-start.7) | collective-permute-done | bytes 196640 | tf_op jit(solution)/shard_map/ppermute | solution.py:136
  31.3 1.7 %shard_map.88 = (bf16[3,128,256]{2,1,0:T(8,128)(2,1)S(1)}, f32[3,32,1152]{2,1,0:T(8,128)S(1)}, f32[3,32,1152]{2,1,0:T(8,128)S(1)}, bf16[3,32,1152]{2,1,0:T(8,128)(2,1)S(1)}, bf16[3,32,1152]{2,1,0:T(8,128)(2,1)S(1)}) custom-call(s32[3]{0:T(128)S(1)} %bitcast.13, f32[3,128,256]{2,1,0:T(8,128)S(1)} %get-tuple-element.35.part, ...), custom_call_target="tpu_custom_call" | custom-call | tf_op jit(solution)/shard_map/pallas_call | solution.py:23
  33.0 0.0 copy-start.4
  33.0 1.9 %collective-permute-start.11 = (bf16[3,32,1152]{2,1,0:T(8,128)(2,1)S(1)}, bf16[3,32,1152]{2,1,0:T(8,128)(2,1)S(1)}, u32[]{:S(2)}, u32[]{:S(2)}) collective-permute-start(bf16[3,32,1152]{2,1,0:T(8,128)(2,1)S(1)} %get-tuple-element.41), channel_id=1, source_target_pairs={{0,4},{1,5},{2,6},{3,7},{4,0},{5,1},{6,2},{7,3},{8,12},{9,13},{10,... | collective-permute-start | bytes 663560 | tf_op jit(solution)/shard_map/ppermute | solution.py:136
  35.0 0.1 collective-permute-start.9
  35.1 6.2 %collective-permute-done.11 = bf16[3,32,1152]{2,1,0:T(8,128)(2,1)S(1)} collective-permute-done((bf16[3,32,1152]{2,1,0:T(8,128)(2,1)S(1)}, bf16[3,32,1152]{2,1,0:T(8,128)(2,1)S(1)}, u32[]{:S(2)}, u32[]{:S(2)}) %collective-permute-start.11) | collective-permute-done | bytes 221216 | tf_op jit(solution)/shard_map/ppermute | solution.py:136
  41.4 2.3 %collective-permute-start.12 = (bf16[3,32,1152]{2,1,0:T(8,128)(2,1)S(1)}, bf16[3,32,1152]{2,1,0:T(8,128)(2,1)S(1)}, u32[]{:S(2)}, u32[]{:S(2)}) collective-permute-start(bf16[3,32,1152]{2,1,0:T(8,128)(2,1)S(1)} %add_convert_fusion), channel_id=1, source_target_pairs={{0,16},{1,8},{2,18},{3,10},{4,20},{5,12},{6,22},{7,14},{8,1},{9,25... | collective-permute-start | bytes 663560 | tf_op jit(solution)/shard_map/ppermute | solution.py:136
  43.7 1.7 %collective-permute-done.9 = bf16[3,32,1152]{2,1,0:T(8,128)(2,1)S(1)} collective-permute-done((bf16[3,32,1152]{2,1,0:T(8,128)(2,1)S(1)}, bf16[3,32,1152]{2,1,0:T(8,128)(2,1)S(1)}, u32[]{:S(2)}, u32[]{:S(2)}) %collective-permute-start.9) | collective-permute-done | bytes 221216 | tf_op jit(solution)/shard_map/ppermute | solution.py:136
  45.4 0.1 fusion
  45.5 1.8 %collective-permute-start.10 = (bf16[3,32,1152]{2,1,0:T(8,128)(2,1)S(1)}, bf16[3,32,1152]{2,1,0:T(8,128)(2,1)S(1)}, u32[]{:S(2)}, u32[]{:S(2)}) collective-permute-start(bf16[3,32,1152]{2,1,0:T(8,128)(2,1)S(1)} %fusion), channel_id=1, source_target_pairs={{0,4},{1,24},{2,6},{3,26},{4,0},{5,28},{6,2},{7,30},{8,17},{9,13},... | collective-permute-start | bytes 663560 | tf_op jit(solution)/shard_map/ppermute | solution.py:136
  47.3 2.1 %collective-permute-done.12 = bf16[3,32,1152]{2,1,0:T(8,128)(2,1)S(1)} collective-permute-done((bf16[3,32,1152]{2,1,0:T(8,128)(2,1)S(1)}, bf16[3,32,1152]{2,1,0:T(8,128)(2,1)S(1)}, u32[]{:S(2)}, u32[]{:S(2)}) %collective-permute-start.12) | collective-permute-done | bytes 221216 | tf_op jit(solution)/shard_map/ppermute | solution.py:136
  49.3 2.1 %collective-permute-done.10 = bf16[3,32,1152]{2,1,0:T(8,128)(2,1)S(1)} collective-permute-done((bf16[3,32,1152]{2,1,0:T(8,128)(2,1)S(1)}, bf16[3,32,1152]{2,1,0:T(8,128)(2,1)S(1)}, u32[]{:S(2)}, u32[]{:S(2)}) %collective-permute-start.10) | collective-permute-done | bytes 221216 | tf_op jit(solution)/shard_map/ppermute | solution.py:136
  51.5 0.1 convert_add_fusion
  51.6 0.8 %collective-permute-start.13 = (f32[3,32,1152]{2,1,0:T(8,128)S(1)}, f32[3,32,1152]{2,1,0:T(8,128)S(1)}, u32[]{:S(2)}, u32[]{:S(2)}) collective-permute-start(f32[3,32,1152]{2,1,0:T(8,128)S(1)} %convert_add_fusion), channel_id=1, source_target_pairs={{0,1},{1,0},{2,3},{3,2},{4,5},{5,4},{6,7},{7,6},{8,9},{9,8},{10,11... | collective-permute-start | bytes 1327112 | tf_op jit(solution)/shard_map/ppermute | solution.py:136
  52.4 0.1 collective-permute-start.14
  52.5 0.1 pad_select_fusion
  52.6 1.4 %collective-permute-done.14 = bf16[3,32,576]{2,1,0:T(8,128)(2,1)S(1)} collective-permute-done((bf16[3,32,576]{2,1,0:T(8,128)(2,1)S(1)}, bf16[3,32,576]{2,1,0:T(8,128)(2,1)S(1)}, u32[]{:S(2)}, u32[]{:S(2)}) %collective-permute-start.14) | collective-permute-done | bytes 110624 | tf_op jit(solution)/shard_map/ppermute | solution.py:136
  54.0 0.2 subtract_convert_fusion
  54.2 3.0 %collective-permute-start.15 = (bf16[3,32,1152]{2,1,0:T(8,128)(2,1)S(1)}, bf16[3,32,1152]{2,1,0:T(8,128)(2,1)S(1)}, u32[]{:S(2)}, u32[]{:S(2)}) collective-permute-start(bf16[3,32,1152]{2,1,0:T(8,128)(2,1)S(1)} %get-tuple-element.47.own), channel_id=1, source_target_pairs={{0,16},{1,8},{2,18},{3,10},{4,20},{5,12},{6,22},{7,14},{8,1},{9,25... | collective-permute-start | bytes 663560 | tf_op jit(solution)/shard_map/ppermute | solution.py:136
  57.2 0.0 collective-permute-start.17
  57.2 6.3 %collective-permute-done.15.r1 = bf16[3,32,1152]{2,1,0:T(8,128)(2,1)S(1)} collective-permute-done((bf16[3,32,1152]{2,1,0:T(8,128)(2,1)S(1)}, bf16[3,32,1152]{2,1,0:T(8,128)(2,1)S(1)}, u32[]{:S(2)}, u32[]{:S(2)}) %collective-permute-start.15) | collective-permute-done | bytes 221216 | tf_op jit(solution)/shard_map/ppermute | solution.py:136
  63.5 0.0 collective-permute-start.16
  63.5 0.5 collective-permute-start.20
  64.0 1.6 %collective-permute-start.19 = (bf16[3,32,1152]{2,1,0:T(8,128)(2,1)S(1)}, bf16[3,32,1152]{2,1,0:T(8,128)(2,1)S(1)}, u32[]{:S(2)}, u32[]{:S(2)}) collective-permute-start(bf16[3,32,1152]{2,1,0:T(8,128)(2,1)S(1)} %collective-permute-done.15.r1), channel_id=1, source_target_pairs={{0,4},{1,5},{2,6},{3,7},{4,0},{5,1},{6,2},{7,3},{8,12},{9,13},{10,... | collective-permute-start | bytes 663560 | tf_op jit(solution)/shard_map/ppermute | solution.py:136
  65.5 0.0 collective-permute-done.17.beside
  65.5 1.4 %collective-permute-done.16.third = bf16[3,32,1152]{2,1,0:T(8,128)(2,1)S(1)} collective-permute-done((bf16[3,32,1152]{2,1,0:T(8,128)(2,1)S(1)}, bf16[3,32,1152]{2,1,0:T(8,128)(2,1)S(1)}, u32[]{:S(2)}, u32[]{:S(2)}) %collective-permute-start.16) | collective-permute-done | bytes 221216 | tf_op jit(solution)/shard_map/ppermute | solution.py:136
  66.9 0.8 fusion.1
  67.7 0.0 collective-permute-done.20.latents_got
  67.7 4.6 %collective-permute-done.19.r3 = bf16[3,32,1152]{2,1,0:T(8,128)(2,1)S(1)} collective-permute-done((bf16[3,32,1152]{2,1,0:T(8,128)(2,1)S(1)}, bf16[3,32,1152]{2,1,0:T(8,128)(2,1)S(1)}, u32[]{:S(2)}, u32[]{:S(2)}) %collective-permute-start.19) | collective-permute-done | bytes 221216 | tf_op jit(solution)/shard_map/ppermute | solution.py:136
  72.3 0.0 collective-permute-done.18.fourth
  72.3 1.3 %shard_map.89 = (f32[3,64,256]{2,1,0:T(8,128)S(1)}, bf16[3,64,256]{2,1,0:T(8,128)(2,1)S(1)}, bf16[3,128,1152]{2,1,0:T(8,128)(2,1)S(1)}) custom-call(s32[3]{0:T(128)S(1)} %pad_add_fusion.info, bf16[3,32,1152]{2,1,0:T(8,128)(2,1)S(1)} %get-tuple-element.47.own, bf16[3,32,1152]{2,1,0:T(8,128)(2,1)S(1)} %collective-permute-done.17.beside, ...), custom_call_target="tpu_custom_call" | custom-call | tf_op jit(solution)/shard_map/pallas_call | solution.py:23
  73.6 0.2 slice_select_fusion
  73.8 1.3 %collective-permute-start.22 = (bf16[3,128,576]{2,1,0:T(8,128)(2,1)S(1)}, bf16[3,128,576]{2,1,0:T(8,128)(2,1)S(1)}, u32[]{:S(2)}, u32[]{:S(2)}) collective-permute-start(bf16[3,128,576]{2,1,0:T(8,128)(2,1)S(1)} %slice_select_fusion), channel_id=1, source_target_pairs={{0,1},{1,0},{2,3},{3,2},{4,5},{5,4},{6,7},{7,6},{8,9},{9,8},{10,11... | collective-permute-start | bytes 1327112 | tf_op jit(solution)/shard_map/ppermute | solution.py:136
  75.1 1.6 %collective-permute-start.21 = (bf16[3,64,256]{2,1,0:T(8,128)(2,1)S(1)}, bf16[3,64,256]{2,1,0:T(8,128)(2,1)S(1)}, u32[]{:S(2)}, u32[]{:S(2)}) collective-permute-start(bf16[3,64,256]{2,1,0:T(8,128)(2,1)S(1)} %get-tuple-element.53), channel_id=1, source_target_pairs={{0,2},{1,3},{2,0},{3,1},{4,6},{5,7},{6,4},{7,5},{8,10},{9,11},{10,... | collective-permute-start | bytes 294920 | tf_op jit(solution)/shard_map/ppermute | solution.py:136
  76.7 0.1 iota_compare_fusion.1
  76.7 0.0 collective-permute-done.22.errors_got
  76.7 2.6 %shard_map.90 = bf16[6,576,256]{2,1,0:T(8,128)(2,1)} custom-call(s32[3]{0:T(128)S(1)} %pad_add_fusion.info, bf16[3,128,1152]{2,1,0:T(8,128)(2,1)S(1)} %get-tuple-element.54.held, bf16[3,128,576]{2,1,0:T(8,128)(2,1)S(1)} %collective-permute-done.22.errors_got, bf16[3,128,256]{2,1,0:T(8,128)(2,1)S(1)} %get-tuple-element.45.latents, ...), custom_call_target="tpu_custom_call" | custom-call | tf_op jit(solution)/shard_map/pallas_call | solution.py:23
  79.3 0.6 collective-permute-done.21
  79.9 0.7 fusion.4
  (13 shorter events, 0.1 us)
Async XLA Ops:
  0.6 1.7 %collective-permute-start = (bf16[3,32,576]{2,1,0:T(8,128)(2,1)}, bf16[3,32,576]{2,1,0:T(8,128)(2,1)S(1)}, u32[]{:S(2)}, u32[]{:S(2)}) collective-permute-start(bf16[3,32,576]{2,1,0:T(8,128)(2,1)} %bitcast.17), channel_id=1, source_target_pairs={{0,1},{1,0},{2,3},{3,2},{4,5},{5,4},{6,7},{7,6},{8,9},{9,8},{10,11... | collective-permute-start | bytes 331784 | tf_op jit(solution)/shard_map/ppermute | solution.py:136
  2.4 23.2 %collective-permute-start.8 = (bf16[6,576,256]{2,1,0:T(8,128)(2,1)}, bf16[6,576,256]{2,1,0:T(8,128)(2,1)S(1)}, u32[]{:S(2)}, u32[]{:S(2)}) collective-permute-start(bf16[6,576,256]{2,1,0:T(8,128)(2,1)} %bitcast.11), channel_id=1, source_target_pairs={{0,1},{1,0},{2,3},{3,2},{4,5},{5,4},{6,7},{7,6},{8,9},{9,8},{10,11... | collective-permute-start | bytes 5308424 | tf_op jit(solution)/shard_map/ppermute | solution.py:136
  2.9 13.9 %collective-permute-start.6 = (bf16[3,576,256]{2,1,0:T(8,128)(2,1)}, bf16[3,576,256]{2,1,0:T(8,128)(2,1)S(1)}, u32[]{:S(2)}, u32[]{:S(2)}) collective-permute-start(bf16[3,576,256]{2,1,0:T(8,128)(2,1)} %own), channel_id=1, source_target_pairs={{0,1},{1,0},{2,3},{3,2},{4,5},{5,4},{6,7},{7,6},{8,9},{9,8},{10,11... | collective-permute-start | bytes 2654216 | tf_op jit(solution)/shard_map/ppermute | solution.py:136
  3.0 10.2 %collective-permute-start.1 = (bf16[3,32,1152]{2,1,0:T(8,128)(2,1)S(1)}, bf16[3,32,1152]{2,1,0:T(8,128)(2,1)S(1)}, u32[]{:S(2)}, u32[]{:S(2)}) collective-permute-start(bf16[3,32,1152]{2,1,0:T(8,128)(2,1)S(1)} %select_select_fusion.own), channel_id=1, source_target_pairs={{0,16},{1,8},{2,18},{3,10},{4,20},{5,12},{6,22},{7,14},{8,1},{9,25... | collective-permute-start | bytes 663560 | tf_op jit(solution)/shard_map/ppermute | solution.py:136
  7.0 8.1 %collective-permute-start.3 = (bf16[3,32,1152]{2,1,0:T(8,128)(2,1)S(1)}, bf16[3,32,1152]{2,1,0:T(8,128)(2,1)S(1)}, u32[]{:S(2)}, u32[]{:S(2)}) collective-permute-start(bf16[3,32,1152]{2,1,0:T(8,128)(2,1)S(1)} %select_select_fusion.own), channel_id=1, source_target_pairs={{0,1},{1,4},{2,3},{3,6},{4,5},{5,0},{6,7},{7,2},{8,13},{9,8},{10,1... | collective-permute-start | bytes 663560 | tf_op jit(solution)/shard_map/ppermute | solution.py:136
  13.2 3.5 %collective-permute-start.2 = (bf16[3,32,1152]{2,1,0:T(8,128)(2,1)S(1)}, bf16[3,32,1152]{2,1,0:T(8,128)(2,1)S(1)}, u32[]{:S(2)}, u32[]{:S(2)}) collective-permute-start(bf16[3,32,1152]{2,1,0:T(8,128)(2,1)S(1)} %collective-permute-done.1.r1), channel_id=1, source_target_pairs={{0,8},{1,0},{2,10},{3,2},{4,12},{5,4},{6,14},{7,6},{8,9},{9,1},{10... | collective-permute-start | bytes 663560 | tf_op jit(solution)/shard_map/ppermute | solution.py:136
  13.3 8.3 %collective-permute-start.5 = (bf16[3,32,1152]{2,1,0:T(8,128)(2,1)S(1)}, bf16[3,32,1152]{2,1,0:T(8,128)(2,1)}, u32[]{:S(2)}, u32[]{:S(2)}) collective-permute-start(bf16[3,32,1152]{2,1,0:T(8,128)(2,1)S(1)} %collective-permute-done.1.r1), channel_id=1, source_target_pairs={{0,4},{1,5},{2,6},{3,7},{4,0},{5,1},{6,2},{7,3},{8,12},{9,13},{10,... | collective-permute-start | bytes 663560 | tf_op jit(solution)/shard_map/ppermute | solution.py:136
  16.7 5.5 %collective-permute-start.4 = (bf16[3,32,1152]{2,1,0:T(8,128)(2,1)S(1)}, bf16[3,32,1152]{2,1,0:T(8,128)(2,1)}, u32[]{:S(2)}, u32[]{:S(2)}) collective-permute-start(bf16[3,32,1152]{2,1,0:T(8,128)(2,1)S(1)} %collective-permute-done.2.third), channel_id=1, source_target_pairs={{0,9},{1,5},{2,11},{3,7},{4,13},{5,1},{6,15},{7,3},{8,12},{9,0},{1... | collective-permute-start | bytes 663560 | tf_op jit(solution)/shard_map/ppermute | solution.py:136
  16.8 1.2 %copy-start.1 = (bf16[3,576,256]{2,1,0:T(8,128)(2,1)S(1)}, bf16[3,576,256]{2,1,0:T(8,128)(2,1)}, u32[]{:S(2)}) copy-start(bf16[3,576,256]{2,1,0:T(8,128)(2,1)} %own) | copy-start | bytes 2654212
  18.6 7.0 %copy-start = (bf16[6,256,576]{1,2,0:T(8,128)(2,1)S(1)}, bf16[6,256,576]{1,2,0:T(8,128)(2,1)}, u32[]{:S(2)}) copy-start(bf16[6,256,576]{1,2,0:T(8,128)(2,1)} %param.10) | copy-start | bytes 5308420
  23.7 7.6 %copy-start.2 = (f32[3,256]{1,0:T(4,128)S(1)}, f32[3,256]{1,0:T(4,128)}, u32[]{:S(2)}) copy-start(f32[3,256]{1,0:T(4,128)} %bias.1) | copy-start | bytes 9220
  23.7 7.6 %copy-start.3 = (s32[3,1]{0,1:T(1,128)S(1)}, s32[3,1]{0,1:T(1,128)}, u32[]{:S(2)}) copy-start(s32[3,1]{0,1:T(1,128)} %param.11) | copy-start | bytes 40
  23.7 7.6 %collective-permute-start.7 = (bf16[3,128,256]{2,1,0:T(8,128)(2,1)S(1)}, bf16[3,128,256]{2,1,0:T(8,128)(2,1)S(1)}, u32[]{:S(2)}, u32[]{:S(2)}) collective-permute-start(bf16[3,128,256]{2,1,0:T(8,128)(2,1)S(1)} %get-tuple-element.36), channel_id=1, source_target_pairs={{0,2},{1,3},{2,0},{3,1},{4,6},{5,7},{6,4},{7,5},{8,10},{9,11},{10,... | collective-permute-start | bytes 589832 | tf_op jit(solution)/shard_map/ppermute | solution.py:136
  33.0 19.4 %copy-start.4 = (bf16[32,3,576]{2,0,1:T(8,128)(2,1)S(1)}, bf16[32,3,576]{2,0,1:T(8,128)(2,1)}, u32[]{:S(2)}) copy-start(bf16[32,3,576]{2,0,1:T(8,128)(2,1)} %param.7) | copy-start | bytes 331780
  33.0 8.3 %collective-permute-start.11 = (bf16[3,32,1152]{2,1,0:T(8,128)(2,1)S(1)}, bf16[3,32,1152]{2,1,0:T(8,128)(2,1)S(1)}, u32[]{:S(2)}, u32[]{:S(2)}) collective-permute-start(bf16[3,32,1152]{2,1,0:T(8,128)(2,1)S(1)} %get-tuple-element.41), channel_id=1, source_target_pairs={{0,4},{1,5},{2,6},{3,7},{4,0},{5,1},{6,2},{7,3},{8,12},{9,13},{10,... | collective-permute-start | bytes 663560 | tf_op jit(solution)/shard_map/ppermute | solution.py:136
  35.0 10.4 %collective-permute-start.9 = (bf16[3,32,1152]{2,1,0:T(8,128)(2,1)S(1)}, bf16[3,32,1152]{2,1,0:T(8,128)(2,1)S(1)}, u32[]{:S(2)}, u32[]{:S(2)}) collective-permute-start(bf16[3,32,1152]{2,1,0:T(8,128)(2,1)S(1)} %get-tuple-element.39), channel_id=1, source_target_pairs={{0,4},{1,5},{2,6},{3,7},{4,0},{5,1},{6,2},{7,3},{8,12},{9,13},{10,... | collective-permute-start | bytes 663560 | tf_op jit(solution)/shard_map/ppermute | solution.py:136
  41.4 7.9 %collective-permute-start.12 = (bf16[3,32,1152]{2,1,0:T(8,128)(2,1)S(1)}, bf16[3,32,1152]{2,1,0:T(8,128)(2,1)S(1)}, u32[]{:S(2)}, u32[]{:S(2)}) collective-permute-start(bf16[3,32,1152]{2,1,0:T(8,128)(2,1)S(1)} %add_convert_fusion), channel_id=1, source_target_pairs={{0,16},{1,8},{2,18},{3,10},{4,20},{5,12},{6,22},{7,14},{8,1},{9,25... | collective-permute-start | bytes 663560 | tf_op jit(solution)/shard_map/ppermute | solution.py:136
  45.5 6.0 %collective-permute-start.10 = (bf16[3,32,1152]{2,1,0:T(8,128)(2,1)S(1)}, bf16[3,32,1152]{2,1,0:T(8,128)(2,1)S(1)}, u32[]{:S(2)}, u32[]{:S(2)}) collective-permute-start(bf16[3,32,1152]{2,1,0:T(8,128)(2,1)S(1)} %fusion), channel_id=1, source_target_pairs={{0,4},{1,24},{2,6},{3,26},{4,0},{5,28},{6,2},{7,30},{8,17},{9,13},... | collective-permute-start | bytes 663560 | tf_op jit(solution)/shard_map/ppermute | solution.py:136
  51.6 2.4 %collective-permute-start.13 = (f32[3,32,1152]{2,1,0:T(8,128)S(1)}, f32[3,32,1152]{2,1,0:T(8,128)S(1)}, u32[]{:S(2)}, u32[]{:S(2)}) collective-permute-start(f32[3,32,1152]{2,1,0:T(8,128)S(1)} %convert_add_fusion), channel_id=1, source_target_pairs={{0,1},{1,0},{2,3},{3,2},{4,5},{5,4},{6,7},{7,6},{8,9},{9,8},{10,11... | collective-permute-start | bytes 1327112 | tf_op jit(solution)/shard_map/ppermute | solution.py:136
  52.4 1.6 %collective-permute-start.14 = (bf16[3,32,576]{2,1,0:T(8,128)(2,1)S(1)}, bf16[3,32,576]{2,1,0:T(8,128)(2,1)S(1)}, u32[]{:S(2)}, u32[]{:S(2)}) collective-permute-start(bf16[3,32,576]{2,1,0:T(8,128)(2,1)S(1)} %bitcast.19), channel_id=1, source_target_pairs={{0,1},{1,0},{2,3},{3,2},{4,5},{5,4},{6,7},{7,6},{8,9},{9,8},{10,11... | collective-permute-start | bytes 331784 | tf_op jit(solution)/shard_map/ppermute | solution.py:136
  54.2 9.3 %collective-permute-start.15 = (bf16[3,32,1152]{2,1,0:T(8,128)(2,1)S(1)}, bf16[3,32,1152]{2,1,0:T(8,128)(2,1)S(1)}, u32[]{:S(2)}, u32[]{:S(2)}) collective-permute-start(bf16[3,32,1152]{2,1,0:T(8,128)(2,1)S(1)} %get-tuple-element.47.own), channel_id=1, source_target_pairs={{0,16},{1,8},{2,18},{3,10},{4,20},{5,12},{6,22},{7,14},{8,1},{9,25... | collective-permute-start | bytes 663560 | tf_op jit(solution)/shard_map/ppermute | solution.py:136
  57.2 8.4 %collective-permute-start.17 = (bf16[3,32,1152]{2,1,0:T(8,128)(2,1)S(1)}, bf16[3,32,1152]{2,1,0:T(8,128)(2,1)S(1)}, u32[]{:S(2)}, u32[]{:S(2)}) collective-permute-start(bf16[3,32,1152]{2,1,0:T(8,128)(2,1)S(1)} %get-tuple-element.47.own), channel_id=1, source_target_pairs={{0,1},{1,4},{2,3},{3,6},{4,5},{5,0},{6,7},{7,2},{8,13},{9,8},{10,1... | collective-permute-start | bytes 663560 | tf_op jit(solution)/shard_map/ppermute | solution.py:136
  63.5 3.5 %collective-permute-start.16 = (bf16[3,32,1152]{2,1,0:T(8,128)(2,1)S(1)}, bf16[3,32,1152]{2,1,0:T(8,128)(2,1)S(1)}, u32[]{:S(2)}, u32[]{:S(2)}) collective-permute-start(bf16[3,32,1152]{2,1,0:T(8,128)(2,1)S(1)} %collective-permute-done.15.r1), channel_id=1, source_target_pairs={{0,8},{1,0},{2,10},{3,2},{4,12},{5,4},{6,14},{7,6},{8,9},{9,1},{10... | collective-permute-start | bytes 663560 | tf_op jit(solution)/shard_map/ppermute | solution.py:136
  63.5 4.2 %collective-permute-start.20 = (bf16[3,128,256]{2,1,0:T(8,128)(2,1)S(1)}, bf16[3,128,256]{2,1,0:T(8,128)(2,1)S(1)}, u32[]{:S(2)}, u32[]{:S(2)}) collective-permute-start(bf16[3,128,256]{2,1,0:T(8,128)(2,1)S(1)} %get-tuple-element.45.latents), channel_id=1, source_target_pairs={{0,1},{1,0},{2,3},{3,2},{4,5},{5,4},{6,7},{7,6},{8,9},{9,8},{10,11... | collective-permute-start | bytes 589832 | tf_op jit(solution)/shard_map/ppermute | solution.py:136
  64.0 8.3 %collective-permute-start.19 = (bf16[3,32,1152]{2,1,0:T(8,128)(2,1)S(1)}, bf16[3,32,1152]{2,1,0:T(8,128)(2,1)S(1)}, u32[]{:S(2)}, u32[]{:S(2)}) collective-permute-start(bf16[3,32,1152]{2,1,0:T(8,128)(2,1)S(1)} %collective-permute-done.15.r1), channel_id=1, source_target_pairs={{0,4},{1,5},{2,6},{3,7},{4,0},{5,1},{6,2},{7,3},{8,12},{9,13},{10,... | collective-permute-start | bytes 663560 | tf_op jit(solution)/shard_map/ppermute | solution.py:136
  66.9 5.4 %collective-permute-start.18 = (bf16[3,32,1152]{2,1,0:T(8,128)(2,1)S(1)}, bf16[3,32,1152]{2,1,0:T(8,128)(2,1)S(1)}, u32[]{:S(2)}, u32[]{:S(2)}) collective-permute-start(bf16[3,32,1152]{2,1,0:T(8,128)(2,1)S(1)} %collective-permute-done.16.third), channel_id=1, source_target_pairs={{0,9},{1,5},{2,11},{3,7},{4,13},{5,1},{6,15},{7,3},{8,12},{9,0},{1... | collective-permute-start | bytes 663560 | tf_op jit(solution)/shard_map/ppermute | solution.py:136
  73.8 2.9 %collective-permute-start.22 = (bf16[3,128,576]{2,1,0:T(8,128)(2,1)S(1)}, bf16[3,128,576]{2,1,0:T(8,128)(2,1)S(1)}, u32[]{:S(2)}, u32[]{:S(2)}) collective-permute-start(bf16[3,128,576]{2,1,0:T(8,128)(2,1)S(1)} %slice_select_fusion), channel_id=1, source_target_pairs={{0,1},{1,0},{2,3},{3,2},{4,5},{5,4},{6,7},{7,6},{8,9},{9,8},{10,11... | collective-permute-start | bytes 1327112 | tf_op jit(solution)/shard_map/ppermute | solution.py:136
  75.1 4.8 %collective-permute-start.21 = (bf16[3,64,256]{2,1,0:T(8,128)(2,1)S(1)}, bf16[3,64,256]{2,1,0:T(8,128)(2,1)S(1)}, u32[]{:S(2)}, u32[]{:S(2)}) collective-permute-start(bf16[3,64,256]{2,1,0:T(8,128)(2,1)S(1)} %get-tuple-element.53), channel_id=1, source_target_pairs={{0,2},{1,3},{2,0},{3,1},{4,6},{5,7},{6,4},{7,5},{8,10},{9,11},{10,... | collective-permute-start | bytes 294920 | tf_op jit(solution)/shard_map/ppermute | solution.py:136

commit v4 on v3

--- a/solution.py
+++ b/solution.py
@@ -57,23 +57,29 @@
     out[:, 3 * rows :, :] = r3[...]
 
 
-def encode_kernel(info, own, beside, third, fourth, r1, r3, weight, part, sent, held):
-    place(info, own, beside, third, fourth, r1, r3, held)
-    for layer in range(part.shape[0]):
-        value = jnp.dot(held[layer], weight[layer], preferred_element_type=F32)
-        part[layer] = value
-        sent[layer] = value.astype(BF)
-
-
-def decode_kernel(counts, part, got, bias, weight, latents, kept0, kept1, sent0, sent1):
+def encode_kernel(lo, info, own, beside, third, fourth, r1, r3, weight, part, sent, held):
+    hi = lo + part.shape[0]
+    blocks = [ref.at[lo:hi] for ref in (own, beside, third, fourth, r1, r3)]
+    place(info, *blocks, held)
+    for layer in range(lo, hi):
+        value = jnp.dot(held[layer - lo], weight[layer], preferred_element_type=F32)
+        part[layer - lo] = value
+        sent[layer - lo] = value.astype(BF)
+
+
+def decode_kernel(lo, layers, counts, part, got, bias, weight, *refs):
+    before, after = refs[:-5], refs[-5:]
+    for old, new in zip(before, after):
+        new[:lo] = old[...]
+    latents, kept0, kept1, sent0, sent1 = after
     kept, sent = (kept0, kept1), (sent0, sent1)
-    layers, held, width = part.shape
+    held, width = part.shape[1:]
     rows = kept0.shape[1]
-    for layer in range(layers):
+    for layer in range(lo, lo + part.shape[0]):
         live = lax.broadcasted_iota(jnp.int32, (held, width), 1) < counts[layer]
-        pre = part[layer] + got[layer].astype(F32) + bias[layer : layer + 1, :]
+        pre = part[layer - lo] + got[layer - lo].astype(F32) + bias[layer : layer + 1, :]
         latents[layer] = jnp.where(live, jnp.maximum(pre, 0.0), 0.0).astype(BF)
-    for target in range(layers):
+    for target in range(lo, lo + part.shape[0]):
         total = None
         for source in range(target + 1):
             value = lax.dot_general(
@@ -204,25 +210,35 @@
         (dec_all,) = fused(stack_kernel, [((blocks, both, latent_width), BF)], info, dec_t, over_c(dec_t))
         wanted = join(own_want, over_c(own_want))
 
-        tile = (layers, held, latent_width)
-        part, sent = fused(
-            encode_kernel,
-            [(tile, F32), (tile, BF)],
-            info,
-            *arrived,
-            enc_all,
-            scratch=[((layers, held, both), BF)],
-        )
-        piece = (layers, rows, both)
-        latents, q0, q2, q1, q3 = fused(
-            decode_kernel,
-            [(tile, BF), (piece, F32), (piece, F32), (piece, BF), (piece, BF)],
-            counts[:, 0],
-            part,
-            over_x(sent),
-            enc_bias,
-            dec_all,
-        )
+        cuts = (0, layers - 1, layers)
+        encoded = []
+        for lo, hi in zip(cuts, cuts[1:]):
+            tile = (hi - lo, held, latent_width)
+            part, sent = fused(
+                functools.partial(encode_kernel, lo),
+                [(tile, F32), (tile, BF)],
+                info,
+                *arrived,
+                enc_all,
+                scratch=[((hi - lo, held, both), BF)],
+            )
+            encoded.append((part, over_x(sent)))
+            arrived, part = lax.optimization_barrier((arrived, part))
+            encoded[-1] = (part, encoded[-1][1])
+        decoded = []
+        for (lo, hi), (part, got) in zip(zip(cuts, cuts[1:]), encoded):
+            piece = (hi, rows, both)
+            decoded = fused(
+                functools.partial(decode_kernel, lo, layers),
+                [((hi, held, latent_width), BF), (piece, F32), (piece, F32), (piece, BF), (piece, BF)],
+                counts[:, 0],
+                part,
+                got,
+                enc_bias,
+                dec_all,
+                *decoded,
+            )
+        latents, q0, q2, q1, q3 = decoded
         mine = reduce(q0, q1, q2, q3, home)
         full = mine + over_c(mine)
         errors = (full - wanted.astype(F32)).astype(BF)

time: 80.8 us -> 80.2 us (level)
  waiting for transfers between devices: 42.7 us -> 40.1 us
  Pallas kernels: 8.52 us -> 10.2 us
    ppermute x23 -> x24, waiting for transfers between devices: 42.7 us -> 40.1 us  [swap(): return lax.ppermute(value, AXES, pairs)]
    pallas_call x6 -> x8, Pallas kernels: 8.52 us -> 10.2 us  [fused(): pl.pallas_call(body, out_shape=out_shape, in_specs=specs, out_specs=[pl.B...]
    ppermute x23 -> x24, starting transfers between devices: 23.8 us -> 24.2 us  [swap(): return lax.ppermute(value, AXES, pairs)]
  transfers between devices with their start and end apart: 23 -> 24, of which waited for: 15 -> 16; matrix products, arithmetic and copies ran while one was open for 3% -> 3% of each run, Pallas kernels for 7% -> 9%
where the time goes in v4:
time: 80.2 us; the launch traced here: 80 us
  waiting for transfers between devices  40.1 us (50%)
  starting transfers between devices  24.2 us (30%)
  Pallas kernels  10.2 us (13%)
  other arithmetic  3.48 us (4%)
  local copies, waits for them, and re-layouts  1.2 us (1%)
    ppermute x24, waiting for transfers between devices, swap(): return lax.ppermute(value, AXES, pairs)  40.1 us
    ppermute x24, starting transfers between devices, swap(): return lax.ppermute(value, AXES, pairs)  24.2 us
    pallas_call x8, Pallas kernels, fused(): pl.pallas_call(body, out_shape=out_shape, in_specs=specs, out_specs=[pl.B...  10.2 us
  transfers between devices with their start and end apart: 24, of which 16 were waited for; matrix products, arithmetic and copies ran while one was open for 3% of the time, Pallas kernels for 9%

profile of v4, /device:TPU:0, one launch (start us, length us, event | category | flops | bytes accessed | tf_op | source)
XLA Modules:
  0.0 80.0 jit_solution(10512161759916455523)
XLA Ops:
  0.6 0.5 collective-permute-start
  1.1 1.1 %pad_select_fusion.1 = bf16[3,32,1152]{2,1,0:T(8,128)(2,1)S(1)} fusion(bf16[3,32,576]{2,1,0:T(8,128)(2,1)} %bitcast.19, pred[]{:T(512)S(6)} %eq.33), kind=kLoop, calls=%fused_computation.10 | loop fusion | flops 110592 | bytes 331777 | tf_op jit(solution)/shard_map/jit(_where)/select_n | solution.py:199
  2.2 0.1 collective-permute-done
  2.3 0.1 select_select_fusion.own
  2.4 0.4 collective-permute-start.8
  2.9 0.1 collective-permute-start.6
  3.0 3.9 %collective-permute-start.1 = (bf16[3,32,1152]{2,1,0:T(8,128)(2,1)S(1)}, bf16[3,32,1152]{2,1,0:T(8,128)(2,1)S(1)}, u32[]{:S(2)}, u32[]{:S(2)}) collective-permute-start(bf16[3,32,1152]{2,1,0:T(8,128)(2,1)S(1)} %select_select_fusion.own), channel_id=1, source_target_pairs={{0,16},{1,8},{2,18},{3,10},{4,20},{5,12},{6,22},{7,14},{8,1},{9,25... | collective-permute-start | bytes 663560 | tf_op jit(solution)/shard_map/ppermute | solution.py:142
  7.0 6.3 %collective-permute-done.1.r1 = bf16[3,32,1152]{2,1,0:T(8,128)(2,1)S(1)} collective-permute-done((bf16[3,32,1152]{2,1,0:T(8,128)(2,1)S(1)}, bf16[3,32,1152]{2,1,0:T(8,128)(2,1)S(1)}, u32[]{:S(2)}, u32[]{:S(2)}) %collective-permute-start.1) | collective-permute-done | bytes 221216 | tf_op jit(solution)/shard_map/ppermute | solution.py:142
  13.3 1.9 %collective-permute-start.5 = (bf16[3,32,1152]{2,1,0:T(8,128)(2,1)S(1)}, bf16[3,32,1152]{2,1,0:T(8,128)(2,1)S(1)}, u32[]{:S(2)}, u32[]{:S(2)}) collective-permute-start(bf16[3,32,1152]{2,1,0:T(8,128)(2,1)S(1)} %collective-permute-done.1.r1), channel_id=1, source_target_pairs={{0,4},{1,5},{2,6},{3,7},{4,0},{5,1},{6,2},{7,3},{8,12},{9,13},{10,... | collective-permute-start | bytes 663560 | tf_op jit(solution)/shard_map/ppermute | solution.py:142
  15.1 1.6 %collective-permute-done.2.third = bf16[3,32,1152]{2,1,0:T(8,128)(2,1)S(1)} collective-permute-done((bf16[3,32,1152]{2,1,0:T(8,128)(2,1)S(1)}, bf16[3,32,1152]{2,1,0:T(8,128)(2,1)S(1)}, u32[]{:S(2)}, u32[]{:S(2)}) %collective-permute-start.2) | collective-permute-done | bytes 221216 | tf_op jit(solution)/shard_map/ppermute | solution.py:142
  16.7 0.0 collective-permute-start.4
  16.7 0.1 pad_add_fusion.info
  16.8 0.0 collective-permute-done.6.other
  16.8 1.2 %copy-done.1 = bf16[3,576,256]{2,1,0:T(8,128)(2,1)S(1)} copy-done((bf16[3,576,256]{2,1,0:T(8,128)(2,1)S(1)}, bf16[3,576,256]{2,1,0:T(8,128)(2,1)}, u32[]{:S(2)}) %copy-start.1) | copy-done | bytes 884760
  18.0 1.3 %shard_map.85.weight = bf16[3,1152,256]{2,1,0:T(8,128)(2,1)S(1)} custom-call(s32[3]{0:T(128)S(1)} %pad_add_fusion.info, bf16[3,576,256]{2,1,0:T(8,128)(2,1)S(1)} %copy-done.1, bf16[3,576,256]{2,1,0:T(8,128)(2,1)} %collective-permute-done.6.other), custom_call_target="tpu_custom_call" | custom-call | tf_op jit(solution)/shard_map/pallas_call | solution.py:23
  19.3 2.2 %collective-permute-done.5.r3 = bf16[3,32,1152]{2,1,0:T(8,128)(2,1)S(1)} collective-permute-done((bf16[3,32,1152]{2,1,0:T(8,128)(2,1)S(1)}, bf16[3,32,1152]{2,1,0:T(8,128)(2,1)S(1)}, u32[]{:S(2)}, u32[]{:S(2)}) %collective-permute-start.5) | collective-permute-done | bytes 221216 | tf_op jit(solution)/shard_map/ppermute | solution.py:142
  21.5 0.6 collective-permute-done.4.fourth
  22.1 0.9 %shard_map.86 = (f32[2,128,256]{2,1,0:T(8,128)S(1)}, bf16[2,128,256]{2,1,0:T(8,128)(2,1)S(1)}) custom-call(s32[3]{0:T(128)S(1)} %pad_add_fusion.info, bf16[3,32,1152]{2,1,0:T(8,128)(2,1)S(1)} %select_select_fusion.own, bf16[3,32,1152]{2,1,0:T(8,128)(2,1)S(1)} %collective-permute-done.3.beside, bf16[3,32,1152]{2,1,0:T(8,128)(2,1)S(1)} %collective-permute-done.2.third, ...), custom_call_target="tpu_custom_call" | custom-call | tf_op jit(solution)/shard_map/pallas_call | solution.py:23
  23.0 0.0 copy-start
  23.0 1.9 %collective-permute-start.9 = (bf16[2,128,256]{2,1,0:T(8,128)(2,1)S(1)}, bf16[2,128,256]{2,1,0:T(8,128)(2,1)S(1)}, u32[]{:S(2)}, u32[]{:S(2)}) collective-permute-start(bf16[2,128,256]{2,1,0:T(8,128)(2,1)S(1)} %get-tuple-element.62), channel_id=1, source_target_pairs={{0,2},{1,3},{2,0},{3,1},{4,6},{5,7},{6,4},{7,5},{8,10},{9,11},{10,... | collective-permute-start | bytes 393224 | tf_op jit(solution)/shard_map/ppermute | solution.py:142
  24.9 0.8 %shard_map.87 = (f32[1,128,256]{2,1,0:T(8,128)S(1)}, bf16[1,128,256]{2,1,0:T(8,128)(2,1)S(1)}) custom-call(s32[3]{0:T(128)S(1)} %pad_add_fusion.info, bf16[3,32,1152]{2,1,0:T(8,128)(2,1)S(1)} %select_select_fusion.own, bf16[3,32,1152]{2,1,0:T(8,128)(2,1)S(1)} %collective-permute-done.3.beside, bf16[3,32,1152]{2,1,0:T(8,128)(2,1)S(1)} %collective-permute-done.2.third, ...), custom_call_target="tpu_custom_call" | custom-call | tf_op jit(solution)/shard_map/pallas_call | solution.py:23
  25.7 0.3 collective-permute-start.7
  26.0 0.0 collective-permute-done.8.other
  26.0 0.8 shard_map.88.weight
  26.8 2.4 %collective-permute-done.9.got = bf16[2,128,256]{2,1,0:T(8,128)(2,1)S(1)} collective-permute-done((bf16[2,128,256]{2,1,0:T(8,128)(2,1)S(1)}, bf16[2,128,256]{2,1,0:T(8,128)(2,1)S(1)}, u32[]{:S(2)}, u32[]{:S(2)}) %collective-permute-start.9) | collective-permute-done | bytes 131104 | tf_op jit(solution)/shard_map/ppermute | solution.py:142
  29.2 1.2 %shard_map.89 = (bf16[2,128,256]{2,1,0:T(8,128)(2,1)S(1)}, f32[2,32,1152]{2,1,0:T(8,128)S(1)}, f32[2,32,1152]{2,1,0:T(8,128)S(1)}, bf16[2,32,1152]{2,1,0:T(8,128)(2,1)S(1)}, bf16[2,32,1152]{2,1,0:T(8,128)(2,1)S(1)}) custom-call(s32[3]{0:T(128)S(1)} %bitcast.13, f32[2,128,256]{2,1,0:T(8,128)S(1)} %get-tuple-element.61.part, ...), custom_call_target="tpu_custom_call" | custom-call | tf_op jit(solution)/shard_map/pallas_call | solution.py:23
  30.4 0.4 collective-permute-done.7.got
  30.8 1.3 %shard_map.90 = (bf16[3,128,256]{2,1,0:T(8,128)(2,1)S(1)}, f32[3,32,1152]{2,1,0:T(8,128)S(1)}, f32[3,32,1152]{2,1,0:T(8,128)S(1)}, bf16[3,32,1152]{2,1,0:T(8,128)(2,1)S(1)}, bf16[3,32,1152]{2,1,0:T(8,128)(2,1)S(1)}) custom-call(s32[3]{0:T(128)S(1)} %bitcast.14, f32[1,128,256]{2,1,0:T(8,128)S(1)} %get-tuple-element.58.part, ...), custom_call_target="tpu_custom_call" | custom-call | tf_op jit(solution)/shard_map/pallas_call | solution.py:23
  32.1 0.0 copy-start.4
  32.1 1.7 %collective-permute-start.12 = (bf16[3,32,1152]{2,1,0:T(8,128)(2,1)S(1)}, bf16[3,32,1152]{2,1,0:T(8,128)(2,1)S(1)}, u32[]{:S(2)}, u32[]{:S(2)}) collective-permute-start(bf16[3,32,1152]{2,1,0:T(8,128)(2,1)S(1)} %get-tuple-element.71), channel_id=1, source_target_pairs={{0,4},{1,5},{2,6},{3,7},{4,0},{5,1},{6,2},{7,3},{8,12},{9,13},{10,... | collective-permute-start | bytes 663560 | tf_op jit(solution)/shard_map/ppermute | solution.py:142
  33.8 0.4 collective-permute-start.10
  34.2 6.2 %collective-permute-done.12 = bf16[3,32,1152]{2,1,0:T(8,128)(2,1)S(1)} collective-permute-done((bf16[3,32,1152]{2,1,0:T(8,128)(2,1)S(1)}, bf16[3,32,1152]{2,1,0:T(8,128)(2,1)S(1)}, u32[]{:S(2)}, u32[]{:S(2)}) %collective-permute-start.12) | collective-permute-done | bytes 221216 | tf_op jit(solution)/shard_map/ppermute | solution.py:142
  40.4 0.1 add_convert_fusion
  40.5 2.2 %collective-permute-start.13 = (bf16[3,32,1152]{2,1,0:T(8,128)(2,1)S(1)}, bf16[3,32,1152]{2,1,0:T(8,128)(2,1)S(1)}, u32[]{:S(2)}, u32[]{:S(2)}) collective-permute-start(bf16[3,32,1152]{2,1,0:T(8,128)(2,1)S(1)} %add_convert_fusion), channel_id=1, source_target_pairs={{0,16},{1,8},{2,18},{3,10},{4,20},{5,12},{6,22},{7,14},{8,1},{9,25... | collective-permute-start | bytes 663560 | tf_op jit(solution)/shard_map/ppermute | solution.py:142
  42.7 1.9 %collective-permute-done.10 = bf16[3,32,1152]{2,1,0:T(8,128)(2,1)S(1)} collective-permute-done((bf16[3,32,1152]{2,1,0:T(8,128)(2,1)S(1)}, bf16[3,32,1152]{2,1,0:T(8,128)(2,1)S(1)}, u32[]{:S(2)}, u32[]{:S(2)}) %collective-permute-start.10) | collective-permute-done | bytes 221216 | tf_op jit(solution)/shard_map/ppermute | solution.py:142
  44.6 1.8 %collective-permute-start.11 = (bf16[3,32,1152]{2,1,0:T(8,128)(2,1)S(1)}, bf16[3,32,1152]{2,1,0:T(8,128)(2,1)S(1)}, u32[]{:S(2)}, u32[]{:S(2)}) collective-permute-start(bf16[3,32,1152]{2,1,0:T(8,128)(2,1)S(1)} %fusion), channel_id=1, source_target_pairs={{0,4},{1,24},{2,6},{3,26},{4,0},{5,28},{6,2},{7,30},{8,17},{9,13},... | collective-permute-start | bytes 663560 | tf_op jit(solution)/shard_map/ppermute | solution.py:142
  46.4 1.0 %collective-permute-done.13 = bf16[3,32,1152]{2,1,0:T(8,128)(2,1)S(1)} collective-permute-done((bf16[3,32,1152]{2,1,0:T(8,128)(2,1)S(1)}, bf16[3,32,1152]{2,1,0:T(8,128)(2,1)S(1)}, u32[]{:S(2)}, u32[]{:S(2)}) %collective-permute-start.13) | collective-permute-done | bytes 221216 | tf_op jit(solution)/shard_map/ppermute | solution.py:142
  47.4 3.2 %collective-permute-done.11 = bf16[3,32,1152]{2,1,0:T(8,128)(2,1)S(1)} collective-permute-done((bf16[3,32,1152]{2,1,0:T(8,128)(2,1)S(1)}, bf16[3,32,1152]{2,1,0:T(8,128)(2,1)S(1)}, u32[]{:S(2)}, u32[]{:S(2)}) %collective-permute-start.11) | collective-permute-done | bytes 221216 | tf_op jit(solution)/shard_map/ppermute | solution.py:142
  50.6 0.1 convert_add_fusion
  50.7 0.9 %collective-permute-start.14 = (f32[3,32,1152]{2,1,0:T(8,128)S(1)}, f32[3,32,1152]{2,1,0:T(8,128)S(1)}, u32[]{:S(2)}, u32[]{:S(2)}) collective-permute-start(f32[3,32,1152]{2,1,0:T(8,128)S(1)} %convert_add_fusion), channel_id=1, source_target_pairs={{0,1},{1,0},{2,3},{3,2},{4,5},{5,4},{6,7},{7,6},{8,9},{9,8},{10,11... | collective-permute-start | bytes 1327112 | tf_op jit(solution)/shard_map/ppermute | solution.py:142
  51.7 0.1 collective-permute-start.15
  51.8 0.1 pad_select_fusion
  51.9 1.4 %collective-permute-done.15 = bf16[3,32,576]{2,1,0:T(8,128)(2,1)S(1)} collective-permute-done((bf16[3,32,576]{2,1,0:T(8,128)(2,1)S(1)}, bf16[3,32,576]{2,1,0:T(8,128)(2,1)S(1)}, u32[]{:S(2)}, u32[]{:S(2)}) %collective-permute-start.15) | collective-permute-done | bytes 110624 | tf_op jit(solution)/shard_map/ppermute | solution.py:142
  53.3 0.2 subtract_convert_fusion
  53.5 2.6 %collective-permute-start.16 = (bf16[3,32,1152]{2,1,0:T(8,128)(2,1)S(1)}, bf16[3,32,1152]{2,1,0:T(8,128)(2,1)S(1)}, u32[]{:S(2)}, u32[]{:S(2)}) collective-permute-start(bf16[3,32,1152]{2,1,0:T(8,128)(2,1)S(1)} %get-tuple-element.77.own), channel_id=1, source_target_pairs={{0,16},{1,8},{2,18},{3,10},{4,20},{5,12},{6,22},{7,14},{8,1},{9,25... | collective-permute-start | bytes 663560 | tf_op jit(solution)/shard_map/ppermute | solution.py:142
  56.1 0.0 collective-permute-start.18
  56.1 6.6 %collective-permute-done.16.r1 = bf16[3,32,1152]{2,1,0:T(8,128)(2,1)S(1)} collective-permute-done((bf16[3,32,1152]{2,1,0:T(8,128)(2,1)S(1)}, bf16[3,32,1152]{2,1,0:T(8,128)(2,1)S(1)}, u32[]{:S(2)}, u32[]{:S(2)}) %collective-permute-start.16) | collective-permute-done | bytes 221216 | tf_op jit(solution)/shard_map/ppermute | solution.py:142
  62.7 0.0 collective-permute-start.17
  62.7 0.5 collective-permute-start.21
  63.2 1.9 %collective-permute-start.20 = (bf16[3,32,1152]{2,1,0:T(8,128)(2,1)S(1)}, bf16[3,32,1152]{2,1,0:T(8,128)(2,1)S(1)}, u32[]{:S(2)}, u32[]{:S(2)}) collective-permute-start(bf16[3,32,1152]{2,1,0:T(8,128)(2,1)S(1)} %collective-permute-done.16.r1), channel_id=1, source_target_pairs={{0,4},{1,5},{2,6},{3,7},{4,0},{5,1},{6,2},{7,3},{8,12},{9,13},{10,... | collective-permute-start | bytes 663560 | tf_op jit(solution)/shard_map/ppermute | solution.py:142
  65.1 0.0 collective-permute-done.18.beside
  65.1 1.1 %collective-permute-done.17.third = bf16[3,32,1152]{2,1,0:T(8,128)(2,1)S(1)} collective-permute-done((bf16[3,32,1152]{2,1,0:T(8,128)(2,1)S(1)}, bf16[3,32,1152]{2,1,0:T(8,128)(2,1)S(1)}, u32[]{:S(2)}, u32[]{:S(2)}) %collective-permute-start.17) | collective-permute-done | bytes 221216 | tf_op jit(solution)/shard_map/ppermute | solution.py:142
  66.2 0.0 collective-permute-start.19
  66.2 0.8 fusion.1
  66.9 4.6 %collective-permute-done.20.r3 = bf16[3,32,1152]{2,1,0:T(8,128)(2,1)S(1)} collective-permute-done((bf16[3,32,1152]{2,1,0:T(8,128)(2,1)S(1)}, bf16[3,32,1152]{2,1,0:T(8,128)(2,1)S(1)}, u32[]{:S(2)}, u32[]{:S(2)}) %collective-permute-start.20) | collective-permute-done | bytes 221216 | tf_op jit(solution)/shard_map/ppermute | solution.py:142
  71.5 0.0 collective-permute-done.19.fourth
  71.5 1.3 %shard_map.91 = (f32[3,64,256]{2,1,0:T(8,128)S(1)}, bf16[3,64,256]{2,1,0:T(8,128)(2,1)S(1)}, bf16[3,128,1152]{2,1,0:T(8,128)(2,1)S(1)}) custom-call(s32[3]{0:T(128)S(1)} %pad_add_fusion.info, bf16[3,32,1152]{2,1,0:T(8,128)(2,1)S(1)} %get-tuple-element.77.own, bf16[3,32,1152]{2,1,0:T(8,128)(2,1)S(1)} %collective-permute-done.18.beside, ...), custom_call_target="tpu_custom_call" | custom-call | tf_op jit(solution)/shard_map/pallas_call | solution.py:23
  72.9 0.2 slice_select_fusion
  73.1 1.4 %collective-permute-start.23 = (bf16[3,128,576]{2,1,0:T(8,128)(2,1)S(1)}, bf16[3,128,576]{2,1,0:T(8,128)(2,1)S(1)}, u32[]{:S(2)}, u32[]{:S(2)}) collective-permute-start(bf16[3,128,576]{2,1,0:T(8,128)(2,1)S(1)} %slice_select_fusion), channel_id=1, source_target_pairs={{0,1},{1,0},{2,3},{3,2},{4,5},{5,4},{6,7},{7,6},{8,9},{9,8},{10,11... | collective-permute-start | bytes 1327112 | tf_op jit(solution)/shard_map/ppermute | solution.py:142
  74.5 1.6 %collective-permute-start.22 = (bf16[3,64,256]{2,1,0:T(8,128)(2,1)S(1)}, bf16[3,64,256]{2,1,0:T(8,128)(2,1)S(1)}, u32[]{:S(2)}, u32[]{:S(2)}) collective-permute-start(bf16[3,64,256]{2,1,0:T(8,128)(2,1)S(1)} %get-tuple-element.83), channel_id=1, source_target_pairs={{0,2},{1,3},{2,0},{3,1},{4,6},{5,7},{6,4},{7,5},{8,10},{9,11},{10,... | collective-permute-start | bytes 294920 | tf_op jit(solution)/shard_map/ppermute | solution.py:142
  76.2 0.1 iota_compare_fusion.1
  76.2 2.6 %shard_map.92 = bf16[6,576,256]{2,1,0:T(8,128)(2,1)} custom-call(s32[3]{0:T(128)S(1)} %pad_add_fusion.info, bf16[3,128,1152]{2,1,0:T(8,128)(2,1)S(1)} %get-tuple-element.84.held, bf16[3,128,576]{2,1,0:T(8,128)(2,1)S(1)} %collective-permute-done.23.errors_got, bf16[3,128,256]{2,1,0:T(8,128)(2,1)S(1)} %get-tuple-element.75.latents, ...), custom_call_target="tpu_custom_call" | custom-call | tf_op jit(solution)/shard_map/pallas_call | solution.py:23
  78.8 0.5 collective-permute-done.22
  79.3 0.7 fusion.4
  (17 shorter events, 0.1 us)
Async XLA Ops:
  0.6 1.7 %collective-permute-start = (bf16[3,32,576]{2,1,0:T(8,128)(2,1)}, bf16[3,32,576]{2,1,0:T(8,128)(2,1)S(1)}, u32[]{:S(2)}, u32[]{:S(2)}) collective-permute-start(bf16[3,32,576]{2,1,0:T(8,128)(2,1)} %bitcast.18), channel_id=1, source_target_pairs={{0,1},{1,0},{2,3},{3,2},{4,5},{5,4},{6,7},{7,6},{8,9},{9,8},{10,11... | collective-permute-start | bytes 331784 | tf_op jit(solution)/shard_map/ppermute | solution.py:142
  2.4 23.6 %collective-permute-start.8 = (bf16[6,576,256]{2,1,0:T(8,128)(2,1)}, bf16[6,576,256]{2,1,0:T(8,128)(2,1)S(1)}, u32[]{:S(2)}, u32[]{:S(2)}) collective-permute-start(bf16[6,576,256]{2,1,0:T(8,128)(2,1)} %bitcast.11), channel_id=1, source_target_pairs={{0,1},{1,0},{2,3},{3,2},{4,5},{5,4},{6,7},{7,6},{8,9},{9,8},{10,11... | collective-permute-start | bytes 5308424 | tf_op jit(solution)/shard_map/ppermute | solution.py:142
  2.9 13.9 %collective-permute-start.6 = (bf16[3,576,256]{2,1,0:T(8,128)(2,1)}, bf16[3,576,256]{2,1,0:T(8,128)(2,1)}, u32[]{:S(2)}, u32[]{:S(2)}) collective-permute-start(bf16[3,576,256]{2,1,0:T(8,128)(2,1)} %own), channel_id=1, source_target_pairs={{0,1},{1,0},{2,3},{3,2},{4,5},{5,4},{6,7},{7,6},{8,9},{9,8},{10,11... | collective-permute-start | bytes 2654216 | tf_op jit(solution)/shard_map/ppermute | solution.py:142
  3.0 10.2 %collective-permute-start.1 = (bf16[3,32,1152]{2,1,0:T(8,128)(2,1)S(1)}, bf16[3,32,1152]{2,1,0:T(8,128)(2,1)S(1)}, u32[]{:S(2)}, u32[]{:S(2)}) collective-permute-start(bf16[3,32,1152]{2,1,0:T(8,128)(2,1)S(1)} %select_select_fusion.own), channel_id=1, source_target_pairs={{0,16},{1,8},{2,18},{3,10},{4,20},{5,12},{6,22},{7,14},{8,1},{9,25... | collective-permute-start | bytes 663560 | tf_op jit(solution)/shard_map/ppermute | solution.py:142
  7.0 8.1 %collective-permute-start.3 = (bf16[3,32,1152]{2,1,0:T(8,128)(2,1)S(1)}, bf16[3,32,1152]{2,1,0:T(8,128)(2,1)S(1)}, u32[]{:S(2)}, u32[]{:S(2)}) collective-permute-start(bf16[3,32,1152]{2,1,0:T(8,128)(2,1)S(1)} %select_select_fusion.own), channel_id=1, source_target_pairs={{0,1},{1,4},{2,3},{3,6},{4,5},{5,0},{6,7},{7,2},{8,13},{9,8},{10,1... | collective-permute-start | bytes 663560 | tf_op jit(solution)/shard_map/ppermute | solution.py:142
  13.2 3.5 %collective-permute-start.2 = (bf16[3,32,1152]{2,1,0:T(8,128)(2,1)S(1)}, bf16[3,32,1152]{2,1,0:T(8,128)(2,1)S(1)}, u32[]{:S(2)}, u32[]{:S(2)}) collective-permute-start(bf16[3,32,1152]{2,1,0:T(8,128)(2,1)S(1)} %collective-permute-done.1.r1), channel_id=1, source_target_pairs={{0,8},{1,0},{2,10},{3,2},{4,12},{5,4},{6,14},{7,6},{8,9},{9,1},{10... | collective-permute-start | bytes 663560 | tf_op jit(solution)/shard_map/ppermute | solution.py:142
  13.3 8.2 %collective-permute-start.5 = (bf16[3,32,1152]{2,1,0:T(8,128)(2,1)S(1)}, bf16[3,32,1152]{2,1,0:T(8,128)(2,1)S(1)}, u32[]{:S(2)}, u32[]{:S(2)}) collective-permute-start(bf16[3,32,1152]{2,1,0:T(8,128)(2,1)S(1)} %collective-permute-done.1.r1), channel_id=1, source_target_pairs={{0,4},{1,5},{2,6},{3,7},{4,0},{5,1},{6,2},{7,3},{8,12},{9,13},{10,... | collective-permute-start | bytes 663560 | tf_op jit(solution)/shard_map/ppermute | solution.py:142
  16.7 5.4 %collective-permute-start.4 = (bf16[3,32,1152]{2,1,0:T(8,128)(2,1)S(1)}, bf16[3,32,1152]{2,1,0:T(8,128)(2,1)S(1)}, u32[]{:S(2)}, u32[]{:S(2)}) collective-permute-start(bf16[3,32,1152]{2,1,0:T(8,128)(2,1)S(1)} %collective-permute-done.2.third), channel_id=1, source_target_pairs={{0,9},{1,5},{2,11},{3,7},{4,13},{5,1},{6,15},{7,3},{8,12},{9,0},{1... | collective-permute-start | bytes 663560 | tf_op jit(solution)/shard_map/ppermute | solution.py:142
  16.8 1.2 %copy-start.1 = (bf16[3,576,256]{2,1,0:T(8,128)(2,1)S(1)}, bf16[3,576,256]{2,1,0:T(8,128)(2,1)}, u32[]{:S(2)}) copy-start(bf16[3,576,256]{2,1,0:T(8,128)(2,1)} %own) | copy-start | bytes 2654212
  23.0 3.0 %copy-start = (bf16[6,256,576]{1,2,0:T(8,128)(2,1)S(1)}, bf16[6,256,576]{1,2,0:T(8,128)(2,1)}, u32[]{:S(2)}) copy-start(bf16[6,256,576]{1,2,0:T(8,128)(2,1)} %param.10) | copy-start | bytes 5308420
  23.0 6.2 %collective-permute-start.9 = (bf16[2,128,256]{2,1,0:T(8,128)(2,1)S(1)}, bf16[2,128,256]{2,1,0:T(8,128)(2,1)S(1)}, u32[]{:S(2)}, u32[]{:S(2)}) collective-permute-start(bf16[2,128,256]{2,1,0:T(8,128)(2,1)S(1)} %get-tuple-element.62), channel_id=1, source_target_pairs={{0,2},{1,3},{2,0},{3,1},{4,6},{5,7},{6,4},{7,5},{8,10},{9,11},{10,... | collective-permute-start | bytes 393224 | tf_op jit(solution)/shard_map/ppermute | solution.py:142
  25.7 5.1 %collective-permute-start.7 = (bf16[1,128,256]{2,1,0:T(8,128)(2,1)S(1)}, bf16[1,128,256]{2,1,0:T(8,128)(2,1)S(1)}, u32[]{:S(2)}, u32[]{:S(2)}) collective-permute-start(bf16[1,128,256]{2,1,0:T(8,128)(2,1)S(1)} %get-tuple-element.59), channel_id=1, source_target_pairs={{0,2},{1,3},{2,0},{3,1},{4,6},{5,7},{6,4},{7,5},{8,10},{9,11},{10,... | collective-permute-start | bytes 196616 | tf_op jit(solution)/shard_map/ppermute | solution.py:142
  26.0 3.2 %copy-start.2 = (f32[3,256]{1,0:T(4,128)S(1)}, f32[3,256]{1,0:T(4,128)}, u32[]{:S(2)}) copy-start(f32[3,256]{1,0:T(4,128)} %bias.3) | copy-start | bytes 9220
  26.0 3.2 %copy-start.3 = (s32[3,1]{0,1:T(1,128)S(1)}, s32[3,1]{0,1:T(1,128)}, u32[]{:S(2)}) copy-start(s32[3,1]{0,1:T(1,128)} %param.11) | copy-start | bytes 40
  32.1 19.6 %copy-start.4 = (bf16[32,3,576]{2,0,1:T(8,128)(2,1)S(1)}, bf16[32,3,576]{2,0,1:T(8,128)(2,1)}, u32[]{:S(2)}) copy-start(bf16[32,3,576]{2,0,1:T(8,128)(2,1)} %param.7) | copy-start | bytes 331780
  32.1 8.3 %collective-permute-start.12 = (bf16[3,32,1152]{2,1,0:T(8,128)(2,1)S(1)}, bf16[3,32,1152]{2,1,0:T(8,128)(2,1)S(1)}, u32[]{:S(2)}, u32[]{:S(2)}) collective-permute-start(bf16[3,32,1152]{2,1,0:T(8,128)(2,1)S(1)} %get-tuple-element.71), channel_id=1, source_target_pairs={{0,4},{1,5},{2,6},{3,7},{4,0},{5,1},{6,2},{7,3},{8,12},{9,13},{10,... | collective-permute-start | bytes 663560 | tf_op jit(solution)/shard_map/ppermute | solution.py:142
  33.8 10.8 %collective-permute-start.10 = (bf16[3,32,1152]{2,1,0:T(8,128)(2,1)S(1)}, bf16[3,32,1152]{2,1,0:T(8,128)(2,1)S(1)}, u32[]{:S(2)}, u32[]{:S(2)}) collective-permute-start(bf16[3,32,1152]{2,1,0:T(8,128)(2,1)S(1)} %get-tuple-element.69), channel_id=1, source_target_pairs={{0,4},{1,5},{2,6},{3,7},{4,0},{5,1},{6,2},{7,3},{8,12},{9,13},{10,... | collective-permute-start | bytes 663560 | tf_op jit(solution)/shard_map/ppermute | solution.py:142
  40.5 7.0 %collective-permute-start.13 = (bf16[3,32,1152]{2,1,0:T(8,128)(2,1)S(1)}, bf16[3,32,1152]{2,1,0:T(8,128)(2,1)S(1)}, u32[]{:S(2)}, u32[]{:S(2)}) collective-permute-start(bf16[3,32,1152]{2,1,0:T(8,128)(2,1)S(1)} %add_convert_fusion), channel_id=1, source_target_pairs={{0,16},{1,8},{2,18},{3,10},{4,20},{5,12},{6,22},{7,14},{8,1},{9,25... | collective-permute-start | bytes 663560 | tf_op jit(solution)/shard_map/ppermute | solution.py:142
  44.6 6.0 %collective-permute-start.11 = (bf16[3,32,1152]{2,1,0:T(8,128)(2,1)S(1)}, bf16[3,32,1152]{2,1,0:T(8,128)(2,1)S(1)}, u32[]{:S(2)}, u32[]{:S(2)}) collective-permute-start(bf16[3,32,1152]{2,1,0:T(8,128)(2,1)S(1)} %fusion), channel_id=1, source_target_pairs={{0,4},{1,24},{2,6},{3,26},{4,0},{5,28},{6,2},{7,30},{8,17},{9,13},... | collective-permute-start | bytes 663560 | tf_op jit(solution)/shard_map/ppermute | solution.py:142
  50.7 2.5 %collective-permute-start.14 = (f32[3,32,1152]{2,1,0:T(8,128)S(1)}, f32[3,32,1152]{2,1,0:T(8,128)S(1)}, u32[]{:S(2)}, u32[]{:S(2)}) collective-permute-start(f32[3,32,1152]{2,1,0:T(8,128)S(1)} %convert_add_fusion), channel_id=1, source_target_pairs={{0,1},{1,0},{2,3},{3,2},{4,5},{5,4},{6,7},{7,6},{8,9},{9,8},{10,11... | collective-permute-start | bytes 1327112 | tf_op jit(solution)/shard_map/ppermute | solution.py:142
  51.7 1.6 %collective-permute-start.15 = (bf16[3,32,576]{2,1,0:T(8,128)(2,1)S(1)}, bf16[3,32,576]{2,1,0:T(8,128)(2,1)S(1)}, u32[]{:S(2)}, u32[]{:S(2)}) collective-permute-start(bf16[3,32,576]{2,1,0:T(8,128)(2,1)S(1)} %bitcast.20), channel_id=1, source_target_pairs={{0,1},{1,0},{2,3},{3,2},{4,5},{5,4},{6,7},{7,6},{8,9},{9,8},{10,11... | collective-permute-start | bytes 331784 | tf_op jit(solution)/shard_map/ppermute | solution.py:142
  53.5 9.3 %collective-permute-start.16 = (bf16[3,32,1152]{2,1,0:T(8,128)(2,1)S(1)}, bf16[3,32,1152]{2,1,0:T(8,128)(2,1)S(1)}, u32[]{:S(2)}, u32[]{:S(2)}) collective-permute-start(bf16[3,32,1152]{2,1,0:T(8,128)(2,1)S(1)} %get-tuple-element.77.own), channel_id=1, source_target_pairs={{0,16},{1,8},{2,18},{3,10},{4,20},{5,12},{6,22},{7,14},{8,1},{9,25... | collective-permute-start | bytes 663560 | tf_op jit(solution)/shard_map/ppermute | solution.py:142
  56.1 9.0 %collective-permute-start.18 = (bf16[3,32,1152]{2,1,0:T(8,128)(2,1)S(1)}, bf16[3,32,1152]{2,1,0:T(8,128)(2,1)S(1)}, u32[]{:S(2)}, u32[]{:S(2)}) collective-permute-start(bf16[3,32,1152]{2,1,0:T(8,128)(2,1)S(1)} %get-tuple-element.77.own), channel_id=1, source_target_pairs={{0,1},{1,4},{2,3},{3,6},{4,5},{5,0},{6,7},{7,2},{8,13},{9,8},{10,1... | collective-permute-start | bytes 663560 | tf_op jit(solution)/shard_map/ppermute | solution.py:142
  62.7 3.5 %collective-permute-start.17 = (bf16[3,32,1152]{2,1,0:T(8,128)(2,1)S(1)}, bf16[3,32,1152]{2,1,0:T(8,128)(2,1)S(1)}, u32[]{:S(2)}, u32[]{:S(2)}) collective-permute-start(bf16[3,32,1152]{2,1,0:T(8,128)(2,1)S(1)} %collective-permute-done.16.r1), channel_id=1, source_target_pairs={{0,8},{1,0},{2,10},{3,2},{4,12},{5,4},{6,14},{7,6},{8,9},{9,1},{10... | collective-permute-start | bytes 663560 | tf_op jit(solution)/shard_map/ppermute | solution.py:142
  62.7 4.2 %collective-permute-start.21 = (bf16[3,128,256]{2,1,0:T(8,128)(2,1)S(1)}, bf16[3,128,256]{2,1,0:T(8,128)(2,1)S(1)}, u32[]{:S(2)}, u32[]{:S(2)}) collective-permute-start(bf16[3,128,256]{2,1,0:T(8,128)(2,1)S(1)} %get-tuple-element.75.latents), channel_id=1, source_target_pairs={{0,1},{1,0},{2,3},{3,2},{4,5},{5,4},{6,7},{7,6},{8,9},{9,8},{10,11... | collective-permute-start | bytes 589832 | tf_op jit(solution)/shard_map/ppermute | solution.py:142
  63.2 8.3 %collective-permute-start.20 = (bf16[3,32,1152]{2,1,0:T(8,128)(2,1)S(1)}, bf16[3,32,1152]{2,1,0:T(8,128)(2,1)S(1)}, u32[]{:S(2)}, u32[]{:S(2)}) collective-permute-start(bf16[3,32,1152]{2,1,0:T(8,128)(2,1)S(1)} %collective-permute-done.16.r1), channel_id=1, source_target_pairs={{0,4},{1,5},{2,6},{3,7},{4,0},{5,1},{6,2},{7,3},{8,12},{9,13},{10,... | collective-permute-start | bytes 663560 | tf_op jit(solution)/shard_map/ppermute | solution.py:142
  66.2 5.4 %collective-permute-start.19 = (bf16[3,32,1152]{2,1,0:T(8,128)(2,1)S(1)}, bf16[3,32,1152]{2,1,0:T(8,128)(2,1)S(1)}, u32[]{:S(2)}, u32[]{:S(2)}) collective-permute-start(bf16[3,32,1152]{2,1,0:T(8,128)(2,1)S(1)} %collective-permute-done.17.third), channel_id=1, source_target_pairs={{0,9},{1,5},{2,11},{3,7},{4,13},{5,1},{6,15},{7,3},{8,12},{9,0},{1... | collective-permute-start | bytes 663560 | tf_op jit(solution)/shard_map/ppermute | solution.py:142
  73.1 3.1 %collective-permute-start.23 = (bf16[3,128,576]{2,1,0:T(8,128)(2,1)S(1)}, bf16[3,128,576]{2,1,0:T(8,128)(2,1)S(1)}, u32[]{:S(2)}, u32[]{:S(2)}) collective-permute-start(bf16[3,128,576]{2,1,0:T(8,128)(2,1)S(1)} %slice_select_fusion), channel_id=1, source_target_pairs={{0,1},{1,0},{2,3},{3,2},{4,5},{5,4},{6,7},{7,6},{8,9},{9,8},{10,11... | collective-permute-start | bytes 1327112 | tf_op jit(solution)/shard_map/ppermute | solution.py:142
  74.5 4.8 %collective-permute-start.22 = (bf16[3,64,256]{2,1,0:T(8,128)(2,1)S(1)}, bf16[3,64,256]{2,1,0:T(8,128)(2,1)S(1)}, u32[]{:S(2)}, u32[]{:S(2)}) collective-permute-start(bf16[3,64,256]{2,1,0:T(8,128)(2,1)S(1)} %get-tuple-element.83), channel_id=1, source_target_pairs={{0,2},{1,3},{2,0},{3,1},{4,6},{5,7},{6,4},{7,5},{8,10},{9,11},{10,... | collective-permute-start | bytes 294920 | tf_op jit(solution)/shard_map/ppermute | solution.py:142

commit v5 on v3

--- a/solution.py
+++ b/solution.py
@@ -46,29 +46,38 @@
     @pl.when(info[HOME] != 0)
     def _():
         out[:, :rows, :] = own[...]
-        out[:, rows : 2 * rows, :] = beside[...]
+        out[:, 2 * rows : 3 * rows, :] = beside[...]
 
     @pl.when(info[HOME] == 0)
     def _():
         out[:, :rows, :] = third[...]
-        out[:, rows : 2 * rows, :] = fourth[...]
-
-    out[:, 2 * rows : 3 * rows, :] = r1[...]
+        out[:, 2 * rows : 3 * rows, :] = fourth[...]
+
+    out[:, rows : 2 * rows, :] = r1[...]
     out[:, 3 * rows :, :] = r3[...]
 
 
-def encode_kernel(info, own, beside, third, fourth, r1, r3, weight, part, sent, held):
-    place(info, own, beside, third, fourth, r1, r3, held)
+def encode_kernel(info, at_home, away, second, weight, part, sent, held):
+    rows = second.shape[1]
+
+    @pl.when(info[HOME] != 0)
+    def _():
+        held[:, :rows, :] = at_home[...]
+
+    @pl.when(info[HOME] == 0)
+    def _():
+        held[:, :rows, :] = away[...]
+
+    held[:, rows:, :] = second[...]
     for layer in range(part.shape[0]):
         value = jnp.dot(held[layer], weight[layer], preferred_element_type=F32)
         part[layer] = value
         sent[layer] = value.astype(BF)
 
 
-def decode_kernel(counts, part, got, bias, weight, latents, kept0, kept1, sent0, sent1):
-    kept, sent = (kept0, kept1), (sent0, sent1)
+def decode_kernel(counts, part, got, bias, weight, latents, first, second):
     layers, held, width = part.shape
-    rows = kept0.shape[1]
+    rows = first.shape[1]
     for layer in range(layers):
         live = lax.broadcasted_iota(jnp.int32, (held, width), 1) < counts[layer]
         pre = part[layer] + got[layer].astype(F32) + bias[layer : layer + 1, :]
@@ -83,14 +92,13 @@
                 preferred_element_type=F32,
             )
             total = value if total is None else total + value
-        for i in range(2):
-            kept[i][target] = total[2 * i * rows : (2 * i + 1) * rows]
-            sent[i][target] = total[(2 * i + 1) * rows : (2 * i + 2) * rows].astype(BF)
+        first[target] = total[:rows].astype(first.dtype)
+        second[target] = total[rows:].astype(second.dtype)
 
 
 def backward_kernel(info, own, beside, third, fourth, r1, r3, weight, kept, sent, held):
     place(info, own, beside, third, fourth, r1, r3, held)
-    layers, half = kept.shape[0], kept.shape[1]
+    layers, rows = kept.shape[0], own.shape[1]
     for source in range(layers):
         total = None
         for target in range(source, layers):
@@ -99,14 +107,16 @@
             )
             total = value if total is None else total + value
         stays = info[NEAR] != 0
-        kept[source] = jnp.where(stays, total[:half], total[half:])
-        sent[source] = jnp.where(stays, total[half:], total[:half]).astype(BF)
-
-
-def weight_grad_kernel(info, held, errors_got, latents, latents_got, out, own):
+        for i in range(2):
+            to = slice(i * rows, (i + 1) * rows)
+            one, two = total[2 * i * rows : (2 * i + 1) * rows], total[(2 * i + 1) * rows : (2 * i + 2) * rows]
+            kept[source, to] = jnp.where(stays, one, two)
+            sent[source, to] = jnp.where(stays, two, one).astype(BF)
+
+
+def weight_grad_kernel(info, held, errors_got, latents, latents_got, out, own, blocks, sems):
     layers = latents.shape[0]
     width = errors_got.shape[2]
-    contract = (((0,), (0,)), ((), ()))
 
     @pl.when(info[CORE] == 0)
     def _():
@@ -116,12 +126,18 @@
     def _():
         own[...] = held[:, :, width:]
 
-    for source in range(layers):
-        values = jnp.concatenate([latents[source], latents_got[source]], 0)
-        for target in range(source, layers):
-            rows = jnp.concatenate([own[target], errors_got[target]], 0)
-            total = lax.dot_general(rows, values, contract, preferred_element_type=F32)
-            out[block_index(source, target, layers)] = total.astype(BF)
+    copies = []
+    for target in range(layers):
+        rows = jnp.concatenate([own[target], errors_got[target]], 0)
+        for source in range(target + 1):
+            values = jnp.concatenate([latents[source], latents_got[source]], 0)
+            total = lax.dot_general(rows, values, (((0,), (0,)), ((), ())), preferred_element_type=F32)
+            at = block_index(source, target, layers)
+            blocks[at] = total.astype(BF)
+            copies.append(pltpu.make_async_copy(blocks.at[at], out.at[at], sems.at[at]))
+            copies[-1].start()
+    for copy in copies:
+        copy.wait()
 
 
 def make_paired(n_tok):
@@ -160,13 +176,16 @@
     def away_over_z3(value):
         return swap(value, lambda z, y, x, c, home: (z, 1 - y, x, c) if home else (z ^ 3, y, x, 1 - c))
 
-    def gather(own):
+    def gather(own, ready=None):
         r1 = over_z2_z1(own)
         beside = to_home_over_y(own)
+        if ready is not None:
+            r1, ready = lax.optimization_barrier((r1, ready))
         third = to_away_over_z1(r1)
         r3 = over_y(r1)
         third, beside = lax.optimization_barrier((third, beside))
-        return own, beside, third, away_over_y(third), r1, r3
+        blocks = own, beside, third, away_over_y(third), r1, r3
+        return blocks if ready is None else blocks + (ready,)
 
     def reduce(q0, q1, q2, q3, home):
         near = q0 + over_y(q1).astype(F32)
@@ -199,30 +218,39 @@
 
         block = join(own_in, over_c(own_in))
         block, enc_weight, dec_t, own_want = lax.optimization_barrier((block, enc_weight, dec_t, own_want))
-        arrived = gather(block)
         (enc_all,) = fused(stack_kernel, [((layers, both, latent_width), BF)], info, enc_weight, over_c(enc_weight))
+        *arrived, enc_all = gather(block, enc_all)
         (dec_all,) = fused(stack_kernel, [((blocks, both, latent_width), BF)], info, dec_t, over_c(dec_t))
         wanted = join(own_want, over_c(own_want))
 
-        tile = (layers, held, latent_width)
-        part, sent = fused(
-            encode_kernel,
-            [(tile, F32), (tile, BF)],
-            info,
-            *arrived,
-            enc_all,
-            scratch=[((layers, held, both), BF)],
-        )
+        own_block, beside, third, fourth, r1, r3 = arrived
+        tile = (layers, 2 * rows, latent_width)
         piece = (layers, rows, both)
-        latents, q0, q2, q1, q3 = fused(
-            decode_kernel,
-            [(tile, BF), (piece, F32), (piece, F32), (piece, BF), (piece, BF)],
-            counts[:, 0],
-            part,
-            over_x(sent),
-            enc_bias,
-            dec_all,
-        )
+
+        def encode(*parts):
+            return fused(
+                encode_kernel,
+                [(tile, F32), (tile, BF)],
+                info,
+                *parts,
+                enc_all,
+                scratch=[((layers, 2 * rows, both), BF)],
+            )
+
+        def decode(part, got, kind):
+            outs = [(tile, BF), (piece, kind), (piece, kind)]
+            return fused(decode_kernel, outs, counts[:, 0], part, got, enc_bias, dec_all)
+
+        part, sent = encode(own_block, third, r1)
+        got = over_x(sent)
+        beside, fourth, r3, part = lax.optimization_barrier((beside, fourth, r3, part))
+        late_part, late_sent = encode(beside, fourth, r3)
+        late_got = over_x(late_sent)
+        part, late_part = lax.optimization_barrier((part, late_part))
+        early, q0, q2 = decode(part, got, F32)
+        late_part, late_got, early = lax.optimization_barrier((late_part, late_got, early))
+        late, q1, q3 = decode(late_part, late_got, BF)
+        latents = jnp.concatenate([early, late], 1)
         mine = reduce(q0, q1, q2, q3, home)
         full = mine + over_c(mine)
         errors = (full - wanted.astype(F32)).astype(BF)
@@ -240,16 +268,20 @@
         )
         got = over_x(sent)
         other = jnp.where(c == 0, all_errors[:, :, width:], all_errors[:, :, :width])
-        (grads,) = fused(
+        vmem = pl.BlockSpec(memory_space=pltpu.VMEM)
+        shape = (blocks, width, latent_width)
+        grads = pl.pallas_call(
             weight_grad_kernel,
-            [((blocks, width, latent_width), BF)],
-            info,
-            all_errors,
-            over_c(other),
-            latents,
-            latents_got,
-            scratch=[((layers, held, width), BF)],
-        )
+            out_shape=jax.ShapeDtypeStruct(shape, BF),
+            in_specs=[pl.BlockSpec(memory_space=pltpu.SMEM)] + [vmem] * 4,
+            out_specs=pl.BlockSpec(memory_space=pl.ANY),
+            scratch_shapes=[
+                pltpu.VMEM((layers, held, width), BF),
+                pltpu.VMEM(shape, BF),
+                pltpu.SemaphoreType.DMA((blocks,)),
+            ],
+            compiler_params=pltpu.CompilerParams(vmem_limit_bytes=40 * 2**20),
+        )(info, all_errors, over_c(other), latents, latents_got)
         got, grads = lax.optimization_barrier((got, grads))
         total = kept + got.astype(F32)
         flipped = jnp.concatenate([total[:, rows:], total[:, :rows]], 1)

time: 80.8 us -> 78.3 us (0.969)
  waiting for transfers between devices: 42.7 us -> 36.3 us
  starting transfers between devices: 23.8 us -> 26 us
  Pallas kernels: 8.52 us -> 10.2 us
    ppermute x23 -> x24, waiting for transfers between devices: 42.7 us -> 36.3 us  [swap(): return lax.ppermute(value, AXES, pairs)]
    pallas_call x0 -> x1, Pallas kernels: none -> 2.18 us  [local(): pl.pallas_call(weight_grad_kernel, out_shape=jax.ShapeDtypeStruct(shape,...]
    ppermute x23 -> x24, starting transfers between devices: 23.8 us -> 26 us  [swap(): return lax.ppermute(value, AXES, pairs)]
    pallas_call x6 -> x7, Pallas kernels: 8.52 us -> 8.05 us  [fused(): pl.pallas_call(body, out_shape=out_shape, in_specs=specs, out_specs=[pl.B...]
  transfers between devices with their start and end apart: 23 -> 24, of which waited for: 15 -> 16; matrix products, arithmetic and copies ran while one was open for 3% -> 3% of each run, Pallas kernels for 7% -> 9%
where the time goes in v5:
time: 78.3 us; the launch traced here: 78.1 us
  waiting for transfers between devices  36.3 us (46%)
  starting transfers between devices  26 us (33%)
  Pallas kernels  10.2 us (13%)
  other arithmetic  3.5 us (4%)
  local copies, waits for them, and re-layouts  1.21 us (2%)
  between operations  0.82 us (1%)
    ppermute x24, waiting for transfers between devices, swap(): return lax.ppermute(value, AXES, pairs)  36.3 us
    ppermute x24, starting transfers between devices, swap(): return lax.ppermute(value, AXES, pairs)  26 us
    pallas_call x7, Pallas kernels, fused(): pl.pallas_call(body, out_shape=out_shape, in_specs=specs, out_specs=[pl.B...  8.05 us
    pallas_call x1, Pallas kernels, local(): pl.pallas_call(weight_grad_kernel, out_shape=jax.ShapeDtypeStruct(shape,...  2.18 us
  transfers between devices with their start and end apart: 24, of which 16 were waited for; matrix products, arithmetic and copies ran while one was open for 3% of the time, Pallas kernels for 9%

profile of v5, /device:TPU:0, one launch (start us, length us, event | category | flops | bytes accessed | tf_op | source)
XLA Modules:
  0.0 78.1 jit_solution(6539378249021368912)
XLA Ops:
  0.6 0.5 collective-permute-start
  1.1 1.1 %pad_select_fusion.1 = bf16[3,32,1152]{2,1,0:T(8,128)(2,1)S(1)} fusion(bf16[3,32,576]{2,1,0:T(8,128)(2,1)} %bitcast.19, pred[]{:T(512)S(6)} %eq.33), kind=kLoop, calls=%fused_computation.10 | loop fusion | flops 110592 | bytes 331777 | tf_op jit(solution)/shard_map/jit(_where)/select_n | solution.py:212
  2.2 0.1 collective-permute-done
  2.3 0.1 select_select_fusion.at_home
  2.4 0.4 collective-permute-start.8
  2.9 0.1 collective-permute-start.2
  3.0 3.9 %collective-permute-start.1 = (bf16[3,32,1152]{2,1,0:T(8,128)(2,1)S(1)}, bf16[3,32,1152]{2,1,0:T(8,128)(2,1)S(1)}, u32[]{:S(2)}, u32[]{:S(2)}) collective-permute-start(bf16[3,32,1152]{2,1,0:T(8,128)(2,1)S(1)} %select_select_fusion.at_home), channel_id=1, source_target_pairs={{0,16},{1,8},{2,18},{3,10},{4,20},{5,12},{6,22},{7,14},{8,1},{9,25... | collective-permute-start | bytes 663560 | tf_op jit(solution)/shard_map/ppermute | solution.py:152
  7.0 0.1 pad_add_fusion.info
  7.0 0.0 collective-permute-start.4
  7.0 0.6 collective-permute-done.2.other
  7.7 1.2 %copy-done.1 = bf16[3,576,256]{2,1,0:T(8,128)(2,1)S(1)} copy-done((bf16[3,576,256]{2,1,0:T(8,128)(2,1)S(1)}, bf16[3,576,256]{2,1,0:T(8,128)(2,1)}, u32[]{:S(2)}) %copy-start.1) | copy-done | bytes 884760
  8.8 0.7 shard_map.85.weight
  9.5 3.7 %collective-permute-done.1.second = bf16[3,32,1152]{2,1,0:T(8,128)(2,1)S(1)} collective-permute-done((bf16[3,32,1152]{2,1,0:T(8,128)(2,1)S(1)}, bf16[3,32,1152]{2,1,0:T(8,128)(2,1)S(1)}, u32[]{:S(2)}, u32[]{:S(2)}) %collective-permute-start.1) | collective-permute-done | bytes 221216 | tf_op jit(solution)/shard_map/ppermute | solution.py:152
  13.2 0.0 collective-permute-start.3
  13.3 1.9 %collective-permute-start.6 = (bf16[3,32,1152]{2,1,0:T(8,128)(2,1)S(1)}, bf16[3,32,1152]{2,1,0:T(8,128)(2,1)S(1)}, u32[]{:S(2)}, u32[]{:S(2)}) collective-permute-start(bf16[3,32,1152]{2,1,0:T(8,128)(2,1)S(1)} %collective-permute-done.1.second), channel_id=1, source_target_pairs={{0,4},{1,5},{2,6},{3,7},{4,0},{5,1},{6,2},{7,3},{8,12},{9,13},{10,... | collective-permute-start | bytes 663560 | tf_op jit(solution)/shard_map/ppermute | solution.py:152
  15.1 0.0 collective-permute-done.4.at_home
  15.1 1.6 %collective-permute-done.3.away = bf16[3,32,1152]{2,1,0:T(8,128)(2,1)S(1)} collective-permute-done((bf16[3,32,1152]{2,1,0:T(8,128)(2,1)S(1)}, bf16[3,32,1152]{2,1,0:T(8,128)(2,1)S(1)}, u32[]{:S(2)}, u32[]{:S(2)}) %collective-permute-start.3) | collective-permute-done | bytes 221216 | tf_op jit(solution)/shard_map/ppermute | solution.py:152
  16.7 0.0 collective-permute-start.5
  16.7 1.0 %shard_map.86 = (f32[3,64,256]{2,1,0:T(8,128)S(1)}, bf16[3,64,256]{2,1,0:T(8,128)(2,1)S(1)}) custom-call(s32[3]{0:T(128)S(1)} %pad_add_fusion.info, bf16[3,32,1152]{2,1,0:T(8,128)(2,1)S(1)} %select_select_fusion.at_home, bf16[3,32,1152]{2,1,0:T(8,128)(2,1)S(1)} %collective-permute-done.3.away, bf16[3,32,1152]{2,1,0:T(8,128)(2,1)S(1)} %collective-permute-done.1.second, ...), custom_call_target="tpu_custom_call" | custom-call | tf_op jit(solution)/shard_map/pallas_call | solution.py:23
  17.7 0.0 copy-start
  17.7 1.9 %collective-permute-start.7 = (bf16[3,64,256]{2,1,0:T(8,128)(2,1)S(1)}, bf16[3,64,256]{2,1,0:T(8,128)(2,1)S(1)}, u32[]{:S(2)}, u32[]{:S(2)}) collective-permute-start(bf16[3,64,256]{2,1,0:T(8,128)(2,1)S(1)} %get-tuple-element.58), channel_id=1, source_target_pairs={{0,2},{1,3},{2,0},{3,1},{4,6},{5,7},{6,4},{7,5},{8,10},{9,11},{10,... | collective-permute-start | bytes 294920 | tf_op jit(solution)/shard_map/ppermute | solution.py:152
  19.6 1.9 %collective-permute-done.6.second = bf16[3,32,1152]{2,1,0:T(8,128)(2,1)S(1)} collective-permute-done((bf16[3,32,1152]{2,1,0:T(8,128)(2,1)S(1)}, bf16[3,32,1152]{2,1,0:T(8,128)(2,1)S(1)}, u32[]{:S(2)}, u32[]{:S(2)}) %collective-permute-start.6) | collective-permute-done | bytes 221216 | tf_op jit(solution)/shard_map/ppermute | solution.py:152
  21.5 0.6 collective-permute-done.5.away
  22.1 1.0 %shard_map.87 = (f32[3,64,256]{2,1,0:T(8,128)S(1)}, bf16[3,64,256]{2,1,0:T(8,128)(2,1)S(1)}) custom-call(s32[3]{0:T(128)S(1)} %pad_add_fusion.info, bf16[3,32,1152]{2,1,0:T(8,128)(2,1)S(1)} %collective-permute-done.4.at_home, bf16[3,32,1152]{2,1,0:T(8,128)(2,1)S(1)} %collective-permute-done.5.away, bf16[3,32,1152]{2,1,0:T(8,128)(2,1)S(1)} %collective-permute-done.6.second, ...), custom_call_target="tpu_custom_call" | custom-call | tf_op jit(solution)/shard_map/pallas_call | solution.py:23
  23.0 1.9 %collective-permute-start.9 = (bf16[3,64,256]{2,1,0:T(8,128)(2,1)S(1)}, bf16[3,64,256]{2,1,0:T(8,128)(2,1)S(1)}, u32[]{:S(2)}, u32[]{:S(2)}) collective-permute-start(bf16[3,64,256]{2,1,0:T(8,128)(2,1)S(1)} %get-tuple-element.62), channel_id=1, source_target_pairs={{0,2},{1,3},{2,0},{3,1},{4,6},{5,7},{6,4},{7,5},{8,10},{9,11},{10,... | collective-permute-start | bytes 294920 | tf_op jit(solution)/shard_map/ppermute | solution.py:152
  24.9 0.0 collective-permute-done.8.other
  24.9 0.8 shard_map.88.weight
  25.7 0.0 collective-permute-done.7.got
  25.7 1.7 %shard_map.89 = (bf16[3,64,256]{2,1,0:T(8,128)(2,1)S(1)}, f32[3,32,1152]{2,1,0:T(8,128)S(1)}, f32[3,32,1152]{2,1,0:T(8,128)S(1)}) custom-call(s32[3]{0:T(128)S(1)} %bitcast.13, f32[3,64,256]{2,1,0:T(8,128)S(1)} %get-tuple-element.57.part, bf16[3,64,256]{2,1,0:T(8,128)(2,1)S(1)} %collective-permute-done.7.got, f32[3,256]{1,0:T(4,128)S(1)} %copy-done.2, ...), custom_call_target="tpu_custom_call" | custom-call | tf_op jit(solution)/shard_map/pallas_call | solution.py:23
  27.5 0.9 %collective-permute-done.9.got = bf16[3,64,256]{2,1,0:T(8,128)(2,1)S(1)} collective-permute-done((bf16[3,64,256]{2,1,0:T(8,128)(2,1)S(1)}, bf16[3,64,256]{2,1,0:T(8,128)(2,1)S(1)}, u32[]{:S(2)}, u32[]{:S(2)}) %collective-permute-start.9) | collective-permute-done | bytes 98336 | tf_op jit(solution)/shard_map/ppermute | solution.py:152
  28.3 1.7 %shard_map.90 = (bf16[3,64,256]{2,1,0:T(8,128)(2,1)S(1)}, bf16[3,32,1152]{2,1,0:T(8,128)(2,1)S(1)}, bf16[3,32,1152]{2,1,0:T(8,128)(2,1)S(1)}) custom-call(s32[3]{0:T(128)S(1)} %bitcast.14, f32[3,64,256]{2,1,0:T(8,128)S(1)} %get-tuple-element.64.part, bf16[3,64,256]{2,1,0:T(8,128)(2,1)S(1)} %collective-permute-done.9.got, f32[3,256]{1,0:T(4,128)S(1)} %copy-done.2, ...), custom_call_target="tpu_custom_call" | custom-call | tf_op jit(solution)/shard_map/pallas_call | solution.py:23
  30.0 0.0 copy-start.4
  30.0 2.1 %collective-permute-start.12 = (bf16[3,32,1152]{2,1,0:T(8,128)(2,1)S(1)}, bf16[3,32,1152]{2,1,0:T(8,128)(2,1)S(1)}, u32[]{:S(2)}, u32[]{:S(2)}) collective-permute-start(bf16[3,32,1152]{2,1,0:T(8,128)(2,1)S(1)} %get-tuple-element.68), channel_id=1, source_target_pairs={{0,4},{1,5},{2,6},{3,7},{4,0},{5,1},{6,2},{7,3},{8,12},{9,13},{10,... | collective-permute-start | bytes 663560 | tf_op jit(solution)/shard_map/ppermute | solution.py:152
  32.2 0.1 collective-permute-start.10
  32.2 6.1 %collective-permute-done.12 = bf16[3,32,1152]{2,1,0:T(8,128)(2,1)S(1)} collective-permute-done((bf16[3,32,1152]{2,1,0:T(8,128)(2,1)S(1)}, bf16[3,32,1152]{2,1,0:T(8,128)(2,1)S(1)}, u32[]{:S(2)}, u32[]{:S(2)}) %collective-permute-start.12) | collective-permute-done | bytes 221216 | tf_op jit(solution)/shard_map/ppermute | solution.py:152
  38.4 2.5 %collective-permute-start.13 = (bf16[3,32,1152]{2,1,0:T(8,128)(2,1)S(1)}, bf16[3,32,1152]{2,1,0:T(8,128)(2,1)S(1)}, u32[]{:S(2)}, u32[]{:S(2)}) collective-permute-start(bf16[3,32,1152]{2,1,0:T(8,128)(2,1)S(1)} %add_convert_fusion), channel_id=1, source_target_pairs={{0,16},{1,8},{2,18},{3,10},{4,20},{5,12},{6,22},{7,14},{8,1},{9,25... | collective-permute-start | bytes 663560 | tf_op jit(solution)/shard_map/ppermute | solution.py:152
  40.9 1.7 %collective-permute-done.10 = bf16[3,32,1152]{2,1,0:T(8,128)(2,1)S(1)} collective-permute-done((bf16[3,32,1152]{2,1,0:T(8,128)(2,1)S(1)}, bf16[3,32,1152]{2,1,0:T(8,128)(2,1)S(1)}, u32[]{:S(2)}, u32[]{:S(2)}) %collective-permute-start.10) | collective-permute-done | bytes 221216 | tf_op jit(solution)/shard_map/ppermute | solution.py:152
  42.6 0.1 fusion
  42.7 1.8 %collective-permute-start.11 = (bf16[3,32,1152]{2,1,0:T(8,128)(2,1)S(1)}, bf16[3,32,1152]{2,1,0:T(8,128)(2,1)S(1)}, u32[]{:S(2)}, u32[]{:S(2)}) collective-permute-start(bf16[3,32,1152]{2,1,0:T(8,128)(2,1)S(1)} %fusion), channel_id=1, source_target_pairs={{0,4},{1,24},{2,6},{3,26},{4,0},{5,28},{6,2},{7,30},{8,17},{9,13},... | collective-permute-start | bytes 663560 | tf_op jit(solution)/shard_map/ppermute | solution.py:152
  44.5 1.0 %collective-permute-done.13 = bf16[3,32,1152]{2,1,0:T(8,128)(2,1)S(1)} collective-permute-done((bf16[3,32,1152]{2,1,0:T(8,128)(2,1)S(1)}, bf16[3,32,1152]{2,1,0:T(8,128)(2,1)S(1)}, u32[]{:S(2)}, u32[]{:S(2)}) %collective-permute-start.13) | collective-permute-done | bytes 221216 | tf_op jit(solution)/shard_map/ppermute | solution.py:152
  45.4 3.2 %collective-permute-done.11 = bf16[3,32,1152]{2,1,0:T(8,128)(2,1)S(1)} collective-permute-done((bf16[3,32,1152]{2,1,0:T(8,128)(2,1)S(1)}, bf16[3,32,1152]{2,1,0:T(8,128)(2,1)S(1)}, u32[]{:S(2)}, u32[]{:S(2)}) %collective-permute-start.11) | collective-permute-done | bytes 221216 | tf_op jit(solution)/shard_map/ppermute | solution.py:152
  48.7 0.1 convert_add_fusion
  48.8 1.0 %collective-permute-start.14 = (f32[3,32,1152]{2,1,0:T(8,128)S(1)}, f32[3,32,1152]{2,1,0:T(8,128)S(1)}, u32[]{:S(2)}, u32[]{:S(2)}) collective-permute-start(f32[3,32,1152]{2,1,0:T(8,128)S(1)} %convert_add_fusion), channel_id=1, source_target_pairs={{0,1},{1,0},{2,3},{3,2},{4,5},{5,4},{6,7},{7,6},{8,9},{9,8},{10,11... | collective-permute-start | bytes 1327112 | tf_op jit(solution)/shard_map/ppermute | solution.py:152
  49.8 0.1 collective-permute-start.15
  49.8 0.1 pad_select_fusion
  50.0 1.4 %collective-permute-done.15 = bf16[3,32,576]{2,1,0:T(8,128)(2,1)S(1)} collective-permute-done((bf16[3,32,576]{2,1,0:T(8,128)(2,1)S(1)}, bf16[3,32,576]{2,1,0:T(8,128)(2,1)S(1)}, u32[]{:S(2)}, u32[]{:S(2)}) %collective-permute-start.15) | collective-permute-done | bytes 110624 | tf_op jit(solution)/shard_map/ppermute | solution.py:152
  51.4 0.2 subtract_convert_fusion
  51.6 2.9 %collective-permute-start.16 = (bf16[3,32,1152]{2,1,0:T(8,128)(2,1)S(1)}, bf16[3,32,1152]{2,1,0:T(8,128)(2,1)S(1)}, u32[]{:S(2)}, u32[]{:S(2)}) collective-permute-start(bf16[3,32,1152]{2,1,0:T(8,128)(2,1)S(1)} %get-tuple-element.75.own), channel_id=1, source_target_pairs={{0,16},{1,8},{2,18},{3,10},{4,20},{5,12},{6,22},{7,14},{8,1},{9,25... | collective-permute-start | bytes 663560 | tf_op jit(solution)/shard_map/ppermute | solution.py:152
  54.4 6.4 %collective-permute-done.16.r1 = bf16[3,32,1152]{2,1,0:T(8,128)(2,1)S(1)} collective-permute-done((bf16[3,32,1152]{2,1,0:T(8,128)(2,1)S(1)}, bf16[3,32,1152]{2,1,0:T(8,128)(2,1)S(1)}, u32[]{:S(2)}, u32[]{:S(2)}) %collective-permute-start.16) | collective-permute-done | bytes 221216 | tf_op jit(solution)/shard_map/ppermute | solution.py:152
  60.8 0.6 collective-permute-start.21
  61.4 1.5 %collective-permute-start.20 = (bf16[3,32,1152]{2,1,0:T(8,128)(2,1)S(1)}, bf16[3,32,1152]{2,1,0:T(8,128)(2,1)S(1)}, u32[]{:S(2)}, u32[]{:S(2)}) collective-permute-start(bf16[3,32,1152]{2,1,0:T(8,128)(2,1)S(1)} %collective-permute-done.16.r1), channel_id=1, source_target_pairs={{0,4},{1,5},{2,6},{3,7},{4,0},{5,1},{6,2},{7,3},{8,12},{9,13},{10,... | collective-permute-start | bytes 663560 | tf_op jit(solution)/shard_map/ppermute | solution.py:152
  62.9 1.4 %collective-permute-done.17.third = bf16[3,32,1152]{2,1,0:T(8,128)(2,1)S(1)} collective-permute-done((bf16[3,32,1152]{2,1,0:T(8,128)(2,1)S(1)}, bf16[3,32,1152]{2,1,0:T(8,128)(2,1)S(1)}, u32[]{:S(2)}, u32[]{:S(2)}) %collective-permute-start.17) | collective-permute-done | bytes 221216 | tf_op jit(solution)/shard_map/ppermute | solution.py:152
  64.3 0.0 collective-permute-start.19
  64.3 0.8 fusion.1
  65.0 0.0 collective-permute-done.21.latents_got
  65.0 4.7 %collective-permute-done.20.r3 = bf16[3,32,1152]{2,1,0:T(8,128)(2,1)S(1)} collective-permute-done((bf16[3,32,1152]{2,1,0:T(8,128)(2,1)S(1)}, bf16[3,32,1152]{2,1,0:T(8,128)(2,1)S(1)}, u32[]{:S(2)}, u32[]{:S(2)}) %collective-permute-start.20) | collective-permute-done | bytes 221216 | tf_op jit(solution)/shard_map/ppermute | solution.py:152
  69.7 1.3 %shard_map.91 = (f32[3,64,256]{2,1,0:T(8,128)S(1)}, bf16[3,64,256]{2,1,0:T(8,128)(2,1)S(1)}, bf16[3,128,1152]{2,1,0:T(8,128)(2,1)S(1)}) custom-call(s32[3]{0:T(128)S(1)} %pad_add_fusion.info, bf16[3,32,1152]{2,1,0:T(8,128)(2,1)S(1)} %get-tuple-element.75.own, bf16[3,32,1152]{2,1,0:T(8,128)(2,1)S(1)} %collective-permute-done.18.beside, ...), custom_call_target="tpu_custom_call" | custom-call | tf_op jit(solution)/shard_map/pallas_call | solution.py:23
  71.0 0.2 slice_select_fusion
  71.2 1.4 %collective-permute-start.23 = (bf16[3,128,576]{2,1,0:T(8,128)(2,1)S(1)}, bf16[3,128,576]{2,1,0:T(8,128)(2,1)S(1)}, u32[]{:S(2)}, u32[]{:S(2)}) collective-permute-start(bf16[3,128,576]{2,1,0:T(8,128)(2,1)S(1)} %slice_select_fusion), channel_id=1, source_target_pairs={{0,1},{1,0},{2,3},{3,2},{4,5},{5,4},{6,7},{7,6},{8,9},{9,8},{10,11... | collective-permute-start | bytes 1327112 | tf_op jit(solution)/shard_map/ppermute | solution.py:152
  72.6 1.4 %collective-permute-start.22 = (bf16[3,64,256]{2,1,0:T(8,128)(2,1)S(1)}, bf16[3,64,256]{2,1,0:T(8,128)(2,1)S(1)}, u32[]{:S(2)}, u32[]{:S(2)}) collective-permute-start(bf16[3,64,256]{2,1,0:T(8,128)(2,1)S(1)} %get-tuple-element.81), channel_id=1, source_target_pairs={{0,2},{1,3},{2,0},{3,1},{4,6},{5,7},{6,4},{7,5},{8,10},{9,11},{10,... | collective-permute-start | bytes 294920 | tf_op jit(solution)/shard_map/ppermute | solution.py:152
  74.0 0.1 iota_compare_fusion.1
  74.1 2.2 %shard_map.92 = bf16[6,576,256]{2,1,0:T(8,128)(2,1)} custom-call(s32[3]{0:T(128)S(1)} %pad_add_fusion.info, bf16[3,128,1152]{2,1,0:T(8,128)(2,1)S(1)} %get-tuple-element.82.held, bf16[3,128,576]{2,1,0:T(8,128)(2,1)S(1)} %collective-permute-done.23.errors_got, bf16[3,128,256]{2,1,0:T(8,128)(2,1)S(1)} %constant_dynamic-update-slice_fusion.latents, ...), custom_call_target="tpu_custom_call" | custom-call | tf_op jit(solution)/shard_map/pallas_call | solution.py:273
  76.3 1.1 %collective-permute-done.22 = bf16[3,64,256]{2,1,0:T(8,128)(2,1)S(1)} collective-permute-done((bf16[3,64,256]{2,1,0:T(8,128)(2,1)S(1)}, bf16[3,64,256]{2,1,0:T(8,128)(2,1)S(1)}, u32[]{:S(2)}, u32[]{:S(2)}) %collective-permute-start.22) | collective-permute-done | bytes 98336 | tf_op jit(solution)/shard_map/ppermute | solution.py:152
  77.4 0.7 fusion.4
  (19 shorter events, 0.1 us)
Async XLA Ops:
  0.6 1.7 %collective-permute-start = (bf16[3,32,576]{2,1,0:T(8,128)(2,1)}, bf16[3,32,576]{2,1,0:T(8,128)(2,1)S(1)}, u32[]{:S(2)}, u32[]{:S(2)}) collective-permute-start(bf16[3,32,576]{2,1,0:T(8,128)(2,1)} %bitcast.18), channel_id=1, source_target_pairs={{0,1},{1,0},{2,3},{3,2},{4,5},{5,4},{6,7},{7,6},{8,9},{9,8},{10,11... | collective-permute-start | bytes 331784 | tf_op jit(solution)/shard_map/ppermute | solution.py:152
  2.4 22.5 %collective-permute-start.8 = (bf16[6,576,256]{2,1,0:T(8,128)(2,1)}, bf16[6,576,256]{2,1,0:T(8,128)(2,1)S(1)}, u32[]{:S(2)}, u32[]{:S(2)}) collective-permute-start(bf16[6,576,256]{2,1,0:T(8,128)(2,1)} %bitcast.11), channel_id=1, source_target_pairs={{0,1},{1,0},{2,3},{3,2},{4,5},{5,4},{6,7},{7,6},{8,9},{9,8},{10,11... | collective-permute-start | bytes 5308424 | tf_op jit(solution)/shard_map/ppermute | solution.py:152
  2.9 4.8 %collective-permute-start.2 = (bf16[3,576,256]{2,1,0:T(8,128)(2,1)}, bf16[3,576,256]{2,1,0:T(8,128)(2,1)S(1)}, u32[]{:S(2)}, u32[]{:S(2)}) collective-permute-start(bf16[3,576,256]{2,1,0:T(8,128)(2,1)} %own), channel_id=1, source_target_pairs={{0,1},{1,0},{2,3},{3,2},{4,5},{5,4},{6,7},{7,6},{8,9},{9,8},{10,11... | collective-permute-start | bytes 2654216 | tf_op jit(solution)/shard_map/ppermute | solution.py:152
  3.0 10.2 %collective-permute-start.1 = (bf16[3,32,1152]{2,1,0:T(8,128)(2,1)S(1)}, bf16[3,32,1152]{2,1,0:T(8,128)(2,1)S(1)}, u32[]{:S(2)}, u32[]{:S(2)}) collective-permute-start(bf16[3,32,1152]{2,1,0:T(8,128)(2,1)S(1)} %select_select_fusion.at_home), channel_id=1, source_target_pairs={{0,16},{1,8},{2,18},{3,10},{4,20},{5,12},{6,22},{7,14},{8,1},{9,25... | collective-permute-start | bytes 663560 | tf_op jit(solution)/shard_map/ppermute | solution.py:152
  7.0 8.1 %collective-permute-start.4 = (bf16[3,32,1152]{2,1,0:T(8,128)(2,1)S(1)}, bf16[3,32,1152]{2,1,0:T(8,128)(2,1)S(1)}, u32[]{:S(2)}, u32[]{:S(2)}) collective-permute-start(bf16[3,32,1152]{2,1,0:T(8,128)(2,1)S(1)} %select_select_fusion.at_home), channel_id=1, source_target_pairs={{0,1},{1,4},{2,3},{3,6},{4,5},{5,0},{6,7},{7,2},{8,13},{9,8},{10,1... | collective-permute-start | bytes 663560 | tf_op jit(solution)/shard_map/ppermute | solution.py:152
  7.7 1.2 %copy-start.1 = (bf16[3,576,256]{2,1,0:T(8,128)(2,1)S(1)}, bf16[3,576,256]{2,1,0:T(8,128)(2,1)}, u32[]{:S(2)}) copy-start(bf16[3,576,256]{2,1,0:T(8,128)(2,1)} %own) | copy-start | bytes 2654212
  13.2 3.5 %collective-permute-start.3 = (bf16[3,32,1152]{2,1,0:T(8,128)(2,1)S(1)}, bf16[3,32,1152]{2,1,0:T(8,128)(2,1)S(1)}, u32[]{:S(2)}, u32[]{:S(2)}) collective-permute-start(bf16[3,32,1152]{2,1,0:T(8,128)(2,1)S(1)} %collective-permute-done.1.second), channel_id=1, source_target_pairs={{0,8},{1,0},{2,10},{3,2},{4,12},{5,4},{6,14},{7,6},{8,9},{9,1},{10... | collective-permute-start | bytes 663560 | tf_op jit(solution)/shard_map/ppermute | solution.py:152
  13.3 8.2 %collective-permute-start.6 = (bf16[3,32,1152]{2,1,0:T(8,128)(2,1)S(1)}, bf16[3,32,1152]{2,1,0:T(8,128)(2,1)S(1)}, u32[]{:S(2)}, u32[]{:S(2)}) collective-permute-start(bf16[3,32,1152]{2,1,0:T(8,128)(2,1)S(1)} %collective-permute-done.1.second), channel_id=1, source_target_pairs={{0,4},{1,5},{2,6},{3,7},{4,0},{5,1},{6,2},{7,3},{8,12},{9,13},{10,... | collective-permute-start | bytes 663560 | tf_op jit(solution)/shard_map/ppermute | solution.py:152
  16.7 5.4 %collective-permute-start.5 = (bf16[3,32,1152]{2,1,0:T(8,128)(2,1)S(1)}, bf16[3,32,1152]{2,1,0:T(8,128)(2,1)S(1)}, u32[]{:S(2)}, u32[]{:S(2)}) collective-permute-start(bf16[3,32,1152]{2,1,0:T(8,128)(2,1)S(1)} %collective-permute-done.3.away), channel_id=1, source_target_pairs={{0,9},{1,5},{2,11},{3,7},{4,13},{5,1},{6,15},{7,3},{8,12},{9,0},{1... | collective-permute-start | bytes 663560 | tf_op jit(solution)/shard_map/ppermute | solution.py:152
  17.7 7.3 %copy-start = (bf16[6,256,576]{1,2,0:T(8,128)(2,1)S(1)}, bf16[6,256,576]{1,2,0:T(8,128)(2,1)}, u32[]{:S(2)}) copy-start(bf16[6,256,576]{1,2,0:T(8,128)(2,1)} %param.10) | copy-start | bytes 5308420
  17.7 8.0 %collective-permute-start.7 = (bf16[3,64,256]{2,1,0:T(8,128)(2,1)S(1)}, bf16[3,64,256]{2,1,0:T(8,128)(2,1)S(1)}, u32[]{:S(2)}, u32[]{:S(2)}) collective-permute-start(bf16[3,64,256]{2,1,0:T(8,128)(2,1)S(1)} %get-tuple-element.58), channel_id=1, source_target_pairs={{0,2},{1,3},{2,0},{3,1},{4,6},{5,7},{6,4},{7,5},{8,10},{9,11},{10,... | collective-permute-start | bytes 294920 | tf_op jit(solution)/shard_map/ppermute | solution.py:152
  23.0 5.3 %collective-permute-start.9 = (bf16[3,64,256]{2,1,0:T(8,128)(2,1)S(1)}, bf16[3,64,256]{2,1,0:T(8,128)(2,1)S(1)}, u32[]{:S(2)}, u32[]{:S(2)}) collective-permute-start(bf16[3,64,256]{2,1,0:T(8,128)(2,1)S(1)} %get-tuple-element.62), channel_id=1, source_target_pairs={{0,2},{1,3},{2,0},{3,1},{4,6},{5,7},{6,4},{7,5},{8,10},{9,11},{10,... | collective-permute-start | bytes 294920 | tf_op jit(solution)/shard_map/ppermute | solution.py:152
  24.9 0.8 %copy-start.2 = (f32[3,256]{1,0:T(4,128)S(1)}, f32[3,256]{1,0:T(4,128)}, u32[]{:S(2)}) copy-start(f32[3,256]{1,0:T(4,128)} %bias.3) | copy-start | bytes 9220
  24.9 0.8 %copy-start.3 = (s32[3,1]{0,1:T(1,128)S(1)}, s32[3,1]{0,1:T(1,128)}, u32[]{:S(2)}) copy-start(s32[3,1]{0,1:T(1,128)} %param.11) | copy-start | bytes 40
  30.0 19.7 %copy-start.4 = (bf16[32,3,576]{2,0,1:T(8,128)(2,1)S(1)}, bf16[32,3,576]{2,0,1:T(8,128)(2,1)}, u32[]{:S(2)}) copy-start(bf16[32,3,576]{2,0,1:T(8,128)(2,1)} %param.7) | copy-start | bytes 331780
  30.0 8.3 %collective-permute-start.12 = (bf16[3,32,1152]{2,1,0:T(8,128)(2,1)S(1)}, bf16[3,32,1152]{2,1,0:T(8,128)(2,1)S(1)}, u32[]{:S(2)}, u32[]{:S(2)}) collective-permute-start(bf16[3,32,1152]{2,1,0:T(8,128)(2,1)S(1)} %get-tuple-element.68), channel_id=1, source_target_pairs={{0,4},{1,5},{2,6},{3,7},{4,0},{5,1},{6,2},{7,3},{8,12},{9,13},{10,... | collective-permute-start | bytes 663560 | tf_op jit(solution)/shard_map/ppermute | solution.py:152
  32.2 10.4 %collective-permute-start.10 = (bf16[3,32,1152]{2,1,0:T(8,128)(2,1)S(1)}, bf16[3,32,1152]{2,1,0:T(8,128)(2,1)S(1)}, u32[]{:S(2)}, u32[]{:S(2)}) collective-permute-start(bf16[3,32,1152]{2,1,0:T(8,128)(2,1)S(1)} %get-tuple-element.66), channel_id=1, source_target_pairs={{0,4},{1,5},{2,6},{3,7},{4,0},{5,1},{6,2},{7,3},{8,12},{9,13},{10,... | collective-permute-start | bytes 663560 | tf_op jit(solution)/shard_map/ppermute | solution.py:152
  38.4 7.0 %collective-permute-start.13 = (bf16[3,32,1152]{2,1,0:T(8,128)(2,1)S(1)}, bf16[3,32,1152]{2,1,0:T(8,128)(2,1)S(1)}, u32[]{:S(2)}, u32[]{:S(2)}) collective-permute-start(bf16[3,32,1152]{2,1,0:T(8,128)(2,1)S(1)} %add_convert_fusion), channel_id=1, source_target_pairs={{0,16},{1,8},{2,18},{3,10},{4,20},{5,12},{6,22},{7,14},{8,1},{9,25... | collective-permute-start | bytes 663560 | tf_op jit(solution)/shard_map/ppermute | solution.py:152
  42.7 6.0 %collective-permute-start.11 = (bf16[3,32,1152]{2,1,0:T(8,128)(2,1)S(1)}, bf16[3,32,1152]{2,1,0:T(8,128)(2,1)S(1)}, u32[]{:S(2)}, u32[]{:S(2)}) collective-permute-start(bf16[3,32,1152]{2,1,0:T(8,128)(2,1)S(1)} %fusion), channel_id=1, source_target_pairs={{0,4},{1,24},{2,6},{3,26},{4,0},{5,28},{6,2},{7,30},{8,17},{9,13},... | collective-permute-start | bytes 663560 | tf_op jit(solution)/shard_map/ppermute | solution.py:152
  48.8 2.6 %collective-permute-start.14 = (f32[3,32,1152]{2,1,0:T(8,128)S(1)}, f32[3,32,1152]{2,1,0:T(8,128)S(1)}, u32[]{:S(2)}, u32[]{:S(2)}) collective-permute-start(f32[3,32,1152]{2,1,0:T(8,128)S(1)} %convert_add_fusion), channel_id=1, source_target_pairs={{0,1},{1,0},{2,3},{3,2},{4,5},{5,4},{6,7},{7,6},{8,9},{9,8},{10,11... | collective-permute-start | bytes 1327112 | tf_op jit(solution)/shard_map/ppermute | solution.py:152
  49.8 1.6 %collective-permute-start.15 = (bf16[3,32,576]{2,1,0:T(8,128)(2,1)S(1)}, bf16[3,32,576]{2,1,0:T(8,128)(2,1)S(1)}, u32[]{:S(2)}, u32[]{:S(2)}) collective-permute-start(bf16[3,32,576]{2,1,0:T(8,128)(2,1)S(1)} %bitcast.20), channel_id=1, source_target_pairs={{0,1},{1,0},{2,3},{3,2},{4,5},{5,4},{6,7},{7,6},{8,9},{9,8},{10,11... | collective-permute-start | bytes 331784 | tf_op jit(solution)/shard_map/ppermute | solution.py:152
  51.6 9.3 %collective-permute-start.16 = (bf16[3,32,1152]{2,1,0:T(8,128)(2,1)S(1)}, bf16[3,32,1152]{2,1,0:T(8,128)(2,1)S(1)}, u32[]{:S(2)}, u32[]{:S(2)}) collective-permute-start(bf16[3,32,1152]{2,1,0:T(8,128)(2,1)S(1)} %get-tuple-element.75.own), channel_id=1, source_target_pairs={{0,16},{1,8},{2,18},{3,10},{4,20},{5,12},{6,22},{7,14},{8,1},{9,25... | collective-permute-start | bytes 663560 | tf_op jit(solution)/shard_map/ppermute | solution.py:152
  54.4 8.5 %collective-permute-start.18 = (bf16[3,32,1152]{2,1,0:T(8,128)(2,1)S(1)}, bf16[3,32,1152]{2,1,0:T(8,128)(2,1)S(1)}, u32[]{:S(2)}, u32[]{:S(2)}) collective-permute-start(bf16[3,32,1152]{2,1,0:T(8,128)(2,1)S(1)} %get-tuple-element.75.own), channel_id=1, source_target_pairs={{0,1},{1,4},{2,3},{3,6},{4,5},{5,0},{6,7},{7,2},{8,13},{9,8},{10,1... | collective-permute-start | bytes 663560 | tf_op jit(solution)/shard_map/ppermute | solution.py:152
  60.8 3.5 %collective-permute-start.17 = (bf16[3,32,1152]{2,1,0:T(8,128)(2,1)S(1)}, bf16[3,32,1152]{2,1,0:T(8,128)(2,1)S(1)}, u32[]{:S(2)}, u32[]{:S(2)}) collective-permute-start(bf16[3,32,1152]{2,1,0:T(8,128)(2,1)S(1)} %collective-permute-done.16.r1), channel_id=1, source_target_pairs={{0,8},{1,0},{2,10},{3,2},{4,12},{5,4},{6,14},{7,6},{8,9},{9,1},{10... | collective-permute-start | bytes 663560 | tf_op jit(solution)/shard_map/ppermute | solution.py:152
  60.8 4.2 %collective-permute-start.21 = (bf16[3,128,256]{2,1,0:T(8,128)(2,1)S(1)}, bf16[3,128,256]{2,1,0:T(8,128)(2,1)S(1)}, u32[]{:S(2)}, u32[]{:S(2)}) collective-permute-start(bf16[3,128,256]{2,1,0:T(8,128)(2,1)S(1)} %constant_dynamic-update-slice_fusion.latents), channel_id=1, source_target_pairs={{0,1},{1,0},{2,3},{3,2},{4,5},{5,4},{6,7},{7,6},{8,9},{9,8},{10,11... | collective-permute-start | bytes 589832 | tf_op jit(solution)/shard_map/ppermute | solution.py:152
  61.4 8.3 %collective-permute-start.20 = (bf16[3,32,1152]{2,1,0:T(8,128)(2,1)S(1)}, bf16[3,32,1152]{2,1,0:T(8,128)(2,1)S(1)}, u32[]{:S(2)}, u32[]{:S(2)}) collective-permute-start(bf16[3,32,1152]{2,1,0:T(8,128)(2,1)S(1)} %collective-permute-done.16.r1), channel_id=1, source_target_pairs={{0,4},{1,5},{2,6},{3,7},{4,0},{5,1},{6,2},{7,3},{8,12},{9,13},{10,... | collective-permute-start | bytes 663560 | tf_op jit(solution)/shard_map/ppermute | solution.py:152
  64.3 5.4 %collective-permute-start.19 = (bf16[3,32,1152]{2,1,0:T(8,128)(2,1)S(1)}, bf16[3,32,1152]{2,1,0:T(8,128)(2,1)S(1)}, u32[]{:S(2)}, u32[]{:S(2)}) collective-permute-start(bf16[3,32,1152]{2,1,0:T(8,128)(2,1)S(1)} %collective-permute-done.17.third), channel_id=1, source_target_pairs={{0,9},{1,5},{2,11},{3,7},{4,13},{5,1},{6,15},{7,3},{8,12},{9,0},{1... | collective-permute-start | bytes 663560 | tf_op jit(solution)/shard_map/ppermute | solution.py:152
  71.2 2.9 %collective-permute-start.23 = (bf16[3,128,576]{2,1,0:T(8,128)(2,1)S(1)}, bf16[3,128,576]{2,1,0:T(8,128)(2,1)S(1)}, u32[]{:S(2)}, u32[]{:S(2)}) collective-permute-start(bf16[3,128,576]{2,1,0:T(8,128)(2,1)S(1)} %slice_select_fusion), channel_id=1, source_target_pairs={{0,1},{1,0},{2,3},{3,2},{4,5},{5,4},{6,7},{7,6},{8,9},{9,8},{10,11... | collective-permute-start | bytes 1327112 | tf_op jit(solution)/shard_map/ppermute | solution.py:152
  72.6 4.8 %collective-permute-start.22 = (bf16[3,64,256]{2,1,0:T(8,128)(2,1)S(1)}, bf16[3,64,256]{2,1,0:T(8,128)(2,1)S(1)}, u32[]{:S(2)}, u32[]{:S(2)}) collective-permute-start(bf16[3,64,256]{2,1,0:T(8,128)(2,1)S(1)} %get-tuple-element.81), channel_id=1, source_target_pairs={{0,2},{1,3},{2,0},{3,1},{4,6},{5,7},{6,4},{7,5},{8,10},{9,11},{10,... | collective-permute-start | bytes 294920 | tf_op jit(solution)/shard_map/ppermute | solution.py:152

commit v6 on v5

--- a/solution.py
+++ b/solution.py
@@ -128,10 +128,10 @@
 
     copies = []
     for target in range(layers):
-        rows = jnp.concatenate([own[target], errors_got[target]], 0)
+        across = jnp.concatenate([own[target], errors_got[target]], 0).T
         for source in range(target + 1):
             values = jnp.concatenate([latents[source], latents_got[source]], 0)
-            total = lax.dot_general(rows, values, (((0,), (0,)), ((), ())), preferred_element_type=F32)
+            total = jnp.dot(across, values, preferred_element_type=F32)
             at = block_index(source, target, layers)
             blocks[at] = total.astype(BF)
             copies.append(pltpu.make_async_copy(blocks.at[at], out.at[at], sems.at[at]))
@@ -247,6 +247,7 @@
         late_part, late_sent = encode(beside, fourth, r3)
         late_got = over_x(late_sent)
         part, late_part = lax.optimization_barrier((part, late_part))
+        part, wanted = lax.optimization_barrier((part, wanted))
         early, q0, q2 = decode(part, got, F32)
         late_part, late_got, early = lax.optimization_barrier((late_part, late_got, early))
         late, q1, q3 = decode(late_part, late_got, BF)

time: 78.3 us -> 78.2 us (level)
  transfers between devices with their start and end apart: 24 -> 24, of which waited for: 16 -> 14; matrix products, arithmetic and copies ran while one was open for 3% -> 3% of each run, Pallas kernels for 9% -> 9%
where the time goes in v6:
time: 78.2 us; the launch traced here: 78 us
  waiting for transfers between devices  35.9 us (46%)
  starting transfers between devices  26.3 us (34%)
  Pallas kernels  10.2 us (13%)
  other arithmetic  3.5 us (4%)
  local copies, waits for them, and re-layouts  1.21 us (2%)
  between operations  0.86 us (1%)
    ppermute x24, waiting for transfers between devices, swap(): return lax.ppermute(value, AXES, pairs)  35.9 us
    ppermute x24, starting transfers between devices, swap(): return lax.ppermute(value, AXES, pairs)  26.3 us
    pallas_call x7, Pallas kernels, fused(): pl.pallas_call(body, out_shape=out_shape, in_specs=specs, out_specs=[pl.B...  8.06 us
    pallas_call x1, Pallas kernels, local(): pl.pallas_call(weight_grad_kernel, out_shape=jax.ShapeDtypeStruct(shape,...  2.18 us
  transfers between devices with their start and end apart: 24, of which 14 were waited for; matrix products, arithmetic and copies ran while one was open for 3% of the time, Pallas kernels for 9%

profile of v6, /device:TPU:0, one launch (start us, length us, event | category | flops | bytes accessed | tf_op | source)
XLA Modules:
  0.0 78.0 jit_solution(7879934768058364803)
XLA Ops:
  0.6 0.5 collective-permute-start
  1.1 1.1 %pad_select_fusion.1 = bf16[3,32,1152]{2,1,0:T(8,128)(2,1)S(1)} fusion(bf16[3,32,576]{2,1,0:T(8,128)(2,1)} %bitcast.19, pred[]{:T(512)S(6)} %eq.33), kind=kLoop, calls=%fused_computation.11 | loop fusion | flops 110592 | bytes 331777 | tf_op jit(solution)/shard_map/jit(_where)/select_n | solution.py:212
  2.2 0.1 collective-permute-done
  2.3 0.1 select_select_fusion.1.at_home
  2.4 0.4 collective-permute-start.2
  2.9 0.1 collective-permute-start.9
  3.0 3.9 %collective-permute-start.1 = (bf16[3,32,1152]{2,1,0:T(8,128)(2,1)S(1)}, bf16[3,32,1152]{2,1,0:T(8,128)(2,1)S(1)}, u32[]{:S(2)}, u32[]{:S(2)}) collective-permute-start(bf16[3,32,1152]{2,1,0:T(8,128)(2,1)S(1)} %select_select_fusion.1.at_home), channel_id=1, source_target_pairs={{0,16},{1,8},{2,18},{3,10},{4,20},{5,12},{6,22},{7,14},{8,1},{9,25... | collective-permute-start | bytes 663560 | tf_op jit(solution)/shard_map/ppermute | solution.py:152
  7.0 0.1 pad_add_fusion.info
  7.0 0.0 collective-permute-start.4
  7.0 0.0 collective-permute-done.2.other
  7.1 0.0 copy-start.1
  7.1 1.2 %copy-done.1 = bf16[3,576,256]{2,1,0:T(8,128)(2,1)S(1)} copy-done((bf16[3,576,256]{2,1,0:T(8,128)(2,1)S(1)}, bf16[3,576,256]{2,1,0:T(8,128)(2,1)}, u32[]{:S(2)}) %copy-start.1) | copy-done | bytes 884760
  8.2 0.7 shard_map.85.weight
  8.9 4.4 %collective-permute-done.1.second = bf16[3,32,1152]{2,1,0:T(8,128)(2,1)S(1)} collective-permute-done((bf16[3,32,1152]{2,1,0:T(8,128)(2,1)S(1)}, bf16[3,32,1152]{2,1,0:T(8,128)(2,1)S(1)}, u32[]{:S(2)}, u32[]{:S(2)}) %collective-permute-start.1) | collective-permute-done | bytes 221216 | tf_op jit(solution)/shard_map/ppermute | solution.py:152
  13.3 0.5 collective-permute-start.7
  13.8 1.9 %collective-permute-start.6 = (bf16[3,32,1152]{2,1,0:T(8,128)(2,1)S(1)}, bf16[3,32,1152]{2,1,0:T(8,128)(2,1)S(1)}, u32[]{:S(2)}, u32[]{:S(2)}) collective-permute-start(bf16[3,32,1152]{2,1,0:T(8,128)(2,1)S(1)} %collective-permute-done.1.second), channel_id=1, source_target_pairs={{0,4},{1,5},{2,6},{3,7},{4,0},{5,1},{6,2},{7,3},{8,12},{9,13},{10,... | collective-permute-start | bytes 663560 | tf_op jit(solution)/shard_map/ppermute | solution.py:152
  15.6 1.1 %collective-permute-done.3.away = bf16[3,32,1152]{2,1,0:T(8,128)(2,1)S(1)} collective-permute-done((bf16[3,32,1152]{2,1,0:T(8,128)(2,1)S(1)}, bf16[3,32,1152]{2,1,0:T(8,128)(2,1)S(1)}, u32[]{:S(2)}, u32[]{:S(2)}) %collective-permute-start.3) | collective-permute-done | bytes 221216 | tf_op jit(solution)/shard_map/ppermute | solution.py:152
  16.7 0.0 collective-permute-start.5
  16.7 0.1 pad_select_fusion
  16.8 1.0 %shard_map.86 = (f32[3,64,256]{2,1,0:T(8,128)S(1)}, bf16[3,64,256]{2,1,0:T(8,128)(2,1)S(1)}) custom-call(s32[3]{0:T(128)S(1)} %pad_add_fusion.info, bf16[3,32,1152]{2,1,0:T(8,128)(2,1)S(1)} %select_select_fusion.1.at_home, bf16[3,32,1152]{2,1,0:T(8,128)(2,1)S(1)} %collective-permute-done.3.away, bf16[3,32,1152]{2,1,0:T(8,128)(2,1)S(1)} %collective-permute-done.1.second, ...), custom_call_target="tpu_custom_call" | custom-call | tf_op jit(solution)/shard_map/pallas_call | solution.py:23
  17.8 0.0 copy-start
  17.8 1.9 %collective-permute-start.8 = (bf16[3,64,256]{2,1,0:T(8,128)(2,1)S(1)}, bf16[3,64,256]{2,1,0:T(8,128)(2,1)S(1)}, u32[]{:S(2)}, u32[]{:S(2)}) collective-permute-start(bf16[3,64,256]{2,1,0:T(8,128)(2,1)S(1)} %get-tuple-element.62), channel_id=1, source_target_pairs={{0,2},{1,3},{2,0},{3,1},{4,6},{5,7},{6,4},{7,5},{8,10},{9,11},{10,... | collective-permute-start | bytes 294920 | tf_op jit(solution)/shard_map/ppermute | solution.py:152
  19.7 2.4 %collective-permute-done.6.second = bf16[3,32,1152]{2,1,0:T(8,128)(2,1)S(1)} collective-permute-done((bf16[3,32,1152]{2,1,0:T(8,128)(2,1)S(1)}, bf16[3,32,1152]{2,1,0:T(8,128)(2,1)S(1)}, u32[]{:S(2)}, u32[]{:S(2)}) %collective-permute-start.6) | collective-permute-done | bytes 221216 | tf_op jit(solution)/shard_map/ppermute | solution.py:152
  22.0 0.0 collective-permute-done.5.away
  22.1 1.0 %shard_map.87 = (f32[3,64,256]{2,1,0:T(8,128)S(1)}, bf16[3,64,256]{2,1,0:T(8,128)(2,1)S(1)}) custom-call(s32[3]{0:T(128)S(1)} %pad_add_fusion.info, bf16[3,32,1152]{2,1,0:T(8,128)(2,1)S(1)} %collective-permute-done.4.at_home, bf16[3,32,1152]{2,1,0:T(8,128)(2,1)S(1)} %collective-permute-done.5.away, bf16[3,32,1152]{2,1,0:T(8,128)(2,1)S(1)} %collective-permute-done.6.second, ...), custom_call_target="tpu_custom_call" | custom-call | tf_op jit(solution)/shard_map/pallas_call | solution.py:23
  23.0 1.9 %collective-permute-start.10 = (bf16[3,64,256]{2,1,0:T(8,128)(2,1)S(1)}, bf16[3,64,256]{2,1,0:T(8,128)(2,1)S(1)}, u32[]{:S(2)}, u32[]{:S(2)}) collective-permute-start(bf16[3,64,256]{2,1,0:T(8,128)(2,1)S(1)} %get-tuple-element.66), channel_id=1, source_target_pairs={{0,2},{1,3},{2,0},{3,1},{4,6},{5,7},{6,4},{7,5},{8,10},{9,11},{10,... | collective-permute-start | bytes 294920 | tf_op jit(solution)/shard_map/ppermute | solution.py:152
  24.9 0.1 select_select_fusion
  25.0 0.0 copy-start.2
  25.0 0.0 copy-start.3
  25.1 0.8 shard_map.88.weight
  25.9 0.0 collective-permute-done.8.got
  25.9 1.7 %shard_map.89 = (bf16[3,64,256]{2,1,0:T(8,128)(2,1)S(1)}, f32[3,32,1152]{2,1,0:T(8,128)S(1)}, f32[3,32,1152]{2,1,0:T(8,128)S(1)}) custom-call(s32[3]{0:T(128)S(1)} %bitcast.13, f32[3,64,256]{2,1,0:T(8,128)S(1)} %get-tuple-element.61.part, bf16[3,64,256]{2,1,0:T(8,128)(2,1)S(1)} %collective-permute-done.8.got, f32[3,256]{1,0:T(4,128)S(1)} %copy-done.2, ...), custom_call_target="tpu_custom_call" | custom-call | tf_op jit(solution)/shard_map/pallas_call | solution.py:23
  27.6 0.6 collective-permute-done.10.got
  28.2 1.7 %shard_map.90 = (bf16[3,64,256]{2,1,0:T(8,128)(2,1)S(1)}, bf16[3,32,1152]{2,1,0:T(8,128)(2,1)S(1)}, bf16[3,32,1152]{2,1,0:T(8,128)(2,1)S(1)}) custom-call(s32[3]{0:T(128)S(1)} %bitcast.14, f32[3,64,256]{2,1,0:T(8,128)S(1)} %get-tuple-element.68.part, bf16[3,64,256]{2,1,0:T(8,128)(2,1)S(1)} %collective-permute-done.10.got, f32[3,256]{1,0:T(4,128)S(1)} %copy-done.2, ...), custom_call_target="tpu_custom_call" | custom-call | tf_op jit(solution)/shard_map/pallas_call | solution.py:23
  29.9 2.2 %collective-permute-start.13 = (bf16[3,32,1152]{2,1,0:T(8,128)(2,1)S(1)}, bf16[3,32,1152]{2,1,0:T(8,128)(2,1)S(1)}, u32[]{:S(2)}, u32[]{:S(2)}) collective-permute-start(bf16[3,32,1152]{2,1,0:T(8,128)(2,1)S(1)} %get-tuple-element.72), channel_id=1, source_target_pairs={{0,4},{1,5},{2,6},{3,7},{4,0},{5,1},{6,2},{7,3},{8,12},{9,13},{10,... | collective-permute-start | bytes 663560 | tf_op jit(solution)/shard_map/ppermute | solution.py:152
  32.1 0.1 collective-permute-start.11
  32.2 6.1 %collective-permute-done.13 = bf16[3,32,1152]{2,1,0:T(8,128)(2,1)S(1)} collective-permute-done((bf16[3,32,1152]{2,1,0:T(8,128)(2,1)S(1)}, bf16[3,32,1152]{2,1,0:T(8,128)(2,1)S(1)}, u32[]{:S(2)}, u32[]{:S(2)}) %collective-permute-start.13) | collective-permute-done | bytes 221216 | tf_op jit(solution)/shard_map/ppermute | solution.py:152
  38.4 2.5 %collective-permute-start.14 = (bf16[3,32,1152]{2,1,0:T(8,128)(2,1)S(1)}, bf16[3,32,1152]{2,1,0:T(8,128)(2,1)S(1)}, u32[]{:S(2)}, u32[]{:S(2)}) collective-permute-start(bf16[3,32,1152]{2,1,0:T(8,128)(2,1)S(1)} %add_convert_fusion), channel_id=1, source_target_pairs={{0,16},{1,8},{2,18},{3,10},{4,20},{5,12},{6,22},{7,14},{8,1},{9,25... | collective-permute-start | bytes 663560 | tf_op jit(solution)/shard_map/ppermute | solution.py:152
  40.9 1.8 %collective-permute-done.11 = bf16[3,32,1152]{2,1,0:T(8,128)(2,1)S(1)} collective-permute-done((bf16[3,32,1152]{2,1,0:T(8,128)(2,1)S(1)}, bf16[3,32,1152]{2,1,0:T(8,128)(2,1)S(1)}, u32[]{:S(2)}, u32[]{:S(2)}) %collective-permute-start.11) | collective-permute-done | bytes 221216 | tf_op jit(solution)/shard_map/ppermute | solution.py:152
  42.7 0.1 fusion
  42.8 1.7 %collective-permute-start.12 = (bf16[3,32,1152]{2,1,0:T(8,128)(2,1)S(1)}, bf16[3,32,1152]{2,1,0:T(8,128)(2,1)S(1)}, u32[]{:S(2)}, u32[]{:S(2)}) collective-permute-start(bf16[3,32,1152]{2,1,0:T(8,128)(2,1)S(1)} %fusion), channel_id=1, source_target_pairs={{0,4},{1,24},{2,6},{3,26},{4,0},{5,28},{6,2},{7,30},{8,17},{9,13},... | collective-permute-start | bytes 663560 | tf_op jit(solution)/shard_map/ppermute | solution.py:152
  44.4 0.9 %collective-permute-done.14 = bf16[3,32,1152]{2,1,0:T(8,128)(2,1)S(1)} collective-permute-done((bf16[3,32,1152]{2,1,0:T(8,128)(2,1)S(1)}, bf16[3,32,1152]{2,1,0:T(8,128)(2,1)S(1)}, u32[]{:S(2)}, u32[]{:S(2)}) %collective-permute-start.14) | collective-permute-done | bytes 221216 | tf_op jit(solution)/shard_map/ppermute | solution.py:152
  45.4 3.4 %collective-permute-done.12 = bf16[3,32,1152]{2,1,0:T(8,128)(2,1)S(1)} collective-permute-done((bf16[3,32,1152]{2,1,0:T(8,128)(2,1)S(1)}, bf16[3,32,1152]{2,1,0:T(8,128)(2,1)S(1)}, u32[]{:S(2)}, u32[]{:S(2)}) %collective-permute-start.12) | collective-permute-done | bytes 221216 | tf_op jit(solution)/shard_map/ppermute | solution.py:152
  48.8 0.1 convert_add_fusion
  48.9 1.1 %collective-permute-start.15 = (f32[3,32,1152]{2,1,0:T(8,128)S(1)}, f32[3,32,1152]{2,1,0:T(8,128)S(1)}, u32[]{:S(2)}, u32[]{:S(2)}) collective-permute-start(f32[3,32,1152]{2,1,0:T(8,128)S(1)} %convert_add_fusion), channel_id=1, source_target_pairs={{0,1},{1,0},{2,3},{3,2},{4,5},{5,4},{6,7},{7,6},{8,9},{9,8},{10,11... | collective-permute-start | bytes 1327112 | tf_op jit(solution)/shard_map/ppermute | solution.py:152
  50.0 1.4 %collective-permute-done.15 = f32[3,32,1152]{2,1,0:T(8,128)S(1)} collective-permute-done((f32[3,32,1152]{2,1,0:T(8,128)S(1)}, f32[3,32,1152]{2,1,0:T(8,128)S(1)}, u32[]{:S(2)}, u32[]{:S(2)}) %collective-permute-start.15) | collective-permute-done | bytes 442400 | tf_op jit(solution)/shard_map/ppermute | solution.py:152
  51.4 0.1 subtract_convert_fusion
  51.5 2.8 %collective-permute-start.16 = (bf16[3,32,1152]{2,1,0:T(8,128)(2,1)S(1)}, bf16[3,32,1152]{2,1,0:T(8,128)(2,1)S(1)}, u32[]{:S(2)}, u32[]{:S(2)}) collective-permute-start(bf16[3,32,1152]{2,1,0:T(8,128)(2,1)S(1)} %get-tuple-element.79.own), channel_id=1, source_target_pairs={{0,16},{1,8},{2,18},{3,10},{4,20},{5,12},{6,22},{7,14},{8,1},{9,25... | collective-permute-start | bytes 663560 | tf_op jit(solution)/shard_map/ppermute | solution.py:152
  54.3 0.0 collective-permute-start.18
  54.3 6.4 %collective-permute-done.16.r1 = bf16[3,32,1152]{2,1,0:T(8,128)(2,1)S(1)} collective-permute-done((bf16[3,32,1152]{2,1,0:T(8,128)(2,1)S(1)}, bf16[3,32,1152]{2,1,0:T(8,128)(2,1)S(1)}, u32[]{:S(2)}, u32[]{:S(2)}) %collective-permute-start.16) | collective-permute-done | bytes 221216 | tf_op jit(solution)/shard_map/ppermute | solution.py:152
  60.7 0.6 collective-permute-start.21
  61.3 1.4 %collective-permute-start.20 = (bf16[3,32,1152]{2,1,0:T(8,128)(2,1)S(1)}, bf16[3,32,1152]{2,1,0:T(8,128)(2,1)S(1)}, u32[]{:S(2)}, u32[]{:S(2)}) collective-permute-start(bf16[3,32,1152]{2,1,0:T(8,128)(2,1)S(1)} %collective-permute-done.16.r1), channel_id=1, source_target_pairs={{0,4},{1,5},{2,6},{3,7},{4,0},{5,1},{6,2},{7,3},{8,12},{9,13},{10,... | collective-permute-start | bytes 663560 | tf_op jit(solution)/shard_map/ppermute | solution.py:152
  62.7 1.5 %collective-permute-done.17.third = bf16[3,32,1152]{2,1,0:T(8,128)(2,1)S(1)} collective-permute-done((bf16[3,32,1152]{2,1,0:T(8,128)(2,1)S(1)}, bf16[3,32,1152]{2,1,0:T(8,128)(2,1)S(1)}, u32[]{:S(2)}, u32[]{:S(2)}) %collective-permute-start.17) | collective-permute-done | bytes 221216 | tf_op jit(solution)/shard_map/ppermute | solution.py:152
  64.2 0.8 fusion.1
  64.9 4.7 %collective-permute-done.20.r3 = bf16[3,32,1152]{2,1,0:T(8,128)(2,1)S(1)} collective-permute-done((bf16[3,32,1152]{2,1,0:T(8,128)(2,1)S(1)}, bf16[3,32,1152]{2,1,0:T(8,128)(2,1)S(1)}, u32[]{:S(2)}, u32[]{:S(2)}) %collective-permute-start.20) | collective-permute-done | bytes 221216 | tf_op jit(solution)/shard_map/ppermute | solution.py:152
  69.6 1.3 %shard_map.91 = (f32[3,64,256]{2,1,0:T(8,128)S(1)}, bf16[3,64,256]{2,1,0:T(8,128)(2,1)S(1)}, bf16[3,128,1152]{2,1,0:T(8,128)(2,1)S(1)}) custom-call(s32[3]{0:T(128)S(1)} %pad_add_fusion.info, bf16[3,32,1152]{2,1,0:T(8,128)(2,1)S(1)} %get-tuple-element.79.own, bf16[3,32,1152]{2,1,0:T(8,128)(2,1)S(1)} %collective-permute-done.18.beside, ...), custom_call_target="tpu_custom_call" | custom-call | tf_op jit(solution)/shard_map/pallas_call | solution.py:23
  70.9 0.2 slice_select_fusion
  71.1 1.4 %collective-permute-start.23 = (bf16[3,128,576]{2,1,0:T(8,128)(2,1)S(1)}, bf16[3,128,576]{2,1,0:T(8,128)(2,1)S(1)}, u32[]{:S(2)}, u32[]{:S(2)}) collective-permute-start(bf16[3,128,576]{2,1,0:T(8,128)(2,1)S(1)} %slice_select_fusion), channel_id=1, source_target_pairs={{0,1},{1,0},{2,3},{3,2},{4,5},{5,4},{6,7},{7,6},{8,9},{9,8},{10,11... | collective-permute-start | bytes 1327112 | tf_op jit(solution)/shard_map/ppermute | solution.py:152
  72.5 1.4 %collective-permute-start.22 = (bf16[3,64,256]{2,1,0:T(8,128)(2,1)S(1)}, bf16[3,64,256]{2,1,0:T(8,128)(2,1)S(1)}, u32[]{:S(2)}, u32[]{:S(2)}) collective-permute-start(bf16[3,64,256]{2,1,0:T(8,128)(2,1)S(1)} %get-tuple-element.85), channel_id=1, source_target_pairs={{0,2},{1,3},{2,0},{3,1},{4,6},{5,7},{6,4},{7,5},{8,10},{9,11},{10,... | collective-permute-start | bytes 294920 | tf_op jit(solution)/shard_map/ppermute | solution.py:152
  73.9 0.1 iota_compare_fusion.1
  74.0 0.0 collective-permute-done.23.errors_got
  74.0 2.2 %shard_map.92 = bf16[6,576,256]{2,1,0:T(8,128)(2,1)} custom-call(s32[3]{0:T(128)S(1)} %pad_add_fusion.info, bf16[3,128,1152]{2,1,0:T(8,128)(2,1)S(1)} %get-tuple-element.86.held, bf16[3,128,576]{2,1,0:T(8,128)(2,1)S(1)} %collective-permute-done.23.errors_got, bf16[3,128,256]{2,1,0:T(8,128)(2,1)S(1)} %constant_dynamic-update-slice_fusion.latents, ...), custom_call_target="tpu_custom_call" | custom-call | tf_op jit(solution)/shard_map/pallas_call | solution.py:274
  76.2 1.1 %collective-permute-done.22 = bf16[3,64,256]{2,1,0:T(8,128)(2,1)S(1)} collective-permute-done((bf16[3,64,256]{2,1,0:T(8,128)(2,1)S(1)}, bf16[3,64,256]{2,1,0:T(8,128)(2,1)S(1)}, u32[]{:S(2)}, u32[]{:S(2)}) %collective-permute-start.22) | collective-permute-done | bytes 98336 | tf_op jit(solution)/shard_map/ppermute | solution.py:152
  77.3 0.7 fusion.4
  (20 shorter events, 0.1 us)
Async XLA Ops:
  0.6 1.7 %collective-permute-start = (bf16[3,32,576]{2,1,0:T(8,128)(2,1)}, bf16[3,32,576]{2,1,0:T(8,128)(2,1)S(1)}, u32[]{:S(2)}, u32[]{:S(2)}) collective-permute-start(bf16[3,32,576]{2,1,0:T(8,128)(2,1)} %bitcast.18), channel_id=1, source_target_pairs={{0,1},{1,0},{2,3},{3,2},{4,5},{5,4},{6,7},{7,6},{8,9},{9,8},{10,11... | collective-permute-start | bytes 331784 | tf_op jit(solution)/shard_map/ppermute | solution.py:152
  2.4 4.6 %collective-permute-start.2 = (bf16[3,576,256]{2,1,0:T(8,128)(2,1)}, bf16[3,576,256]{2,1,0:T(8,128)(2,1)S(1)}, u32[]{:S(2)}, u32[]{:S(2)}) collective-permute-start(bf16[3,576,256]{2,1,0:T(8,128)(2,1)} %own), channel_id=1, source_target_pairs={{0,1},{1,0},{2,3},{3,2},{4,5},{5,4},{6,7},{7,6},{8,9},{9,8},{10,11... | collective-permute-start | bytes 2654216 | tf_op jit(solution)/shard_map/ppermute | solution.py:152
  2.9 22.2 %collective-permute-start.9 = (bf16[6,576,256]{2,1,0:T(8,128)(2,1)}, bf16[6,576,256]{2,1,0:T(8,128)(2,1)S(1)}, u32[]{:S(2)}, u32[]{:S(2)}) collective-permute-start(bf16[6,576,256]{2,1,0:T(8,128)(2,1)} %bitcast.11), channel_id=1, source_target_pairs={{0,1},{1,0},{2,3},{3,2},{4,5},{5,4},{6,7},{7,6},{8,9},{9,8},{10,11... | collective-permute-start | bytes 5308424 | tf_op jit(solution)/shard_map/ppermute | solution.py:152
  3.0 10.2 %collective-permute-start.1 = (bf16[3,32,1152]{2,1,0:T(8,128)(2,1)S(1)}, bf16[3,32,1152]{2,1,0:T(8,128)(2,1)S(1)}, u32[]{:S(2)}, u32[]{:S(2)}) collective-permute-start(bf16[3,32,1152]{2,1,0:T(8,128)(2,1)S(1)} %select_select_fusion.1.at_home), channel_id=1, source_target_pairs={{0,16},{1,8},{2,18},{3,10},{4,20},{5,12},{6,22},{7,14},{8,1},{9,25... | collective-permute-start | bytes 663560 | tf_op jit(solution)/shard_map/ppermute | solution.py:152
  7.0 8.6 %collective-permute-start.4 = (bf16[3,32,1152]{2,1,0:T(8,128)(2,1)S(1)}, bf16[3,32,1152]{2,1,0:T(8,128)(2,1)S(1)}, u32[]{:S(2)}, u32[]{:S(2)}) collective-permute-start(bf16[3,32,1152]{2,1,0:T(8,128)(2,1)S(1)} %select_select_fusion.1.at_home), channel_id=1, source_target_pairs={{0,1},{1,4},{2,3},{3,6},{4,5},{5,0},{6,7},{7,2},{8,13},{9,8},{10,1... | collective-permute-start | bytes 663560 | tf_op jit(solution)/shard_map/ppermute | solution.py:152
  7.1 1.2 %copy-start.1 = (bf16[3,576,256]{2,1,0:T(8,128)(2,1)S(1)}, bf16[3,576,256]{2,1,0:T(8,128)(2,1)}, u32[]{:S(2)}) copy-start(bf16[3,576,256]{2,1,0:T(8,128)(2,1)} %own) | copy-start | bytes 2654212
  8.2 5.0 %copy-start.4 = (bf16[32,3,576]{2,0,1:T(8,128)(2,1)S(1)}, bf16[32,3,576]{2,0,1:T(8,128)(2,1)}, u32[]{:S(2)}) copy-start(bf16[32,3,576]{2,0,1:T(8,128)(2,1)} %param.7) | copy-start | bytes 331780
  13.2 3.5 %collective-permute-start.3 = (bf16[3,32,1152]{2,1,0:T(8,128)(2,1)S(1)}, bf16[3,32,1152]{2,1,0:T(8,128)(2,1)S(1)}, u32[]{:S(2)}, u32[]{:S(2)}) collective-permute-start(bf16[3,32,1152]{2,1,0:T(8,128)(2,1)S(1)} %collective-permute-done.1.second), channel_id=1, source_target_pairs={{0,8},{1,0},{2,10},{3,2},{4,12},{5,4},{6,14},{7,6},{8,9},{9,1},{10... | collective-permute-start | bytes 663560 | tf_op jit(solution)/shard_map/ppermute | solution.py:152
  13.3 11.7 %collective-permute-start.7 = (bf16[3,32,576]{2,1,0:T(8,128)(2,1)S(1)}, bf16[3,32,576]{2,1,0:T(8,128)(2,1)S(1)}, u32[]{:S(2)}, u32[]{:S(2)}) collective-permute-start(bf16[3,32,576]{2,1,0:T(8,128)(2,1)S(1)} %bitcast.20), channel_id=1, source_target_pairs={{0,1},{1,0},{2,3},{3,2},{4,5},{5,4},{6,7},{7,6},{8,9},{9,8},{10,11... | collective-permute-start | bytes 331784 | tf_op jit(solution)/shard_map/ppermute | solution.py:152
  13.8 8.3 %collective-permute-start.6 = (bf16[3,32,1152]{2,1,0:T(8,128)(2,1)S(1)}, bf16[3,32,1152]{2,1,0:T(8,128)(2,1)S(1)}, u32[]{:S(2)}, u32[]{:S(2)}) collective-permute-start(bf16[3,32,1152]{2,1,0:T(8,128)(2,1)S(1)} %collective-permute-done.1.second), channel_id=1, source_target_pairs={{0,4},{1,5},{2,6},{3,7},{4,0},{5,1},{6,2},{7,3},{8,12},{9,13},{10,... | collective-permute-start | bytes 663560 | tf_op jit(solution)/shard_map/ppermute | solution.py:152
  16.7 5.4 %collective-permute-start.5 = (bf16[3,32,1152]{2,1,0:T(8,128)(2,1)S(1)}, bf16[3,32,1152]{2,1,0:T(8,128)(2,1)S(1)}, u32[]{:S(2)}, u32[]{:S(2)}) collective-permute-start(bf16[3,32,1152]{2,1,0:T(8,128)(2,1)S(1)} %collective-permute-done.3.away), channel_id=1, source_target_pairs={{0,9},{1,5},{2,11},{3,7},{4,13},{5,1},{6,15},{7,3},{8,12},{9,0},{1... | collective-permute-start | bytes 663560 | tf_op jit(solution)/shard_map/ppermute | solution.py:152
  17.8 7.3 %copy-start = (bf16[6,256,576]{1,2,0:T(8,128)(2,1)S(1)}, bf16[6,256,576]{1,2,0:T(8,128)(2,1)}, u32[]{:S(2)}) copy-start(bf16[6,256,576]{1,2,0:T(8,128)(2,1)} %param.10) | copy-start | bytes 5308420
  17.8 8.1 %collective-permute-start.8 = (bf16[3,64,256]{2,1,0:T(8,128)(2,1)S(1)}, bf16[3,64,256]{2,1,0:T(8,128)(2,1)S(1)}, u32[]{:S(2)}, u32[]{:S(2)}) collective-permute-start(bf16[3,64,256]{2,1,0:T(8,128)(2,1)S(1)} %get-tuple-element.62), channel_id=1, source_target_pairs={{0,2},{1,3},{2,0},{3,1},{4,6},{5,7},{6,4},{7,5},{8,10},{9,11},{10,... | collective-permute-start | bytes 294920 | tf_op jit(solution)/shard_map/ppermute | solution.py:152
  23.0 5.2 %collective-permute-start.10 = (bf16[3,64,256]{2,1,0:T(8,128)(2,1)S(1)}, bf16[3,64,256]{2,1,0:T(8,128)(2,1)S(1)}, u32[]{:S(2)}, u32[]{:S(2)}) collective-permute-start(bf16[3,64,256]{2,1,0:T(8,128)(2,1)S(1)} %get-tuple-element.66), channel_id=1, source_target_pairs={{0,2},{1,3},{2,0},{3,1},{4,6},{5,7},{6,4},{7,5},{8,10},{9,11},{10,... | collective-permute-start | bytes 294920 | tf_op jit(solution)/shard_map/ppermute | solution.py:152
  25.0 0.8 %copy-start.2 = (f32[3,256]{1,0:T(4,128)S(1)}, f32[3,256]{1,0:T(4,128)}, u32[]{:S(2)}) copy-start(f32[3,256]{1,0:T(4,128)} %bias.3) | copy-start | bytes 9220
  25.0 0.8 %copy-start.3 = (s32[3,1]{0,1:T(1,128)S(1)}, s32[3,1]{0,1:T(1,128)}, u32[]{:S(2)}) copy-start(s32[3,1]{0,1:T(1,128)} %param.11) | copy-start | bytes 40
  29.9 8.4 %collective-permute-start.13 = (bf16[3,32,1152]{2,1,0:T(8,128)(2,1)S(1)}, bf16[3,32,1152]{2,1,0:T(8,128)(2,1)S(1)}, u32[]{:S(2)}, u32[]{:S(2)}) collective-permute-start(bf16[3,32,1152]{2,1,0:T(8,128)(2,1)S(1)} %get-tuple-element.72), channel_id=1, source_target_pairs={{0,4},{1,5},{2,6},{3,7},{4,0},{5,1},{6,2},{7,3},{8,12},{9,13},{10,... | collective-permute-start | bytes 663560 | tf_op jit(solution)/shard_map/ppermute | solution.py:152
  32.1 10.6 %collective-permute-start.11 = (bf16[3,32,1152]{2,1,0:T(8,128)(2,1)S(1)}, bf16[3,32,1152]{2,1,0:T(8,128)(2,1)S(1)}, u32[]{:S(2)}, u32[]{:S(2)}) collective-permute-start(bf16[3,32,1152]{2,1,0:T(8,128)(2,1)S(1)} %get-tuple-element.70), channel_id=1, source_target_pairs={{0,4},{1,5},{2,6},{3,7},{4,0},{5,1},{6,2},{7,3},{8,12},{9,13},{10,... | collective-permute-start | bytes 663560 | tf_op jit(solution)/shard_map/ppermute | solution.py:152
  38.4 7.0 %collective-permute-start.14 = (bf16[3,32,1152]{2,1,0:T(8,128)(2,1)S(1)}, bf16[3,32,1152]{2,1,0:T(8,128)(2,1)S(1)}, u32[]{:S(2)}, u32[]{:S(2)}) collective-permute-start(bf16[3,32,1152]{2,1,0:T(8,128)(2,1)S(1)} %add_convert_fusion), channel_id=1, source_target_pairs={{0,16},{1,8},{2,18},{3,10},{4,20},{5,12},{6,22},{7,14},{8,1},{9,25... | collective-permute-start | bytes 663560 | tf_op jit(solution)/shard_map/ppermute | solution.py:152
  42.8 6.0 %collective-permute-start.12 = (bf16[3,32,1152]{2,1,0:T(8,128)(2,1)S(1)}, bf16[3,32,1152]{2,1,0:T(8,128)(2,1)S(1)}, u32[]{:S(2)}, u32[]{:S(2)}) collective-permute-start(bf16[3,32,1152]{2,1,0:T(8,128)(2,1)S(1)} %fusion), channel_id=1, source_target_pairs={{0,4},{1,24},{2,6},{3,26},{4,0},{5,28},{6,2},{7,30},{8,17},{9,13},... | collective-permute-start | bytes 663560 | tf_op jit(solution)/shard_map/ppermute | solution.py:152
  48.9 2.5 %collective-permute-start.15 = (f32[3,32,1152]{2,1,0:T(8,128)S(1)}, f32[3,32,1152]{2,1,0:T(8,128)S(1)}, u32[]{:S(2)}, u32[]{:S(2)}) collective-permute-start(f32[3,32,1152]{2,1,0:T(8,128)S(1)} %convert_add_fusion), channel_id=1, source_target_pairs={{0,1},{1,0},{2,3},{3,2},{4,5},{5,4},{6,7},{7,6},{8,9},{9,8},{10,11... | collective-permute-start | bytes 1327112 | tf_op jit(solution)/shard_map/ppermute | solution.py:152
  51.5 9.2 %collective-permute-start.16 = (bf16[3,32,1152]{2,1,0:T(8,128)(2,1)S(1)}, bf16[3,32,1152]{2,1,0:T(8,128)(2,1)S(1)}, u32[]{:S(2)}, u32[]{:S(2)}) collective-permute-start(bf16[3,32,1152]{2,1,0:T(8,128)(2,1)S(1)} %get-tuple-element.79.own), channel_id=1, source_target_pairs={{0,16},{1,8},{2,18},{3,10},{4,20},{5,12},{6,22},{7,14},{8,1},{9,25... | collective-permute-start | bytes 663560 | tf_op jit(solution)/shard_map/ppermute | solution.py:152
  54.3 8.4 %collective-permute-start.18 = (bf16[3,32,1152]{2,1,0:T(8,128)(2,1)S(1)}, bf16[3,32,1152]{2,1,0:T(8,128)(2,1)S(1)}, u32[]{:S(2)}, u32[]{:S(2)}) collective-permute-start(bf16[3,32,1152]{2,1,0:T(8,128)(2,1)S(1)} %get-tuple-element.79.own), channel_id=1, source_target_pairs={{0,1},{1,4},{2,3},{3,6},{4,5},{5,0},{6,7},{7,2},{8,13},{9,8},{10,1... | collective-permute-start | bytes 663560 | tf_op jit(solution)/shard_map/ppermute | solution.py:152
  60.7 3.5 %collective-permute-start.17 = (bf16[3,32,1152]{2,1,0:T(8,128)(2,1)S(1)}, bf16[3,32,1152]{2,1,0:T(8,128)(2,1)S(1)}, u32[]{:S(2)}, u32[]{:S(2)}) collective-permute-start(bf16[3,32,1152]{2,1,0:T(8,128)(2,1)S(1)} %collective-permute-done.16.r1), channel_id=1, source_target_pairs={{0,8},{1,0},{2,10},{3,2},{4,12},{5,4},{6,14},{7,6},{8,9},{9,1},{10... | collective-permute-start | bytes 663560 | tf_op jit(solution)/shard_map/ppermute | solution.py:152
  60.7 4.2 %collective-permute-start.21 = (bf16[3,128,256]{2,1,0:T(8,128)(2,1)S(1)}, bf16[3,128,256]{2,1,0:T(8,128)(2,1)S(1)}, u32[]{:S(2)}, u32[]{:S(2)}) collective-permute-start(bf16[3,128,256]{2,1,0:T(8,128)(2,1)S(1)} %constant_dynamic-update-slice_fusion.latents), channel_id=1, source_target_pairs={{0,1},{1,0},{2,3},{3,2},{4,5},{5,4},{6,7},{7,6},{8,9},{9,8},{10,11... | collective-permute-start | bytes 589832 | tf_op jit(solution)/shard_map/ppermute | solution.py:152
  61.3 8.3 %collective-permute-start.20 = (bf16[3,32,1152]{2,1,0:T(8,128)(2,1)S(1)}, bf16[3,32,1152]{2,1,0:T(8,128)(2,1)S(1)}, u32[]{:S(2)}, u32[]{:S(2)}) collective-permute-start(bf16[3,32,1152]{2,1,0:T(8,128)(2,1)S(1)} %collective-permute-done.16.r1), channel_id=1, source_target_pairs={{0,4},{1,5},{2,6},{3,7},{4,0},{5,1},{6,2},{7,3},{8,12},{9,13},{10,... | collective-permute-start | bytes 663560 | tf_op jit(solution)/shard_map/ppermute | solution.py:152
  64.2 5.4 %collective-permute-start.19 = (bf16[3,32,1152]{2,1,0:T(8,128)(2,1)S(1)}, bf16[3,32,1152]{2,1,0:T(8,128)(2,1)S(1)}, u32[]{:S(2)}, u32[]{:S(2)}) collective-permute-start(bf16[3,32,1152]{2,1,0:T(8,128)(2,1)S(1)} %collective-permute-done.17.third), channel_id=1, source_target_pairs={{0,9},{1,5},{2,11},{3,7},{4,13},{5,1},{6,15},{7,3},{8,12},{9,0},{1... | collective-permute-start | bytes 663560 | tf_op jit(solution)/shard_map/ppermute | solution.py:152
  71.1 2.9 %collective-permute-start.23 = (bf16[3,128,576]{2,1,0:T(8,128)(2,1)S(1)}, bf16[3,128,576]{2,1,0:T(8,128)(2,1)S(1)}, u32[]{:S(2)}, u32[]{:S(2)}) collective-permute-start(bf16[3,128,576]{2,1,0:T(8,128)(2,1)S(1)} %slice_select_fusion), channel_id=1, source_target_pairs={{0,1},{1,0},{2,3},{3,2},{4,5},{5,4},{6,7},{7,6},{8,9},{9,8},{10,11... | collective-permute-start | bytes 1327112 | tf_op jit(solution)/shard_map/ppermute | solution.py:152
  72.5 4.8 %collective-permute-start.22 = (bf16[3,64,256]{2,1,0:T(8,128)(2,1)S(1)}, bf16[3,64,256]{2,1,0:T(8,128)(2,1)S(1)}, u32[]{:S(2)}, u32[]{:S(2)}) collective-permute-start(bf16[3,64,256]{2,1,0:T(8,128)(2,1)S(1)} %get-tuple-element.85), channel_id=1, source_target_pairs={{0,2},{1,3},{2,0},{3,1},{4,6},{5,7},{6,4},{7,5},{8,10},{9,11},{10,... | collective-permute-start | bytes 294920 | tf_op jit(solution)/shard_map/ppermute | solution.py:152
